TPU v7x, 32 devices: a whole 2x2x4 slice. The times are simulated.
32 devices in a mesh: batch: 4 (over z), seq: 8 (over y, x, core).
Axes of the slice: x: 2, y: 2, z: 4, core: 2. Of those that a mesh axis runs over, the one named last changes fastest.
Arguments:
- mel_inputs: bfloat16 [8, 1536, 200], P('batch', 'seq'), may hold values from -6 to 6
- text_ids: int32 [8, 1536], P('batch', 'seq'), may hold values from 0 to 2545
- segment_ids: int32 [8, 1536], P('batch'), may hold values from 0 to 3, as said below
- key_mask: int32 [8, 1536], P('batch'), may hold values from 0 to 1, as said below
- time_index: int32 [8, 4], P('batch'), may hold values from 0 to 31
- input_proj: bfloat16 [712, 1024], P(None, ('batch', 'seq')), may hold values from -0.21875 to 0.21875
- conv_first: bfloat16 [31, 1024, 64], P(None, ('batch', 'seq')), may hold values from -0.125 to 0.125
- conv_second: bfloat16 [31, 1024, 64], P(None, ('batch', 'seq')), may hold values from -0.125 to 0.125
- time_table: bfloat16 [32, 1024], P(None, ('batch', 'seq')), may hold values from -6 to 6
- adaln_proj: bfloat16 [1024, 6144], P(None, ('batch', 'seq')), may hold values from -0.1875 to 0.1875
- qkv_proj: bfloat16 [1024, 3072], P(None, ('batch', 'seq')), may hold values from -0.1875 to 0.1875
- out_proj: bfloat16 [1024, 1024], P(None, ('batch', 'seq')), may hold values from -2.5 to 2.5
- up_proj: bfloat16 [1024, 2048], P(None, ('batch', 'seq')), may hold values from -0.1875 to 0.1875
- down_proj: bfloat16 [2048, 1024], P(None, ('batch', 'seq')), may hold values from -0.125 to 0.125
- text_table: bfloat16 [2546, 512], P(None, ('batch', 'seq')), may hold values from -6 to 6
- grad_out: bfloat16 [8, 1536, 1024], P('batch', 'seq'), may hold values from -6 to 6
Outputs:
- block_out: bfloat16 [8, 1536, 1024], P('batch', 'seq')
- grad_mels: float32 [8, 1536, 200], P('batch', 'seq')
- grad_input_proj: float32 [712, 1024], P(None, ('batch', 'seq'))
- grad_conv_first: float32 [31, 1024, 64], P(None, ('batch', 'seq'))
- grad_conv_second: float32 [31, 1024, 64], P(None, ('batch', 'seq'))
- grad_time_table: float32 [32, 1024], P(None, ('batch', 'seq'))
- grad_adaln_proj: float32 [1024, 6144], P(None, ('batch', 'seq'))
- grad_qkv_proj: float32 [1024, 3072], P(None, ('batch', 'seq'))
- grad_out_proj: float32 [1024, 1024], P(None, ('batch', 'seq'))
- grad_up_proj: float32 [1024, 2048], P(None, ('batch', 'seq'))
- grad_down_proj: float32 [2048, 1024], P(None, ('batch', 'seq'))
- grad_text_table: float32 [2546, 512], P(None, ('batch', 'seq'))
Inputs may be any that keep to these rules, and one draw needn't show every extreme that they name: `segment_ids`: in each row utterance numbers start at 0 and rise by one at each boundary; a row holds 1 to 4 utterances, each of 192 frames or more; of the 2 rows of each index of batch, one is a single utterance. `key_mask`: each row is 1 except for its last 48 to 191 frames.
All inputs are finite; a program needn't handle non-finite values.
Results may differ from a plain program's by a relative error of at most 0.023.
Values may be sent and summed in bfloat16 or wider, within the bound.
A program may use at most 448 MiB of HBM per device.

v0:
```python
import math

import jax
import jax.numpy as jnp
from jax import lax
from jax.sharding import PartitionSpec as P

D = 1024
HEADS = 16
HEAD = 64
MEL = 100
VOCAB = 2546
KERNEL = 31
GROUPS = 16
STEPS = 32
SEGS = 4


EPSILON = 1e-06
MASKED = -1e30
EXACT = lax.Precision.HIGHEST


def padded_2(block, sides, width):
    for axis, dim in sides:
        count = lax.axis_size(axis)
        forward = [(i, i + 1) for i in range(count - 1)]
        backward = [(target, source) for source, target in forward]
        low = lax.ppermute(
            lax.slice_in_dim(block, block.shape[dim] - width, None, axis=dim), axis, forward
        )
        high = lax.ppermute(lax.slice_in_dim(block, 0, width, axis=dim), axis, backward)
        block = jnp.concatenate([low, block, high], axis=dim)
    return block


def matmul(left_side, right_side):
    return jnp.dot(left_side, right_side, preferred_element_type=jnp.float32)


def matmul_back(left_side, right_side):
    return lax.dot_general(
        left_side, right_side, (((1,), (1,)), ((), ())), preferred_element_type=jnp.float32
    )


def contract_rows(left_side, right_side):
    return lax.dot_general(
        left_side, right_side, (((0,), (0,)), ((), ())), preferred_element_type=jnp.float32
    )


def layer_norm(field):
    centre = field - jnp.mean(field, axis=-1, keepdims=True)
    return centre * lax.rsqrt(jnp.mean(centre * centre, axis=-1, keepdims=True) + EPSILON)


def modulate(field, scaling, shifting):
    return layer_norm(field) * (1.0 + scaling) + shifting


def mish_curve(inputs):
    return inputs * jnp.tanh(jax.nn.softplus(inputs))


def gelu_curve(inputs):
    return jax.nn.gelu(inputs, approximate=True)


def rotary_tables(positions):
    inverse_freq = 10000.0 ** (-jnp.arange(0, HEAD, 2).astype(jnp.float32) / HEAD)
    angles = positions[..., None] * inverse_freq
    return (jnp.cos(angles), jnp.sin(angles))


def rotate(field, cos_tab, sin_tab):
    paired = field.reshape(field.shape[:-1] + (HEAD // 2, 2))
    even_part = paired[..., 0]
    odd_part = paired[..., 1]
    cos_heads = cos_tab[..., None, :]
    sin_heads = sin_tab[..., None, :]
    turned = jnp.stack(
        [
            even_part * cos_heads - odd_part * sin_heads,
            even_part * sin_heads + odd_part * cos_heads,
        ],
        axis=-1,
    )
    return turned.reshape(field.shape)


def widen(field):
    return padded_2(field, (("seq", 1),), KERNEL // 2)


def neighbour_masks(segment_ids, first_frame, frames):
    half_width = KERNEL // 2
    border = jnp.full((segment_ids.shape[0], half_width), -1, jnp.int32)
    padded = jnp.concatenate([border, segment_ids, border], axis=1)
    window = lax.dynamic_slice_in_dim(padded, first_frame, frames + 2 * half_width, 1)
    own_ids = window[:, half_width : half_width + frames]
    return jnp.stack(
        [
            (window[:, kernel_tap : kernel_tap + frames] == own_ids).astype(jnp.bfloat16)
            for kernel_tap in range(KERNEL)
        ]
    )


def conv_apply(padded, kernel, near_masks):
    row_count, frames = (near_masks.shape[1], near_masks.shape[2])
    channel = kernel.shape[2]
    grouped = kernel.reshape(KERNEL, GROUPS, channel, channel)
    summed = jnp.zeros((row_count, frames, GROUPS, channel), jnp.float32)
    for kernel_tap in range(KERNEL):
        tap_mask = near_masks[kernel_tap][:, :, None]
        block_in = (padded[:, kernel_tap : kernel_tap + frames] * tap_mask).reshape(
            row_count, frames, GROUPS, channel
        )
        summed = summed + jnp.einsum(
            "rfgi,gio->rfgo", block_in, grouped[kernel_tap], preferred_element_type=jnp.float32
        )
    return summed.reshape(row_count, frames, GROUPS * channel)


def conv_back(padded_in, padded_grad, grad_own, kernel, near_masks):
    row_count, frames = (near_masks.shape[1], near_masks.shape[2])
    channel = kernel.shape[2]
    grouped = kernel.reshape(KERNEL, GROUPS, channel, channel)
    own_grad = grad_own.reshape(row_count, frames, GROUPS, channel)
    summed = jnp.zeros((row_count, frames, GROUPS, channel), jnp.float32)
    tap_grads = []
    for kernel_tap in range(KERNEL):
        tap_mask = near_masks[kernel_tap][:, :, None]
        grad_block = (padded_grad[:, kernel_tap : kernel_tap + frames] * tap_mask).reshape(
            row_count, frames, GROUPS, channel
        )
        summed = summed + jnp.einsum(
            "rfgo,gio->rfgi",
            grad_block,
            grouped[KERNEL - 1 - kernel_tap],
            preferred_element_type=jnp.float32,
        )
        source = (padded_in[:, kernel_tap : kernel_tap + frames] * tap_mask).reshape(
            row_count, frames, GROUPS, channel
        )
        tap_grads.append(
            jnp.einsum(
                "rfgi,rfgo->gio", source, own_grad, preferred_element_type=jnp.float32
            ).reshape(GROUPS * channel, channel)
        )
    return (summed.reshape(row_count, frames, GROUPS * channel), jnp.stack(tap_grads))


def allowed_pairs(own_ids, segment_ids, key_mask, offset, piece_len):
    key_ids = lax.dynamic_slice_in_dim(segment_ids, offset, piece_len, 1)
    key_keep = lax.dynamic_slice_in_dim(key_mask, offset, piece_len, 1)
    return (own_ids[:, :, None] == key_ids[:, None, :]) & (key_keep[:, None, :] > 0)


def fold_blocks(step_fn, running, pieces, block_len):
    row_count, piece_len = (pieces[0].shape[0], pieces[0].shape[1])
    block_count = piece_len // block_len
    split = tuple(
        (
            jnp.moveaxis(piece.reshape((row_count, block_count, block_len) + piece.shape[2:]), 1, 0)
            for piece in pieces
        )
    )

    def scan_step(state_now, inputs):
        return (step_fn(state_now, inputs[1:], inputs[0] * block_len), None)

    running, unused = lax.scan(
        scan_step, running, (jnp.arange(block_count, dtype=jnp.int32),) + split
    )
    return running


def forward_compute(state_now, inputs):
    queries, key_block, value_block, allowed = inputs
    running_max, running_sum, weighted = state_now
    scores = (
        jnp.einsum("rqhd,rkhd->rhqk", queries, key_block, preferred_element_type=jnp.float32)
        * 0.125
    )
    scores = jnp.where(allowed, scores, MASKED)
    new_max = jnp.maximum(running_max, jnp.max(scores, axis=-1))
    factor = jnp.exp(running_max - new_max)
    weights = jnp.where(allowed, jnp.exp(scores - new_max[..., None]), 0.0)
    running_sum = running_sum * factor + jnp.sum(weights, axis=-1)
    weighted = weighted * jnp.transpose(factor, (0, 2, 1))[..., None] + jnp.einsum(
        "rhqk,rkhd->rqhd",
        weights.astype(jnp.bfloat16),
        value_block,
        preferred_element_type=jnp.float32,
    )
    return (new_max, running_sum, weighted)


def attention_forward(queries, key_heads, value_heads, own_ids, segment_ids, key_mask):
    row_count, frames = (queries.shape[0], queries.shape[1])

    def block_step(running, blocks, offset):
        key_block, value_block = blocks
        allowed = allowed_pairs(own_ids, segment_ids, key_mask, offset, key_block.shape[1])[:, None]
        return forward_compute(running, (queries, key_block, value_block, allowed))

    def update(running, block_in, offset):
        return fold_blocks(block_step, running, block_in, math.gcd(block_in[0].shape[1], frames))

    start_state = (
        jnp.full((row_count, HEADS, frames), MASKED, jnp.float32),
        jnp.zeros((row_count, HEADS, frames), jnp.float32),
        jnp.zeros(queries.shape, jnp.float32),
    )
    running_max, running_sum, weighted = update(
        start_state,
        (
            lax.all_gather(key_heads, "seq", axis=1, tiled=True),
            lax.all_gather(value_heads, "seq", axis=1, tiled=True),
        ),
        jnp.int32(0),
    )
    attended = weighted / jnp.transpose(running_sum, (0, 2, 1))[..., None]
    return (attended, running_max + jnp.log(running_sum))


def query_side(inputs):
    queries, grad_att, log_sum, row_delta, key_block, value_block, allowed = inputs
    scores = (
        jnp.einsum("rqhd,rkhd->rhqk", queries, key_block, preferred_element_type=jnp.float32)
        * 0.125
    )
    attn_probs = jnp.where(allowed, jnp.exp(scores - log_sum[..., None]), 0.0)
    grad_probs = jnp.einsum(
        "rqhd,rkhd->rhqk", grad_att, value_block, preferred_element_type=jnp.float32
    )
    grad_scores = (attn_probs * (grad_probs - row_delta[..., None])).astype(jnp.bfloat16)
    return (attn_probs, grad_scores)


def attention_backward(
    queries, key_heads, value_heads, grad_att, row_delta, log_sum, own_ids, segment_ids, key_mask
):
    row_count, frames = (queries.shape[0], queries.shape[1])
    row_len = segment_ids.shape[1]
    zeros_query = jnp.zeros(queries.shape, jnp.float32)

    def block_step(running, blocks, offset):
        key_block, value_block = blocks
        piece_len = key_block.shape[1]
        allowed = allowed_pairs(own_ids, segment_ids, key_mask, offset, piece_len)[:, None]
        inputs = (queries, grad_att, log_sum, row_delta, key_block, value_block, allowed)
        grad_query, grad_keys, grad_values = running
        attn_probs, grad_scores = query_side(inputs)
        part_rows = grad_query.shape[0]
        grad_query = (
            grad_query
            + jnp.einsum(
                "rhqk,rkhd->rqhd", grad_scores, inputs[4], preferred_element_type=jnp.float32
            )
            * 0.125
        )
        key_term = (
            jnp.einsum(
                "rhqk,rqhd->rkhd", grad_scores, inputs[0], preferred_element_type=jnp.float32
            )
            * 0.125
        )
        value_term = jnp.einsum(
            "rhqk,rqhd->rkhd",
            attn_probs.astype(jnp.bfloat16),
            inputs[1],
            preferred_element_type=jnp.float32,
        )
        key_old = lax.dynamic_slice_in_dim(grad_keys, offset, piece_len, 1)
        value_old = lax.dynamic_slice_in_dim(grad_values, offset, piece_len, 1)
        grad_keys = lax.dynamic_update_slice_in_dim(
            grad_keys, key_old + key_term.reshape(part_rows, piece_len, HEADS * HEAD), offset, 1
        )
        grad_values = lax.dynamic_update_slice_in_dim(
            grad_values,
            value_old + value_term.reshape(part_rows, piece_len, HEADS * HEAD),
            offset,
            1,
        )
        return (grad_query, grad_keys, grad_values)

    zeros_full = jnp.zeros((row_count, row_len, HEADS * HEAD), jnp.float32)
    start_state = (zeros_query, zeros_full, zeros_full)

    def update(running, block_in, offset):
        return fold_blocks(block_step, running, block_in, math.gcd(block_in[0].shape[1], frames))

    folded = update(
        start_state,
        (
            lax.all_gather(key_heads, "seq", axis=1, tiled=True),
            lax.all_gather(value_heads, "seq", axis=1, tiled=True),
        ),
        jnp.int32(0),
    )
    grad_keys, grad_values = (
        lax.psum_scatter(
            folded[1].astype(jnp.bfloat16), "seq", scatter_dimension=1, tiled=True
        ).astype(jnp.float32),
        lax.psum_scatter(
            folded[2].astype(jnp.bfloat16), "seq", scatter_dimension=1, tiled=True
        ).astype(jnp.float32),
    )
    return (folded[0], grad_keys, grad_values)


def on_device(
    mel_inputs,
    text_ids,
    segment_ids,
    key_mask,
    time_index,
    input_proj,
    conv_first,
    conv_second,
    time_table,
    adaln_proj,
    qkv_proj,
    out_proj,
    up_proj,
    down_proj,
    text_table,
    grad_out,
):
    row_count, frames = (mel_inputs.shape[0], mel_inputs.shape[1])
    tokens = row_count * frames
    first_frame = lax.axis_index("seq") * frames
    owner_flag = (lax.axis_index("seq") == 0).astype(jnp.float32)
    gathered = (
        lax.all_gather(input_proj, ("batch", "seq"), axis=1, tiled=True),
        lax.all_gather(conv_first, ("batch", "seq"), axis=1, tiled=True),
        lax.all_gather(conv_second, ("batch", "seq"), axis=1, tiled=True),
        lax.all_gather(time_table, ("batch", "seq"), axis=1, tiled=True),
        lax.all_gather(adaln_proj, ("batch", "seq"), axis=1, tiled=True),
        lax.all_gather(qkv_proj, ("batch", "seq"), axis=1, tiled=True),
        lax.all_gather(out_proj, ("batch", "seq"), axis=1, tiled=True),
        lax.all_gather(up_proj, ("batch", "seq"), axis=1, tiled=True),
        lax.all_gather(down_proj, ("batch", "seq"), axis=1, tiled=True),
        lax.all_gather(text_table, ("batch", "seq"), axis=1, tiled=True),
    )
    (
        full_in,
        full_first,
        full_second,
        full_time,
        full_ada,
        full_qkv,
        full_out,
        full_up,
        full_down,
        full_text,
    ) = gathered
    seg_index = jnp.arange(SEGS, dtype=jnp.int32)
    own_ids = lax.dynamic_slice_in_dim(segment_ids, first_frame, frames, 1)
    select = (own_ids[:, :, None] == seg_index).astype(jnp.float32)
    near_masks = neighbour_masks(segment_ids, first_frame, frames)
    text_embed = jnp.take(full_text, text_ids.reshape(-1), axis=0)
    joined = jnp.concatenate([mel_inputs.reshape(tokens, 2 * MEL), text_embed], axis=1)
    hidden = matmul(joined, full_in).reshape(row_count, frames, D)
    padded_one = widen(hidden.astype(jnp.bfloat16))
    conv_one = conv_apply(padded_one, full_first, near_masks)
    act_one = mish_curve(conv_one).astype(jnp.bfloat16)
    padded_two = widen(act_one)
    conv_two = conv_apply(padded_two, full_second, near_masks)
    embedded = hidden + mish_curve(conv_two)
    cond_rows = jnp.take(full_time, time_index.reshape(-1), axis=0)
    cond_value = cond_rows.astype(jnp.float32)
    soft_cond = jax.nn.silu(cond_value).astype(jnp.bfloat16)
    modulation = matmul(soft_cond, full_ada).reshape(row_count, SEGS, 6 * D)
    per_frame = jnp.einsum("rfs,rsc->rfc", select, modulation, precision=EXACT)
    shift_attn, scale_attn, gate_attn, shift_feed, scale_feed, gate_feed = jnp.split(
        per_frame, 6, axis=2
    )
    normed = modulate(embedded, scale_attn, shift_attn).astype(jnp.bfloat16)
    projected = matmul(normed.reshape(tokens, D), full_qkv)
    query_raw, key_raw, value_raw = jnp.split(
        projected.reshape(row_count, frames, 3 * HEADS, HEAD), 3, axis=2
    )
    starts = jnp.sum((segment_ids[:, None, :] < seg_index[None, :, None]).astype(jnp.int32), axis=2)
    own_start = jnp.sum(jnp.where(own_ids[:, :, None] == seg_index, starts[:, None, :], 0), axis=2)
    positions = (first_frame + jnp.arange(frames, dtype=jnp.int32)[None, :] - own_start).astype(
        jnp.float32
    )
    cos_tab, sin_tab = rotary_tables(positions)
    turned_query = rotate(query_raw, cos_tab, sin_tab).astype(jnp.bfloat16)
    turned_key = rotate(key_raw, cos_tab, sin_tab).astype(jnp.bfloat16)
    value_heads = value_raw.astype(jnp.bfloat16)
    attended, log_sum = attention_forward(
        turned_query, turned_key, value_heads, own_ids, segment_ids, key_mask
    )
    attended_low = attended.reshape(tokens, D).astype(jnp.bfloat16)
    branch = matmul(attended_low, full_out).reshape(row_count, frames, D)
    middle = embedded + gate_attn * branch
    normed_feed = modulate(middle, scale_feed, shift_feed).astype(jnp.bfloat16)
    up_value = matmul(normed_feed.reshape(tokens, D), full_up)
    gelu_low = gelu_curve(up_value).astype(jnp.bfloat16)
    feed_out = matmul(gelu_low, full_down).reshape(row_count, frames, D)
    block_out = (middle + gate_feed * feed_out).astype(jnp.bfloat16)
    cotangent = grad_out.astype(jnp.float32)
    grad_gate_feed = cotangent * feed_out
    grad_feed = (gate_feed * cotangent).astype(jnp.bfloat16).reshape(tokens, D)
    grad_down = contract_rows(gelu_low, grad_feed)
    grad_gelu = matmul_back(grad_feed, full_down)
    grad_up_value = jax.vjp(gelu_curve, up_value)[1](grad_gelu)[0].astype(jnp.bfloat16)
    grad_up = contract_rows(normed_feed.reshape(tokens, D), grad_up_value)
    grad_normed_feed = matmul_back(grad_up_value, full_up).reshape(row_count, frames, D)
    grad_mid_part, grad_scale_feed, grad_shift_feed = jax.vjp(
        modulate, middle, scale_feed, shift_feed
    )[1](grad_normed_feed)
    grad_middle = cotangent + grad_mid_part
    grad_gate_attn = grad_middle * branch
    grad_branch = (gate_attn * grad_middle).astype(jnp.bfloat16).reshape(tokens, D)
    grad_out_weights = contract_rows(attended_low, grad_branch)
    grad_att = (
        matmul_back(grad_branch, full_out)
        .astype(jnp.bfloat16)
        .reshape(row_count, frames, HEADS, HEAD)
    )
    row_delta = jnp.transpose(jnp.sum(grad_att.astype(jnp.float32) * attended, axis=-1), (0, 2, 1))
    grad_query, grad_keys, grad_values = attention_backward(
        turned_query,
        turned_key,
        value_heads,
        grad_att,
        row_delta,
        log_sum,
        own_ids,
        segment_ids,
        key_mask,
    )
    head_shape = (row_count, frames, HEADS, HEAD)
    grad_projected = (
        jnp.concatenate(
            [
                rotate(grad_query, cos_tab, -sin_tab),
                rotate(grad_keys.reshape(head_shape), cos_tab, -sin_tab),
                grad_values.reshape(head_shape),
            ],
            axis=2,
        )
        .astype(jnp.bfloat16)
        .reshape(tokens, 3 * D)
    )
    grad_qkv_weights = contract_rows(normed.reshape(tokens, D), grad_projected)
    grad_normed = matmul_back(grad_projected, full_qkv).reshape(row_count, frames, D)
    grad_emb_part, grad_scale_attn, grad_shift_attn = jax.vjp(
        modulate, embedded, scale_attn, shift_attn
    )[1](grad_normed)
    grad_embedded = grad_middle + grad_emb_part
    grad_frame = jnp.concatenate(
        [
            grad_shift_attn,
            grad_scale_attn,
            grad_gate_attn,
            grad_shift_feed,
            grad_scale_feed,
            grad_gate_feed,
        ],
        axis=2,
    )
    local_sums = jnp.einsum("rfs,rfc->rsc", select, grad_frame, precision=EXACT)
    grad_mod = lax.psum(local_sums.astype(jnp.bfloat16), "seq").reshape(row_count * SEGS, 6 * D)
    step_hot = (
        time_index.reshape(-1)[:, None] == jnp.arange(STEPS, dtype=jnp.int32)[None, :]
    ).astype(jnp.bfloat16)
    grad_adaln = contract_rows(soft_cond, grad_mod) * owner_flag
    grad_soft = matmul_back(grad_mod, full_ada)
    grad_cond = jax.vjp(jax.nn.silu, cond_value)[1](grad_soft)[0]
    grad_time = jnp.dot(step_hot.astype(jnp.float32).T, grad_cond, precision=EXACT) * owner_flag
    grad_conv_two = jax.vjp(mish_curve, conv_two)[1](grad_embedded)[0].astype(jnp.bfloat16)
    grad_act_one, grad_second = conv_back(
        padded_two, widen(grad_conv_two), grad_conv_two, full_second, near_masks
    )
    grad_conv_one = jax.vjp(mish_curve, conv_one)[1](grad_act_one)[0].astype(jnp.bfloat16)
    grad_hidden_conv, grad_first = conv_back(
        padded_one, widen(grad_conv_one), grad_conv_one, full_first, near_masks
    )
    grad_hidden = (grad_embedded + grad_hidden_conv).astype(jnp.bfloat16).reshape(tokens, D)
    grad_input = contract_rows(joined, grad_hidden)
    grad_joined = matmul_back(grad_hidden, full_in)
    grad_mels = grad_joined[:, : 2 * MEL].reshape(row_count, frames, 2 * MEL)
    grad_embed = grad_joined[:, 2 * MEL :].astype(jnp.bfloat16)
    text_hot = (
        text_ids.reshape(-1)[:, None] == jnp.arange(VOCAB, dtype=jnp.int32)[None, :]
    ).astype(jnp.bfloat16)
    grad_text = contract_rows(text_hot, grad_embed)
    reduced = (
        lax.psum_scatter(grad_input, ("batch", "seq"), scatter_dimension=1, tiled=True),
        lax.psum_scatter(grad_first, ("batch", "seq"), scatter_dimension=1, tiled=True),
        lax.psum_scatter(grad_second, ("batch", "seq"), scatter_dimension=1, tiled=True),
        lax.psum_scatter(grad_time, ("batch", "seq"), scatter_dimension=1, tiled=True),
        lax.psum_scatter(grad_adaln, ("batch", "seq"), scatter_dimension=1, tiled=True),
        lax.psum_scatter(grad_qkv_weights, ("batch", "seq"), scatter_dimension=1, tiled=True),
        lax.psum_scatter(grad_out_weights, ("batch", "seq"), scatter_dimension=1, tiled=True),
        lax.psum_scatter(grad_up, ("batch", "seq"), scatter_dimension=1, tiled=True),
        lax.psum_scatter(grad_down, ("batch", "seq"), scatter_dimension=1, tiled=True),
        lax.psum_scatter(grad_text, ("batch", "seq"), scatter_dimension=1, tiled=True),
    )
    return (
        block_out,
        grad_mels,
        reduced[0],
        reduced[1],
        reduced[2],
        reduced[3],
        reduced[4],
        reduced[5],
        reduced[6],
        reduced[7],
        reduced[8],
        reduced[9],
    )


def solution(mesh):
    in_specs = (
        P("batch", "seq", None),
        P("batch", "seq"),
        P("batch", None),
        P("batch", None),
        P("batch", None),
        P(None, ("batch", "seq")),
        P(None, ("batch", "seq"), None),
        P(None, ("batch", "seq"), None),
        P(None, ("batch", "seq")),
        P(None, ("batch", "seq")),
        P(None, ("batch", "seq")),
        P(None, ("batch", "seq")),
        P(None, ("batch", "seq")),
        P(None, ("batch", "seq")),
        P(None, ("batch", "seq")),
        P("batch", "seq", None),
    )
    out_specs = (
        P("batch", "seq", None),
        P("batch", "seq", None),
        P(None, ("batch", "seq")),
        P(None, ("batch", "seq"), None),
        P(None, ("batch", "seq"), None),
        P(None, ("batch", "seq")),
        P(None, ("batch", "seq")),
        P(None, ("batch", "seq")),
        P(None, ("batch", "seq")),
        P(None, ("batch", "seq")),
        P(None, ("batch", "seq")),
        P(None, ("batch", "seq")),
    )
    return jax.shard_map(
        on_device, mesh=mesh, in_specs=in_specs, out_specs=out_specs, check_vma=False
    )
```

profile of v0, /device:TPU:1, one launch (start us, length us, event | category | flops | bytes accessed | tf_op | source)
XLA Modules:
  0.0 3450.2 jit_solution(13149546287737103825)
XLA Ops:
  15.7 44.2 %all_gather.42 = bf16[32,1024]{0,1:T(8,128)(2,1)S(1)} all-gather(bf16[32,32]{0,1:T(8,128)(2,1)S(1)} %copy.2774), channel_id=1, replica_groups=mesh['batch'=4,'seq'=8] {'batch','seq'}, dimensions={1}, use_global_device_ids=true | all-gather | bytes 67584 | tf_op jit(solution)/shard_map/all_gather | solution.py:341
  64.1 7.3 all-gather.12.cloned.1.call-done
  77.0 51.2 %all-gather.14.cloned.1.call-done = bf16[712,1024]{0,1:T(8,128)(2,1)} async-done(((bf16[712,32]{0,1:T(8,128)(2,1)}), bf16[712,1024]{0,1:T(8,128)(2,1)}) %all-gather.14.cloned.1.call-update) | async-done | bytes 1458192 | tf_op jit(solution)/shard_map/all_gather | solution.py:338
  274.8 15.4 bitcast_add_fusion.46
  448.0 15.4 bitcast_add_fusion.32
  476.8 7.9 fusion.585
  525.6 52.2 %all-gather.26.cloned.1.call-done = bf16[2,1536,16,64]{3,2,0,1:T(8,128)(2,1)} async-done(((bf16[2,192,16,64]{3,2,0,1:T(8,128)(2,1)}), bf16[2,1536,16,64]{3,2,0,1:T(8,128)(2,1)}) %all-gather.26.cloned.1.call-update) | async-done | bytes 6291472 | tf_op jit(solution)/shard_map/all_gather | solution.py:221
  577.7 17.4 copy.2790
  595.1 56.6 %all-gather.24.cloned.1.call-done = bf16[2,1536,16,64]{3,2,0,1:T(8,128)(2,1)} async-done(((bf16[2,192,16,64]{3,2,0,1:T(8,128)(2,1)}), bf16[2,1536,16,64]{3,2,0,1:T(8,128)(2,1)}) %all-gather.24.cloned.1.call-update) | async-done | bytes 6291472 | tf_op jit(solution)/shard_map/all_gather | solution.py:220
  651.8 17.3 copy.2791
  669.1 79.0 %while.30 = (s32[]{:T(128)}, f32[2,16,192]{2,1,0:T(8,128)S(1)}, f32[2,16,192]{2,1,0:T(8,128)S(1)}, f32[2,192,16,64]{1,3,2,0:T(8,128)S(1)}, s32[2,192]{1,0:T(2,12...) while((s32[]{:T(128)}, f32[2,16,192]{2,1,0:T(8,128)S(1)}, ...), condition=%wide.region_7.8_spmd.clone, body=%wide.region_4.7_spmd.clone.sunk | while | flops 318689664 | bytes 20881900 | solution.py:174
  762.2 12.3 all-gather.32.cloned.1.call-done
  780.4 57.7 %all-gather.30.cloned.1.call-done = bf16[1024,2048]{0,1:T(8,128)(2,1)} async-done(((bf16[1024,64]{0,1:T(8,128)(2,1)}), bf16[1024,2048]{0,1:T(8,128)(2,1)}) %all-gather.30.cloned.1.call-update) | async-done | bytes 4194320 | tf_op jit(solution)/shard_map/all_gather | solution.py:345
  838.1 7.2 fusion.53
  871.4 301.7 %while.31 = (s32[]{:T(128)}, f32[2,192,16,64]{1,3,2,0:T(8,128)}, f32[2,1536,1024]{2,0,1:T(2,128)}, f32[2,1536,1024]{2,0,1:T(2,128)}, bf16[8,2,192,16,64]{2,4,3,1...) while((s32[]{:T(128)}, f32[2,192,16,64]{1,3,2,0:T(8,128)}, ...), condition=%wide.region_14.15_spmd.clone, body=%wide.region_13.14_spmd.clone.sunk | while | flops 769278336 | bytes 91267744 | solution.py:174
  1173.1 10.7 convert_element_type.289
  1194.3 165.9 %all-reduce.8.cloned.1.call-done = (bf16[2,1536,1024]{2,0,1:T(2,128)(2,1)}, bf16[2,1536,1024]{2,0,1:T(2,128)(2,1)}) async-done(((bf16[2,1536,1024]{2,0,1:T(2,128)(2,1)}, bf16[2,1536,1024]{2,0,1:T(2,128)(2,1)}), (bf16[2,1536,1024]{2,0,1:T(2,128)(2,1)}, bf16[2,1536,1024]{2,0,1:T(2,128)(2,1)})) %all-reduce.8.cloned.1.call-update) | async-done | bytes 12582928
  1541.3 19.0 bitcast_add_fusion.18
  1748.8 19.0 bitcast_add_fusion.4
  1781.9 6.9 convolution_convert_fusion
  1790.0 52.7 %all-reduce.6.cloned.1.call-done = bf16[8,6144]{1,0:T(8,128)(2,1)} async-done(((bf16[8,6144]{1,0:T(8,128)(2,1)}), bf16[8,6144]{1,0:T(8,128)(2,1)}) %all-reduce.6.cloned.1.call-update) | async-done | bytes 98320 | tf_op jit(solution)/shard_map/psum | solution.py:470
  1866.6 7.6 fusion.591
  1988.4 10.2 broadcast_multiply_fusion
  2001.9 117.0 %reduce-scatter.23.cloned.1.call-done = f32[1024,32]{0,1:T(8,128)} async-done(((f32[1024,1024]{0,1:T(8,128)}), f32[1024,32]{0,1:T(8,128)}) %reduce-scatter.23.cloned.1.call-update) | async-done | bytes 131088 | tf_op jit(solution)/shard_map/reduce_scatter | solution.py:502
  2118.9 107.8 %reduce-scatter.13.cloned.1.call-done = f32[712,32]{0,1:T(8,128)} async-done(((f32[712,1024]{0,1:T(8,128)}), f32[712,32]{0,1:T(8,128)}) %reduce-scatter.13.cloned.1.call-update) | async-done | bytes 91152 | tf_op jit(solution)/shard_map/reduce_scatter | solution.py:496
  2226.7 147.0 %reduce-scatter.25.cloned.1.call-done = f32[1024,64]{0,1:T(8,128)} async-done(((f32[1024,2048]{0,1:T(8,128)}), f32[1024,64]{0,1:T(8,128)}) %reduce-scatter.25.cloned.1.call-update) | async-done | bytes 262160 | tf_op jit(solution)/shard_map/reduce_scatter | solution.py:503
  2373.7 147.6 %reduce-scatter.27.cloned.1.call-done = f32[2048,32]{0,1:T(8,128)} async-done(((f32[2048,1024]{0,1:T(8,128)}), f32[2048,32]{0,1:T(8,128)}) %reduce-scatter.27.cloned.1.call-update) | async-done | bytes 262160 | tf_op jit(solution)/shard_map/reduce_scatter | solution.py:504
  2521.3 142.0 %reduce-scatter.29.cloned.1.call-done = f32[2546,16]{0,1:T(8,128)} async-done(((f32[2546,512]{0,1:T(8,128)}), f32[2546,16]{0,1:T(8,128)}) %reduce-scatter.29.cloned.1.call-update) | async-done | bytes 162960 | tf_op jit(solution)/shard_map/reduce_scatter | solution.py:505
  2663.3 182.0 %reduce-scatter.17.cloned.1.call-done = f32[31,32,64]{2,1,0:T(8,128)} async-done(((f32[31,1024,64]{2,1,0:T(8,128)}), f32[31,32,64]{2,1,0:T(8,128)}) %reduce-scatter.17.cloned.1.call-update) | async-done | bytes 253968 | tf_op jit(solution)/shard_map/reduce_scatter | solution.py:498
  2845.3 182.0 %reduce-scatter.15.cloned.1.call-done = f32[31,32,64]{2,1,0:T(8,128)} async-done(((f32[31,1024,64]{2,1,0:T(8,128)}), f32[31,32,64]{2,1,0:T(8,128)}) %reduce-scatter.15.cloned.1.call-update) | async-done | bytes 253968 | tf_op jit(solution)/shard_map/reduce_scatter | solution.py:497
  3027.3 163.4 %reduce-scatter.21.cloned.1.call-done = f32[1024,96]{0,1:T(8,128)} async-done(((f32[1024,3072]{0,1:T(8,128)}), f32[1024,96]{0,1:T(8,128)}) %reduce-scatter.21.cloned.1.call-update) | async-done | bytes 393232 | tf_op jit(solution)/shard_map/reduce_scatter | solution.py:501
  3190.8 252.7 %reduce-scatter.19.cloned.1.call-done = f32[1024,192]{0,1:T(8,128)} async-done(((f32[1024,6144]{0,1:T(8,128)}), f32[1024,192]{0,1:T(8,128)}) %reduce-scatter.19.cloned.1.call-update) | async-done | bytes 786448 | tf_op jit(solution)/shard_map/reduce_scatter | solution.py:500
  (1484 shorter events, 1325.6 us)
Async XLA Ops:
  7.2 64.3 %all-gather.12.cloned.1.call-start = ((), (), s32[]{:S(2)}) async-start(), calls=%async_computation.10 | async-start | bytes 2703360 | tf_op jit(solution)/shard_map/all_gather | solution.py:347
  7.9 120.3 %all-gather.14.cloned.1.call-start = ((), (), s32[]{:S(2)}) async-start(), calls=%async_computation.11 | async-start | bytes 1622016 | tf_op jit(solution)/shard_map/all_gather | solution.py:338
  8.7 213.6 %all-gather.16.cloned.1.call-start = ((), (), s32[]{:S(2)}) async-start(), calls=%async_computation.12 | async-start | bytes 8380416 | tf_op jit(solution)/shard_map/all_gather | solution.py:339
  9.4 288.0 %all-gather.18.cloned.1.call-start = ((), (), s32[]{:S(2)}) async-start(), calls=%async_computation.13 | async-start | bytes 8380416 | tf_op jit(solution)/shard_map/all_gather | solution.py:340
  10.0 466.3 %all-gather.20.cloned.1.call-start = ((), (), s32[]{:S(2)}) async-start(), calls=%async_computation.14 | async-start | bytes 12976128 | tf_op jit(solution)/shard_map/all_gather | solution.py:342
  10.6 484.3 %all-gather.22.cloned.1.call-start = ((), (), s32[]{:S(2)}) async-start(), calls=%async_computation.15 | async-start | bytes 6488064 | tf_op jit(solution)/shard_map/all_gather | solution.py:343
  11.1 566.6 %all-gather.26.cloned.1.call-start = ((), (), s32[]{:S(2)}) async-start(), calls=%async_computation.17 | async-start | bytes 14155776 | tf_op jit(solution)/shard_map/all_gather | solution.py:221
  131.7 10.6 collective-permute-start.1
  135.2 15.5 collective-permute-start
  308.5 17.4 collective-permute-start.2
  311.6 6.0 collective-permute-start.3
  316.9 118.7 %copy-start.187 = (bf16[1,1024,64]{2,1,0:T(8,128)(2,1)}, bf16[1,1024,64]{2,1,0:T(8,128)(2,1)S(1)}, u32[]{:S(2)}) copy-start(bf16[1,1024,64]{2,1,0:T(8,128)(2,1)S(1)} %get-tuple-element.554) | copy-start | bytes 393220
  506.5 145.3 %all-gather.24.cloned.1.call-start = ((), (), s32[]{:S(2)}) async-start(), calls=%async_computation.16 | async-start | bytes 14155776 | tf_op jit(solution)/shard_map/all_gather | solution.py:220
  523.2 228.1 %all-gather.28.cloned.1.call-start = ((), (), s32[]{:S(2)}) async-start(), calls=%async_computation.18 | async-start | bytes 2162688 | tf_op jit(solution)/shard_map/all_gather | solution.py:344
  523.9 250.6 %all-gather.32.cloned.1.call-start = ((), (), s32[]{:S(2)}) async-start(), calls=%async_computation.20 | async-start | bytes 4325376 | tf_op jit(solution)/shard_map/all_gather | solution.py:346
  524.5 313.6 %all-gather.30.cloned.1.call-start = ((), (), s32[]{:S(2)}) async-start(), calls=%async_computation.19 | async-start | bytes 4325376 | tf_op jit(solution)/shard_map/all_gather | solution.py:345
  525.3 834.9 %all-reduce.8.cloned.1.call-start = ((), (), s32[]{:S(2)}) async-start(), calls=%async_computation.32 | async-start | bytes 25165824
  1189.3 653.4 %all-reduce.6.cloned.1.call-start = ((), (), s32[]{:S(2)}) async-start(), calls=%async_computation.24 | async-start | bytes 196608 | tf_op jit(solution)/shard_map/psum | solution.py:470
  1389.7 29.3 collective-permute-start.4
  1393.5 5.8 collective-permute-start.5
  1569.2 32.2 collective-permute-start.6
  1571.7 5.8 collective-permute-start.7
  1789.4 211.1 %reduce-scatter.31.cloned.1.call-start = ((), (), s32[]{:S(2)}) async-start(), calls=%async_computation.31 | async-start | bytes 540672
  1850.5 268.4 %reduce-scatter.23.cloned.1.call-start = ((), (), s32[]{:S(2)}) async-start(), calls=%async_computation.27 | async-start | bytes 4325376 | tf_op jit(solution)/shard_map/reduce_scatter | solution.py:502
  1854.0 372.6 %reduce-scatter.13.cloned.1.call-start = ((), (), s32[]{:S(2)}) async-start(), calls=%async_computation.21 | async-start | bytes 3244032 | tf_op jit(solution)/shard_map/reduce_scatter | solution.py:496
  1858.1 515.6 %reduce-scatter.25.cloned.1.call-start = ((), (), s32[]{:S(2)}) async-start(), calls=%async_computation.28 | async-start | bytes 8650752 | tf_op jit(solution)/shard_map/reduce_scatter | solution.py:503
  1865.4 655.8 %reduce-scatter.27.cloned.1.call-start = ((), (), s32[]{:S(2)}) async-start(), calls=%async_computation.29 | async-start | bytes 8650752 | tf_op jit(solution)/shard_map/reduce_scatter | solution.py:504
  1874.2 789.1 %reduce-scatter.29.cloned.1.call-start = ((), (), s32[]{:S(2)}) async-start(), calls=%async_computation.30 | async-start | bytes 5406720 | tf_op jit(solution)/shard_map/reduce_scatter | solution.py:505
  1891.0 954.3 %reduce-scatter.17.cloned.1.call-start = ((), (), s32[]{:S(2)}) async-start(), calls=%async_computation.23 | async-start | bytes 16760832 | tf_op jit(solution)/shard_map/reduce_scatter | solution.py:498
  1926.4 1101.0 %reduce-scatter.15.cloned.1.call-start = ((), (), s32[]{:S(2)}) async-start(), calls=%async_computation.22 | async-start | bytes 16760832 | tf_op jit(solution)/shard_map/reduce_scatter | solution.py:497
  1967.7 1223.1 %reduce-scatter.21.cloned.1.call-start = ((), (), s32[]{:S(2)}) async-start(), calls=%async_computation.26 | async-start | bytes 12976128 | tf_op jit(solution)/shard_map/reduce_scatter | solution.py:501
  1987.5 1456.0 %reduce-scatter.19.cloned.1.call-start = ((), (), s32[]{:S(2)}) async-start(), calls=%async_computation.25 | async-start | bytes 25952256 | tf_op jit(solution)/shard_map/reduce_scatter | solution.py:500
  (327 other events, 2385.6 us)
Sparse Core Ops, SparseCore 0:
  10.8 60.5 all-gather.11
  74.3 53.8 all-gather.13
  131.1 82.1 all-gather.15
  216.0 81.4 all-gather.17
  300.1 94.4 all-gather.19
  397.3 67.7 all-gather.21
  506.6 71.0 all-gather.25
  579.6 72.1 all-gather.23
  654.6 56.3 all-gather.27
  713.8 60.6 all-gather.31
  777.4 60.6 all-gather.29
  1189.4 170.6 all-reduce.7
  1789.5 53.1 all-reduce.5
  1850.6 128.6 reduce-scatter.30
  1982.2 136.6 reduce-scatter.22
  2125.6 100.9 reduce-scatter.12
  2229.5 144.1 reduce-scatter.24
  2376.5 144.7 reduce-scatter.26
  2524.2 138.9 reduce-scatter.28
  2666.1 179.1 reduce-scatter.16
  2848.2 179.0 reduce-scatter.14
  3035.0 155.7 reduce-scatter.20
  3197.8 245.6 reduce-scatter.18
where the time goes:
time: 3460 us; the launch traced here: 3450 us
  waiting for transfers between devices  1910 us (55%)
  matrix products  628 us (18%)
  local copies, waits for them, and re-layouts  624 us (18%)
  other arithmetic  190 us (5%)
  blocking collectives  44.2 us (1%)
    reduce_scatter x1, waiting for transfers between devices, on_device(): lax.psum_scatter(grad_adaln, ('batch', 'seq'), scatter_dimension=1, tiled...  253 us
    dot_general x62, matrix products, conv_back(): jnp.einsum('rfgo,gio->rfgi', grad_block, grouped[KERNEL - 1 - kernel_tap]...  210 us
    reduce_scatter x1, waiting for transfers between devices, on_device(): lax.psum_scatter(grad_second, ('batch', 'seq'), scatter_dimension=1, tile...  182 us
    reduce_scatter x1, waiting for transfers between devices, on_device(): lax.psum_scatter(grad_first, ('batch', 'seq'), scatter_dimension=1, tiled...  182 us
    unnamed x25, waiting for transfers between devices  172 us
    reduce_scatter x1, waiting for transfers between devices, on_device(): lax.psum_scatter(grad_qkv_weights, ('batch', 'seq'), scatter_dimension=1,...  163 us
    reduce_scatter x1, waiting for transfers between devices, on_device(): lax.psum_scatter(grad_down, ('batch', 'seq'), scatter_dimension=1, tiled=...  148 us
    reduce_scatter x1, waiting for transfers between devices, on_device(): lax.psum_scatter(grad_up, ('batch', 'seq'), scatter_dimension=1, tiled=True)  147 us
  transfers between devices with their start and end apart: 31, of which 21 were waited for; matrix products, arithmetic and copies ran while one was open for 20% of the time, Pallas kernels for 0%

commit v1 on v0

v1 whole, which is shorter than its diff:
```python
import functools

import jax
import jax.numpy as jnp
import numpy as np
from jax import lax
from jax.experimental import pallas as pl
from jax.experimental.pallas import tpu as pltpu
from jax.sharding import PartitionSpec as P

D = 1024
HEADS = 16
HEAD = 64
MEL = 100
VOCAB = 2546
KERNEL = 31
HALF = KERNEL // 2
CHAN = 64
STEPS = 32
SEGS = 4
GAP = 16
FOLD = 4
TAPS = KERNEL + FOLD - 1

EPSILON = 1e-06
MASKED = -1e30
EXACT = lax.Precision.HIGHEST
MESH = pl.DeviceIdType.MESH
ANY = pl.BlockSpec(memory_space=pl.ANY)
VMEM_LIMIT = 56 * 1024 * 1024
F32 = jnp.float32
BF16 = jnp.bfloat16


def dims():
    return lax.axis_size("batch"), lax.axis_size("seq")


def params(cid=None):
    if cid is None:
        return pltpu.CompilerParams(vmem_limit_bytes=VMEM_LIMIT)
    return pltpu.CompilerParams(
        collective_id=cid, has_side_effects=True, vmem_limit_bytes=VMEM_LIMIT
    )


def greet_all(nb, n, b, s):
    sem = pltpu.get_barrier_semaphore()
    me = b * n + s
    for d in range(1, nb * n):
        other = lax.rem(me + d, nb * n)
        pl.semaphore_signal(
            sem,
            inc=1,
            device_id={"batch": other // n, "seq": lax.rem(other, n)},
            device_id_type=MESH,
        )
    pl.semaphore_wait(sem, nb * n - 1)


def greet_group(n, s):
    sem = pltpu.get_barrier_semaphore()
    for d in range(1, n):
        pl.semaphore_signal(
            sem, inc=1, device_id={"seq": lax.rem(s + d, n)}, device_id_type=MESH
        )
    pl.semaphore_wait(sem, n - 1)


def remote(src, dst, send, recv, **where):
    return pltpu.make_async_remote_copy(
        src_ref=src,
        dst_ref=dst,
        send_sem=send,
        recv_sem=recv,
        device_id=where,
        device_id_type=MESH,
    )


def swap_kernel(count, n, parts, *refs):
    ins, outs = refs[:count], refs[count : 2 * count]
    send, recv, local = refs[2 * count :]
    s = lax.axis_index("seq")
    greet_group(n, s)
    copies = []
    for a in range(count):
        src, dst = parts(ins[a], outs[a], s)
        own = pltpu.make_async_copy(src(s), dst, local.at[a])
        own.start()
        copies.append(own)
    for d in range(1, n):
        t = lax.rem(s + d, n)
        for a in range(count):
            src, dst = parts(ins[a], outs[a], s)
            copy = remote(src(t), dst, send.at[a, d], recv.at[a, d], seq=t)
            copy.start()
            copies.append(copy)
    for copy in copies:
        copy.wait()


def swap_call(arrays, shapes, parts, cid):
    n = dims()[1]
    count = len(arrays)
    return pl.pallas_call(
        functools.partial(swap_kernel, count, n, parts),
        out_shape=[jax.ShapeDtypeStruct(shape, a.dtype) for shape, a in zip(shapes, arrays)],
        in_specs=[ANY] * count,
        out_specs=[ANY] * count,
        scratch_shapes=[
            pltpu.SemaphoreType.DMA((count, n)),
            pltpu.SemaphoreType.DMA((count, n)),
            pltpu.SemaphoreType.DMA((count,)),
        ],
        compiler_params=params(cid),
    )(*arrays)


def blocks_part(x, o, s):
    return (lambda t: x.at[t]), o.at[s]


def to_channels(arrays, cid):
    n = dims()[1]
    rows, frames = arrays[0].shape[:2]
    width = arrays[0].shape[2] // n
    if width % 128 == 0:

        def parts(x, o, s):
            first = pl.multiple_of(s * frames, 16)
            return (
                lambda t: x.at[:, :, pl.ds(pl.multiple_of(t * width, 128), width)]
            ), o.at[:, pl.ds(first, frames), :]

        return swap_call(arrays, [(rows, n * frames, width)] * len(arrays), parts, cid)
    split = [a.reshape(rows, frames, n, width).transpose(2, 0, 1, 3) for a in arrays]
    got = swap_call(split, [a.shape for a in split], blocks_part, cid)
    return [g.transpose(1, 0, 2, 3).reshape(rows, n * frames, width) for g in got]


def to_frames(arrays, cid):
    n = dims()[1]
    rows, length, width = arrays[0].shape
    frames = length // n
    if width % 128 == 0:

        def parts(x, o, s):
            first = pl.multiple_of(s * width, 128)
            return (
                lambda t: x.at[:, pl.ds(pl.multiple_of(t * frames, 16), frames), :]
            ), o.at[:, :, pl.ds(first, width)]

        return swap_call(arrays, [(rows, frames, n * width)] * len(arrays), parts, cid)
    split = [a.reshape(rows, n, frames, width).transpose(1, 0, 2, 3) for a in arrays]
    got = swap_call(split, [a.shape for a in split], blocks_part, cid)
    return [g.transpose(1, 2, 0, 3).reshape(rows, frames, n * width) for g in got]


def group_gather_kernel(n, x, o, send, recv, local):
    s = lax.axis_index("seq")
    core = lax.rem(s, 2)
    sibling = s + 1 - 2 * core
    chips = n // 2
    greet_group(n, s)
    own = pltpu.make_async_copy(x, o.at[:, s], local)
    own.start()
    far, near = [], []
    for d in range(1, chips):
        copy = remote(x, o.at[:, s], send.at[d], recv.at[d], seq=lax.rem(s + 2 * d, n))
        copy.start()
        far.append(copy)
    copy = remote(x, o.at[:, s], send.at[0], recv.at[0], seq=sibling)
    copy.start()
    near.append(copy)
    for d in range(1, chips):
        far[d - 1].wait_recv()
        source = lax.rem(s - 2 * d + n, n)
        copy = remote(
            o.at[:, source],
            o.at[:, source],
            send.at[chips + d],
            recv.at[chips + d],
            seq=sibling,
        )
        copy.start()
        near.append(copy)
    own.wait()
    for copy in far:
        copy.wait_send()
    for copy in near:
        copy.wait()


def group_gather(x, cid):
    n = dims()[1]
    return pl.pallas_call(
        functools.partial(group_gather_kernel, n),
        out_shape=jax.ShapeDtypeStruct((x.shape[0], n) + x.shape[1:], x.dtype),
        in_specs=[ANY],
        out_specs=ANY,
        scratch_shapes=[
            pltpu.SemaphoreType.DMA((n,)),
            pltpu.SemaphoreType.DMA((n,)),
            pltpu.SemaphoreType.DMA,
        ],
        compiler_params=params(cid),
    )(x)


def group_sum_kernel(n, x, o, mine, first, passed, second, total, send, recv, local, out_sem):
    s = lax.axis_index("seq")
    core = lax.rem(s, 2)
    sibling = s + 1 - 2 * core
    chips = n // 2
    chip = s // 2
    greet_group(n, s)
    order = [lax.rem(chip + d, chips) for d in list(range(1, chips)) + [0]]
    pair, own = [], []
    for k, c in enumerate(order):
        copy = remote(
            x.at[:, 2 * c + 1 - core], first.at[k], send.at[k], recv.at[k], seq=sibling
        )
        copy.start()
        pair.append(copy)
        copy = pltpu.make_async_copy(x.at[:, 2 * c + core], mine.at[k], local.at[k])
        copy.start()
        own.append(copy)
    rows, frames = x.shape[0], x.shape[2]
    step = 16
    far = []
    for k in range(chips):
        pair[k].wait_recv()
        own[k].wait()
        if k < chips - 1:

            def add(i, carry, k=k):
                at = pl.ds(pl.multiple_of(i * step, step), step)
                for r in range(rows):
                    passed[k, r, at, :] = (
                        mine[k, r, at, :].astype(F32) + first[k, r, at, :].astype(F32)
                    ).astype(BF16)
                return carry

            lax.fori_loop(0, frames // step, add, 0)
            copy = remote(
                passed.at[k],
                second.at[k],
                send.at[chips + k],
                recv.at[chips + k],
                seq=2 * order[k] + core,
            )
            copy.start()
            far.append(copy)
    for copy in far:
        copy.wait_recv()

    def finish(i, carry):
        at = pl.ds(pl.multiple_of(i * step, step), step)
        for r in range(rows):
            value = mine[chips - 1, r, at, :].astype(F32) + first[chips - 1, r, at, :].astype(F32)
            for k in range(chips - 1):
                value = value + second[k, r, at, :].astype(F32)
            total[r, at, :] = value
        return carry

    lax.fori_loop(0, frames // step, finish, 0)
    out = pltpu.make_async_copy(total, o, out_sem)
    out.start()
    for copy in pair + far:
        copy.wait_send()
    out.wait()


def group_sum(x, cid):
    n = dims()[1]
    rows, _, frames, width = x.shape
    chips = n // 2
    slots = pltpu.VMEM((chips, rows, frames, width), BF16)
    fewer = pltpu.VMEM((chips - 1, rows, frames, width), BF16)
    return pl.pallas_call(
        functools.partial(group_sum_kernel, n),
        out_shape=jax.ShapeDtypeStruct((rows, frames, width), F32),
        in_specs=[ANY],
        out_specs=ANY,
        scratch_shapes=[
            slots,
            slots,
            fewer,
            fewer,
            pltpu.VMEM((rows, frames, width), F32),
            pltpu.SemaphoreType.DMA((n,)),
            pltpu.SemaphoreType.DMA((n,)),
            pltpu.SemaphoreType.DMA((chips,)),
            pltpu.SemaphoreType.DMA,
        ],
        compiler_params=params(cid),
    )(x)


def start_kernel(nb, n, wide, *refs):
    count = wide + 3
    ins, outs = refs[:count], refs[count : 2 * count]
    z_send, z_recv, p_send, p_recv, c_send, c_recv, local, g_send, g_recv = refs[2 * count :]
    b, s = lax.axis_index("batch"), lax.axis_index("seq")
    core = lax.rem(s, 2)
    sibling = s + 1 - 2 * core
    chips = n // 2
    ndev = nb * n
    me = b * n + s
    greet_all(nb, n, b, s)
    copies = []
    z_copies = {}
    for a in range(wide):
        copy = pltpu.make_async_copy(ins[a], outs[a].at[b, s], local.at[a])
        copy.start()
        copies.append(copy)
    for d in range(1, nb):
        for a in range(wide):
            copy = remote(
                ins[a],
                outs[a].at[b, s],
                z_send.at[a, d],
                z_recv.at[a, d],
                batch=lax.rem(b + d, nb),
                seq=s,
            )
            copy.start()
            z_copies[a, d] = copy
    far = []
    near = []

    def spread(a, d):
        plane = lax.rem(b - d + nb, nb)
        source = ins[a] if d == 0 else outs[a].at[plane, s]
        for c in range(1, chips):
            copy = remote(
                source,
                outs[a].at[plane, s],
                p_send.at[a, d, c],
                p_recv.at[a, d, c],
                seq=lax.rem(s + 2 * c, n),
            )
            copy.start()
            far.append((a, d, c, plane, copy))
        copy = remote(
            source,
            outs[a].at[plane, s],
            c_send.at[a, d, 0],
            c_recv.at[a, d, 0],
            seq=sibling,
        )
        copy.start()
        near.append(copy)

    for a in range(wide):
        spread(a, 0)

    pieces = []
    for a in range(2):
        pieces.append((ins[wide + a], outs[wide + a], me // nb, lax.rem(me, nb), a))
    for j in range(3):
        granule = 3 * me + j
        part = granule // ndev
        column = lax.rem(granule, ndev)
        pieces.append(
            (
                ins[wide + 2].at[j],
                outs[wide + 2].at[part],
                column // nb,
                lax.rem(column, nb),
                2 + j,
            )
        )
    slots = [g_recv.at[0], g_recv.at[1], g_recv.at[2], g_recv.at[3], g_recv.at[4]]
    sends = []
    for source, target, owner, slot, k in pieces:
        if k < 2:
            arrived = g_recv.at[k, slot]
        else:
            arrived = g_recv.at[2 + (3 * me + k - 2) // ndev, slot]
        for d in range(nb):
            plane = lax.rem(b + d, nb)
            if d == 0:

                @pl.when(owner == s)
                def _(source=source, target=target, slot=slot, arrived=arrived):
                    pltpu.make_async_copy(source, target.at[slot], arrived).start()

                @pl.when(owner != s)
                def _(source=source, target=target, slot=slot, arrived=arrived, k=k, owner=owner, plane=plane):
                    remote(
                        source,
                        target.at[slot],
                        g_send.at[k, 0],
                        arrived,
                        batch=plane,
                        seq=owner,
                    ).start()
            else:
                copy = remote(
                    source, target.at[slot], g_send.at[k, d], arrived, batch=plane, seq=owner
                )
                copy.start()
                sends.append(copy)

    for d in range(1, nb):
        for a in range(wide):
            z_copies[a, d].wait_recv()
            spread(a, d)
    for a, d, c, plane, copy in far:
        copy.wait_recv()
        source = lax.rem(s - 2 * c + n, n)
        onward = remote(
            outs[a].at[plane, source],
            outs[a].at[plane, source],
            c_send.at[a, d, c],
            c_recv.at[a, d, c],
            seq=sibling,
        )
        onward.start()
        near.append(onward)
    for copy in copies:
        copy.wait()
    for copy in z_copies.values():
        copy.wait_send()
    for entry in far:
        entry[4].wait_send()
    for copy in near:
        copy.wait()
    for copy in sends:
        copy.wait_send()
    for source, target, owner, slot, k in pieces:

        @pl.when(owner != s)
        def _(source=source, target=target, slot=slot, k=k, owner=owner):
            remote(
                source, target.at[slot], g_send.at[k, 0], g_recv.at[k, slot], batch=b, seq=owner
            ).wait_send()

    for a in range(2):
        for j in range(nb):
            pltpu.make_async_copy(ins[wide + a], outs[wide + a].at[j], g_recv.at[a, j]).wait()
    for p in range(3):
        for j in range(nb):
            pltpu.make_async_copy(
                ins[wide + 2].at[0], outs[wide + 2].at[p, j], g_recv.at[2 + p, j]
            ).wait()


def start_gather(wide_arrays, conv_first, conv_second, qkv_rows, cid):
    nb, n = dims()
    chips = n // 2
    wide = len(wide_arrays)
    arrays = list(wide_arrays) + [conv_first, conv_second, qkv_rows]
    shapes = [(nb, n) + a.shape for a in wide_arrays]
    shapes += [(nb,) + conv_first.shape, (nb,) + conv_second.shape]
    shapes += [(3, nb) + qkv_rows.shape[1:]]
    dma = pltpu.SemaphoreType.DMA
    return pl.pallas_call(
        functools.partial(start_kernel, nb, n, wide),
        out_shape=[jax.ShapeDtypeStruct(sh, a.dtype) for sh, a in zip(shapes, arrays)],
        in_specs=[ANY] * len(arrays),
        out_specs=[ANY] * len(arrays),
        scratch_shapes=[
            dma((wide, nb)),
            dma((wide, nb)),
            dma((wide, nb, chips)),
            dma((wide, nb, chips)),
            dma((wide, nb, chips)),
            dma((wide, nb, chips)),
            dma((wide,)),
            dma((5, nb)),
            dma((5, nb)),
        ],
        compiler_params=params(cid),
    )(*arrays)


def spray_kernel(nb, n, by_batch, x, o, send, recv, local):
    b, s = lax.axis_index("batch"), lax.axis_index("seq")
    me = b * n + s
    ndev = nb * n
    greet_all(nb, n, b, s)
    own = pltpu.make_async_copy(x.at[b if by_batch else me], o.at[me], local)
    own.start()
    copies = []
    for d in range(1, ndev):
        other = lax.rem(me + d, ndev)
        plane, place = other // n, lax.rem(other, n)
        copy = remote(
            x.at[plane if by_batch else other],
            o.at[me],
            send.at[d],
            recv.at[d],
            batch=plane,
            seq=place,
        )
        copy.start()
        copies.append(copy)
    own.wait()
    for copy in copies:
        copy.wait()


def spray(x, by_batch, cid):
    nb, n = dims()
    ndev = nb * n
    return pl.pallas_call(
        functools.partial(spray_kernel, nb, n, by_batch),
        out_shape=jax.ShapeDtypeStruct((ndev,) + x.shape[1:], x.dtype),
        in_specs=[ANY],
        out_specs=ANY,
        scratch_shapes=[
            pltpu.SemaphoreType.DMA((ndev,)),
            pltpu.SemaphoreType.DMA((ndev,)),
            pltpu.SemaphoreType.DMA,
        ],
        compiler_params=params(cid),
    )(x)


def columns_kernel(nb, n, count, kinds, *refs):
    ins, outs = refs[:count], refs[count : 2 * count]
    send, recv = refs[2 * count :]
    b, s = lax.axis_index("batch"), lax.axis_index("seq")
    ndev = nb * n
    me = b * n + s
    greet_all(nb, n, b, s)
    base = 0
    pieces = []
    for a in range(count):
        for p in range(kinds[a]):
            for j in range(nb):
                column = p * ndev + s * nb + j
                owner = column // kinds[a]
                part = lax.rem(column, kinds[a])
                pieces.append(
                    (
                        ins[a].at[p, j],
                        outs[a].at[b, part],
                        owner,
                        send.at[base + p, j],
                        recv.at[b, base + part],
                    )
                )
        base += kinds[a]
    for source, target, owner, sent, arrived in pieces:

        @pl.when(owner == me)
        def _(source=source, target=target, arrived=arrived):
            pltpu.make_async_copy(source, target, arrived).start()

        @pl.when(owner != me)
        def _(source=source, target=target, owner=owner, sent=sent, arrived=arrived):
            remote(
                source, target, sent, arrived, batch=owner // n, seq=lax.rem(owner, n)
            ).start()

    for source, target, owner, sent, arrived in pieces:

        @pl.when(owner != me)
        def _(source=source, target=target, owner=owner, sent=sent, arrived=arrived):
            remote(
                source, target, sent, arrived, batch=owner // n, seq=lax.rem(owner, n)
            ).wait_send()

    base = 0
    for a in range(count):
        for p in range(kinds[a]):
            for j in range(nb):
                pltpu.make_async_copy(
                    ins[a].at[0, 0], outs[a].at[j, p], recv.at[j, base + p]
                ).wait()
        base += kinds[a]


def column_grads(arrays, cid):
    nb, n = dims()
    kinds = tuple(a.shape[0] for a in arrays)
    total = sum(kinds)
    return pl.pallas_call(
        functools.partial(columns_kernel, nb, n, len(arrays), kinds),
        out_shape=[
            jax.ShapeDtypeStruct((nb, a.shape[0]) + a.shape[2:], a.dtype) for a in arrays
        ],
        in_specs=[ANY] * len(arrays),
        out_specs=[ANY] * len(arrays),
        scratch_shapes=[
            pltpu.SemaphoreType.DMA((total, nb)),
            pltpu.SemaphoreType.DMA((nb, total)),
        ],
        compiler_params=params(cid),
    )(*arrays)


def scatter_kernel(nb, n, count, *refs):
    ins, outs = refs[:count], refs[count : 2 * count]
    scratch = refs[2 * count : 2 * count + 5 * count]
    send, recv, local, z_send, z_recv, z_local = refs[7 * count :]
    b, s = lax.axis_index("batch"), lax.axis_index("seq")
    core = lax.rem(s, 2)
    sibling = s + 1 - 2 * core
    chips = n // 2
    chip = s // 2
    greet_all(nb, n, b, s)
    order = [lax.rem(chip + d, chips) for d in list(range(1, chips)) + [0]]
    pair, own, far, last = {}, {}, {}, []
    for k, c in enumerate(order):
        for a in range(count):
            mine, first = scratch[5 * a], scratch[5 * a + 1]
            copy = remote(
                ins[a].at[:, 2 * c + 1 - core],
                first.at[k],
                send.at[a, k],
                recv.at[a, k],
                seq=sibling,
            )
            copy.start()
            pair[a, k] = copy
            copy = pltpu.make_async_copy(ins[a].at[:, 2 * c + core], mine.at[k], local.at[a, k])
            copy.start()
            own[a, k] = copy
    for k in range(chips - 1):
        for a in range(count):
            mine, first, passed, second, total = scratch[5 * a : 5 * a + 5]
            pair[a, k].wait_recv()
            own[a, k].wait()

            def add(i, carry, k=k, mine=mine, first=first, passed=passed):
                passed[k, i] = (mine[k, i].astype(F32) + first[k, i].astype(F32)).astype(BF16)
                return carry

            lax.fori_loop(0, nb, add, 0)
            copy = remote(
                passed.at[k],
                second.at[k],
                send.at[a, chips + k],
                recv.at[a, chips + k],
                seq=2 * order[k] + core,
            )
            copy.start()
            far[a, k] = copy
    for a in range(count):
        mine, first, passed, second, total = scratch[5 * a : 5 * a + 5]
        pair[a, chips - 1].wait_recv()
        own[a, chips - 1].wait()
        for k in range(chips - 1):
            far[a, k].wait_recv()

        def finish(i, carry, mine=mine, first=first, second=second, total=total):
            value = mine[chips - 1, i].astype(F32) + first[chips - 1, i].astype(F32)
            for k in range(chips - 1):
                value = value + second[k, i].astype(F32)
            total[i] = value.astype(BF16)
            return carry

        lax.fori_loop(0, nb, finish, 0)
        for d in range(1, nb):
            plane = lax.rem(b + d, nb)
            copy = remote(
                total.at[plane],
                outs[a].at[b],
                z_send.at[a, d],
                z_recv.at[a, d],
                batch=plane,
                seq=s,
            )
            copy.start()
            last.append(copy)
        copy = pltpu.make_async_copy(total.at[b], outs[a].at[b], z_local.at[a])
        copy.start()
        last.append(copy)
    for copy in list(pair.values()) + list(far.values()):
        copy.wait_send()
    for copy in last:
        copy.wait()


def scatter_sum(arrays, cid):
    nb, n = dims()
    chips = n // 2
    count = len(arrays)
    scratch = []
    for a in arrays:
        block = (nb,) + a.shape[2:]
        scratch += [
            pltpu.VMEM((chips,) + block, BF16),
            pltpu.VMEM((chips,) + block, BF16),
            pltpu.VMEM((chips - 1,) + block, BF16),
            pltpu.VMEM((chips - 1,) + block, BF16),
            pltpu.VMEM(block, BF16),
        ]
    dma = pltpu.SemaphoreType.DMA
    return pl.pallas_call(
        functools.partial(scatter_kernel, nb, n, count),
        out_shape=[jax.ShapeDtypeStruct((nb,) + a.shape[2:], a.dtype) for a in arrays],
        in_specs=[ANY] * count,
        out_specs=[ANY] * count,
        scratch_shapes=scratch
        + [
            dma((count, n)),
            dma((count, n)),
            dma((count, chips)),
            dma((count, nb)),
            dma((count, nb)),
            dma((count,)),
        ],
        compiler_params=params(cid),
    )(*arrays)


def mish_parts(v):
    e = jnp.exp(jnp.minimum(v, 20.0))
    n = e * (e + 2.0)
    inverse = 1.0 / (n + 2.0)
    return e, n, inverse


def mish(v):
    e, n, inverse = mish_parts(v)
    return v * (n * inverse)


def mish_slope(v):
    e, n, inverse = mish_parts(v)
    return n * inverse + v * (4.0 * e * (1.0 + e)) * inverse * inverse


CHUNK = 128


def place(buf, source, seg, length):
    rows = buf.shape[0]

    def clear(i, carry):
        buf[pl.ds(pl.multiple_of(i * 8, 8), 8), :] = jnp.zeros((8, buf.shape[1]), F32)
        return carry

    lax.fori_loop(0, rows // 8, clear, 0)

    def move(i, carry):
        at = pl.multiple_of(i * CHUNK, CHUNK)
        value = source(at)
        ids = seg[0, pl.ds(at, CHUNK), :]
        for u in range(SEGS):
            to = pl.ds(at + GAP * (u + 1), CHUNK)
            buf[to, :] = buf[to, :] + jnp.where(ids == u, value, 0.0)
        return carry

    lax.fori_loop(0, length // CHUNK, move, 0)


def unplace(buf, sink, seg, length):
    def move(i, carry):
        at = pl.multiple_of(i * CHUNK, CHUNK)
        ids = seg[0, pl.ds(at, CHUNK), :]
        value = buf[pl.ds(at + GAP, CHUNK), :]
        for u in range(1, SEGS):
            value = jnp.where(ids == u, buf[pl.ds(at + GAP * (u + 1), CHUNK), :], value)
        sink[0, pl.ds(at, CHUNK), :] = value.astype(sink.dtype)
        return carry

    lax.fori_loop(0, length // CHUNK, move, 0)


def spread_taps(x, buf, count, width):
    for k in range(TAPS):
        x[:, k * width : (k + 1) * width] = buf[pl.ds(k + 1, count, stride=FOLD), :].astype(BF16)


def fill_band(band, kernel, width):
    band[...] = jnp.zeros_like(band)
    for m in range(FOLD):
        band[m * width : (m + KERNEL) * width, m * width : (m + 1) * width] = kernel[...]


def conv_forward_kernel(count, length, width, u, seg, k1, k2, c1, c2, out, buf, live, x, band1, band2):
    @pl.when(pl.program_id(0) == 0)
    def _():
        fill_band(band1, k1, width)
        fill_band(band2, k2, width)

    place(live, lambda at: jnp.ones((CHUNK, width), F32), seg, length)
    place(buf, lambda at: u[0, pl.ds(at, CHUNK), :].astype(F32), seg, length)
    spread_taps(x, buf, count, width)
    c1[0] = jnp.dot(x[...], band1[...], preferred_element_type=F32)
    for m in range(FOLD):
        at = pl.ds(GAP + m, count, stride=FOLD)
        buf[at, :] = mish(c1[0, :, m * width : (m + 1) * width]) * live[at, :]
    spread_taps(x, buf, count, width)
    c2[0] = jnp.dot(x[...], band2[...], preferred_element_type=F32)
    for m in range(FOLD):
        at = pl.ds(GAP + m, count, stride=FOLD)
        buf[at, :] = mish(c2[0, :, m * width : (m + 1) * width])
    unplace(buf, out, seg, length)


def conv_sizes(length):
    count = -(-(length + GAP * (SEGS - 1)) // FOLD)
    count = -(-count // 16) * 16
    return count, FOLD * count + 48


def whole(shape):
    zeros = (0,) * len(shape)
    return pl.BlockSpec(shape, lambda *i: zeros)


def by_row(shape):
    return pl.BlockSpec((1,) + tuple(shape[1:]), lambda r: (r,) + (0,) * (len(shape) - 1))


def conv_forward(u, seg, k1, k2):
    rows, length, width = u.shape
    count, buffer = conv_sizes(length)
    folded = (rows, count, FOLD * width)
    return pl.pallas_call(
        functools.partial(conv_forward_kernel, count, length, width),
        grid=(rows,),
        in_specs=[by_row(u.shape), by_row(seg.shape), whole(k1.shape), whole(k2.shape)],
        out_specs=[by_row(folded), by_row(folded), by_row(u.shape)],
        out_shape=[
            jax.ShapeDtypeStruct(folded, F32),
            jax.ShapeDtypeStruct(folded, F32),
            jax.ShapeDtypeStruct(u.shape, BF16),
        ],
        scratch_shapes=[
            pltpu.VMEM((buffer, width), F32),
            pltpu.VMEM((buffer, width), F32),
            pltpu.VMEM((count, TAPS * width), BF16),
            pltpu.VMEM((TAPS * width, FOLD * width), BF16),
            pltpu.VMEM((TAPS * width, FOLD * width), BF16),
        ],
        compiler_params=params(),
    )(u, seg, k1, k2)


def weight_sums(grad, turned, x, width):
    pair = 2 * width
    for t in range(TAPS // 2):
        product = jnp.dot(
            turned[...], x[:, t * pair : (t + 1) * pair], preferred_element_type=F32
        )
        for half in range(2):
            for m in range(FOLD):
                k = 2 * t + half - m
                if 0 <= k < KERNEL:
                    grad[k] = grad[k] + product[
                        m * width : (m + 1) * width, half * width : (half + 1) * width
                    ]


def conv_backward_kernel(
    count, length, width, d, u, seg, c1, c2, k1, k2, dh, g1, g2, buf, grads, live, x, turned, band1, band2
):
    @pl.when(pl.program_id(0) == 0)
    def _():
        fill_band(band1, k1, width)
        fill_band(band2, k2, width)
        g1[...] = jnp.zeros_like(g1)
        g2[...] = jnp.zeros_like(g2)

    place(live, lambda at: jnp.ones((CHUNK, width), F32), seg, length)
    place(grads, lambda at: d[0, pl.ds(at, CHUNK), :].astype(F32), seg, length)
    for m in range(FOLD):
        at = pl.ds(GAP + m, count, stride=FOLD)
        lanes = slice(m * width, (m + 1) * width)
        value = grads[at, :] * mish_slope(c2[0, :, lanes])
        grads[at, :] = value
        turned[lanes, :] = value.T.astype(BF16)
    place(buf, lambda at: jnp.zeros((CHUNK, width), F32), seg, length)
    for m in range(FOLD):
        at = pl.ds(GAP + m, count, stride=FOLD)
        buf[at, :] = mish(c1[0, :, m * width : (m + 1) * width]) * live[at, :]
    spread_taps(x, buf, count, width)
    weight_sums(g2, turned, x, width)
    spread_taps(x, grads, count, width)
    folded = jnp.dot(x[...], band2[...], preferred_element_type=F32)
    for m in range(FOLD):
        at = pl.ds(GAP + m, count, stride=FOLD)
        lanes = slice(m * width, (m + 1) * width)
        value = folded[:, lanes] * mish_slope(c1[0, :, lanes]) * live[at, :]
        grads[at, :] = value
        turned[lanes, :] = value.T.astype(BF16)
    place(buf, lambda at: u[0, pl.ds(at, CHUNK), :].astype(F32), seg, length)
    spread_taps(x, buf, count, width)
    weight_sums(g1, turned, x, width)
    spread_taps(x, grads, count, width)
    folded = jnp.dot(x[...], band1[...], preferred_element_type=F32)
    for m in range(FOLD):
        at = pl.ds(GAP + m, count, stride=FOLD)
        buf[at, :] = folded[:, m * width : (m + 1) * width]
    unplace(buf, dh, seg, length)


def conv_backward(d, u, seg, c1, c2, k1, k2):
    rows, length, width = u.shape
    count, buffer = conv_sizes(length)
    grad = (KERNEL, width, width)
    band = pltpu.VMEM((TAPS * width, FOLD * width), BF16)
    return pl.pallas_call(
        functools.partial(conv_backward_kernel, count, length, width),
        grid=(rows,),
        in_specs=[
            by_row(d.shape),
            by_row(u.shape),
            by_row(seg.shape),
            by_row(c1.shape),
            by_row(c2.shape),
            whole(k1.shape),
            whole(k2.shape),
        ],
        out_specs=[by_row(u.shape), whole(grad), whole(grad)],
        out_shape=[
            jax.ShapeDtypeStruct(u.shape, BF16),
            jax.ShapeDtypeStruct(grad, F32),
            jax.ShapeDtypeStruct(grad, F32),
        ],
        scratch_shapes=[
            pltpu.VMEM((buffer, width), F32),
            pltpu.VMEM((buffer, width), F32),
            pltpu.VMEM((buffer, width), F32),
            pltpu.VMEM((count, TAPS * width), BF16),
            pltpu.VMEM((FOLD * width, count), BF16),
            band,
            band,
        ],
        compiler_params=params(),
    )(d, u, seg, c1, c2, k1, k2)


def pair_swap(x):
    width = x.shape[1]
    if width % 128:
        x = jnp.concatenate([x, x], axis=1)
    lane = lax.broadcasted_iota(jnp.int32, x.shape, 1)
    after = pltpu.roll(x, x.shape[1] - 1, 1)
    before = pltpu.roll(x, 1, 1)
    return jnp.where(lax.rem(lane, 2) == 0, -after, before)[:, :width]


def qkv_kernel(width, x, w, cos, sin, q, k, v):
    got = lax.dot_general(
        x[0], w[...], (((1,), (1,)), ((), ())), preferred_element_type=F32
    )
    for p, out in enumerate((q, k)):
        part = got[:, p * width : (p + 1) * width]
        out[0] = (part * cos[0] + pair_swap(part) * sin[0]).astype(BF16)
    v[0] = got[:, 2 * width :].astype(BF16)


def qkv_forward(x, w, cos, sin):
    rows, length, depth = x.shape
    width = w.shape[0] // 3
    block = 512
    spec = pl.BlockSpec((1, block, width), lambda r, i: (r, i, 0))
    shape = jax.ShapeDtypeStruct((rows, length, width), BF16)
    return pl.pallas_call(
        functools.partial(qkv_kernel, width),
        grid=(rows, length // block),
        in_specs=[
            pl.BlockSpec((1, block, depth), lambda r, i: (r, i, 0)),
            whole(w.shape),
            spec,
            spec,
        ],
        out_specs=[spec] * 3,
        out_shape=[shape] * 3,
        compiler_params=params(),
    )(x, w, cos, sin)


def attention_forward_kernel(width, q, k, v, q_code, k_code, out, low, log_sum):
    heads = width // HEAD
    lane = lax.broadcasted_iota(jnp.int32, q.shape[1:], 1) // HEAD
    allowed = q_code[0] == k_code[0]
    queries = q[0] * 0.125
    result, logs = None, None
    for h in range(heads):
        chosen = jnp.where(lane == h, queries, jnp.zeros_like(queries))
        scores = lax.dot_general(
            chosen, k[0], (((1,), (1,)), ((), ())), preferred_element_type=F32
        )
        scores = jnp.where(allowed, scores, MASKED)
        peak = jnp.max(scores, axis=1, keepdims=True)
        weights = jnp.exp(scores - peak)
        total = jnp.sum(weights, axis=1, keepdims=True)
        value = jnp.dot(weights.astype(BF16), v[0], preferred_element_type=F32) / total
        log = jnp.broadcast_to(peak + jnp.log(total), value.shape)
        result = value if h == 0 else jnp.where(lane == h, value, result)
        logs = log if h == 0 else jnp.where(lane == h, log, logs)
    out[0] = result
    low[0] = result.astype(BF16)
    log_sum[0] = logs


def attention_forward(q, k, v, q_code, k_code):
    rows, length, width = q.shape
    block = 256
    spec = pl.BlockSpec((1, block, width), lambda r, i: (r, i, 0))
    row = pl.BlockSpec((1, length, width), lambda r, i: (r, 0, 0))
    return pl.pallas_call(
        functools.partial(attention_forward_kernel, width),
        grid=(rows, length // block),
        in_specs=[
            spec,
            row,
            row,
            pl.BlockSpec((1, block, 1), lambda r, i: (r, i, 0)),
            pl.BlockSpec((1, 1, length), lambda r, i: (r, 0, 0)),
        ],
        out_specs=[spec] * 3,
        out_shape=[
            jax.ShapeDtypeStruct(q.shape, F32),
            jax.ShapeDtypeStruct(q.shape, BF16),
            jax.ShapeDtypeStruct(q.shape, F32),
        ],
        compiler_params=params(),
    )(q, k, v, q_code, k_code)


BLOCK = 256


def attention_backward_kernel(
    length, width, low_edge, high_edge, q, k, v, g, log_sum, delta, k_code, q_code, cos, sin, out, dq, dk, dv
):
    heads = width // HEAD
    row = pl.program_id(0)
    lane = lax.broadcasted_iota(jnp.int32, (BLOCK, width), 1) // HEAD
    dk[...] = jnp.zeros_like(dk)
    dv[...] = jnp.zeros_like(dv)

    def outer(i, carry):
        at = pl.ds(pl.multiple_of(i * BLOCK, BLOCK), BLOCK)
        queries = q[0, at, :] * 0.125
        grads = g[0, at, :]
        zero = jnp.zeros_like(queries)
        queries_of = [jnp.where(lane == h, queries, zero) for h in range(heads)]
        grads_of = [jnp.where(lane == h, grads, zero) for h in range(heads)]
        dq[...] = jnp.zeros_like(dq)

        def inner(j, carry):
            to = pl.ds(pl.multiple_of(j * BLOCK, BLOCK), BLOCK)
            keys, values = k[0, to, :], v[0, to, :]
            allowed = k_code[0, to, :] == q_code[0, :, at]
            dk_part, dv_part, dq_part = None, None, None
            for h in range(heads):
                keys_of = jnp.where(lane == h, keys, zero)
                scores = lax.dot_general(
                    keys, queries_of[h], (((1,), (1,)), ((), ())), preferred_element_type=F32
                )
                probs = jnp.where(allowed, jnp.exp(scores - log_sum[0, h : h + 1, at]), 0.0)
                grad_probs = lax.dot_general(
                    values, grads_of[h], (((1,), (1,)), ((), ())), preferred_element_type=F32
                )
                grad_scores = (probs * (grad_probs - delta[0, h : h + 1, at])).astype(BF16)
                a = jnp.dot(probs.astype(BF16), grads_of[h], preferred_element_type=F32)
                c = jnp.dot(grad_scores, queries_of[h], preferred_element_type=F32)
                e = lax.dot_general(
                    grad_scores, keys_of, (((0,), (0,)), ((), ())), preferred_element_type=F32
                )
                dv_part = a if h == 0 else dv_part + a
                dk_part = c if h == 0 else dk_part + c
                dq_part = e if h == 0 else dq_part + e
            dv[to, :] = dv[to, :] + dv_part
            dk[to, :] = dk[to, :] + dk_part
            dq[...] = dq[...] + dq_part
            return carry

        lax.fori_loop(low_edge[row, i], high_edge[row, i], inner, 0)
        grad = dq[...] * 0.125
        turned = grad * cos[0, at, :] - pair_swap(grad) * sin[0, at, :]
        out[0, at, 0:width] = turned.astype(BF16)
        return carry

    lax.fori_loop(0, length // BLOCK, outer, 0)

    def finish(i, carry):
        at = pl.ds(pl.multiple_of(i * BLOCK, BLOCK), BLOCK)
        grad = dk[at, :]
        turned = grad * cos[0, at, :] - pair_swap(grad) * sin[0, at, :]
        out[0, at, width : 2 * width] = turned.astype(BF16)
        out[0, at, 2 * width : 3 * width] = dv[at, :].astype(BF16)
        return carry

    lax.fori_loop(0, length // BLOCK, finish, 0)


def attention_backward(q, k, v, g, log_sum, delta, k_code, q_code, cos, sin, low_edge, high_edge):
    rows, length, width = q.shape

    def spec(shape):
        return pl.BlockSpec((1,) + tuple(shape[1:]), lambda r, *_: (r,) + (0,) * (len(shape) - 1))

    arrays = (q, k, v, g, log_sum, delta, k_code, q_code, cos, sin)
    out = (rows, length, 3 * width)
    return pl.pallas_call(
        functools.partial(attention_backward_kernel, length, width),
        grid_spec=pltpu.PrefetchScalarGridSpec(
            num_scalar_prefetch=2,
            grid=(rows,),
            in_specs=[spec(a.shape) for a in arrays],
            out_specs=spec(out),
            scratch_shapes=[
                pltpu.VMEM((BLOCK, width), F32),
                pltpu.VMEM((length, width), F32),
                pltpu.VMEM((length, width), F32),
            ],
        ),
        out_shape=jax.ShapeDtypeStruct(out, BF16),
        compiler_params=params(),
    )(low_edge, high_edge, *arrays)


def times(left, right):
    return lax.dot_general(left, right, (((1,), (0,)), ((), ())), preferred_element_type=F32)


def times_t(left, right):
    return lax.dot_general(left, right, (((1,), (1,)), ((), ())), preferred_element_type=F32)


def rows_sum(left, right):
    return lax.dot_general(left, right, (((0,), (0,)), ((), ())), preferred_element_type=F32)


def layer_norm(field):
    centre = field - jnp.mean(field, axis=-1, keepdims=True)
    return centre * lax.rsqrt(jnp.mean(centre * centre, axis=-1, keepdims=True) + EPSILON)


def modulate(field, scaling, shifting):
    return layer_norm(field) * (1.0 + scaling) + shifting


def gelu_curve(inputs):
    return jax.nn.gelu(inputs, approximate=True)


def by_segment(ids, table):
    value = table[:, SEGS - 1][:, None, :]
    for u in range(SEGS - 2, -1, -1):
        value = jnp.where(ids[:, :, None] == u, table[:, u][:, None, :], value)
    return value


def rope_tables(segment_ids, starts, width):
    length = segment_ids.shape[1]
    pairs = (np.arange(width) % HEAD) // 2
    freq = 10000.0 ** (-2.0 * pairs / HEAD)
    angle = np.arange(length)[:, None] * freq[None, :]
    cos_t = jnp.asarray(np.cos(angle).astype(np.float32))[None]
    sin_t = jnp.asarray(np.sin(angle).astype(np.float32))[None]
    offset = starts.astype(F32)[:, :, None] * jnp.asarray(freq.astype(np.float32))
    cos_o = by_segment(segment_ids, jnp.cos(offset))
    sin_o = by_segment(segment_ids, jnp.sin(offset))
    return cos_t * cos_o + sin_t * sin_o, sin_t * cos_o - cos_t * sin_o


def conv_blocks(got, width):
    own = jnp.moveaxis(got, 0, 1).reshape(KERNEL, width, CHAN)
    groups = width // CHAN
    if groups == 1:
        return own
    index = np.arange(width) // CHAN
    same = jnp.asarray((index[:, None] == index[None, :]).astype(np.float32)).astype(BF16)
    return jnp.tile(own, (1, 1, groups)) * same


def on_device(
    mel_inputs,
    text_ids,
    segment_ids,
    key_mask,
    time_index,
    input_proj,
    conv_first,
    conv_second,
    time_table,
    adaln_proj,
    qkv_proj,
    out_proj,
    up_proj,
    down_proj,
    text_table,
    grad_out,
):
    nb, n = dims()
    ndev = nb * n
    rows, frames = mel_inputs.shape[:2]
    tokens = rows * frames
    length = frames * n
    width = D // n
    part = D // ndev
    mine = lax.axis_index("seq")
    first_frame = mine * frames

    out_t, up_t, down_t = out_proj.T, up_proj.T, down_proj.T
    wide_t = jnp.concatenate([out_t, up_t, down_t[:, :D], down_t[:, D:]], axis=0)
    per = wide_t.shape[0]
    late = lax.all_gather(wide_t, ("batch", "seq"), axis=0, tiled=True).reshape(ndev, per, D)

    full_in, full_text, full_time, all_index, got_first, got_second, got_qkv = start_gather(
        [input_proj.T, text_table.T, time_table.T, time_index],
        conv_first,
        conv_second,
        qkv_proj.T.reshape(3, part, D),
        0,
    )
    in_t = full_in.reshape(D, input_proj.shape[0])
    text_t = full_text.reshape(-1, VOCAB)
    time_t = full_time.reshape(D, STEPS)
    slot_steps = all_index[:, 0].reshape(nb * rows * SEGS)
    qkv_t = got_qkv.reshape(3 * width, D)
    block_first = conv_blocks(got_first, width)
    block_second = conv_blocks(got_second, width)

    own_ids = lax.dynamic_slice_in_dim(segment_ids, first_frame, frames, 1)
    seg_column = segment_ids[:, :, None]
    seg_index = jnp.arange(SEGS, dtype=jnp.int32)
    starts = jnp.sum((segment_ids[:, None, :] < seg_index[None, :, None]).astype(jnp.int32), axis=2)

    text_hot = (
        text_ids.reshape(-1)[:, None] == jnp.arange(VOCAB, dtype=jnp.int32)[None, :]
    ).astype(BF16)
    text_embed = times_t(text_hot, text_t).astype(BF16)
    joined = jnp.concatenate([mel_inputs.reshape(tokens, 2 * MEL), text_embed], axis=1)
    hidden = times_t(joined, in_t).reshape(rows, frames, D)

    step_hot = (
        slot_steps[:, None] == jnp.arange(STEPS, dtype=jnp.int32)[None, :]
    ).astype(BF16)
    cond_value = times_t(step_hot, time_t)
    soft_cond = jax.nn.silu(cond_value).astype(BF16)
    own_mod = times(soft_cond, adaln_proj)
    mod_got = spray(own_mod.reshape(nb, rows * SEGS, 6 * part), True, 1)
    modulation = mod_got.transpose(1, 0, 2).reshape(rows, SEGS, 6, D)
    shift_attn, scale_attn, gate_attn, shift_feed, scale_feed, gate_feed = (
        by_segment(own_ids, modulation[:, :, i]) for i in range(6)
    )

    (hidden_c,) = to_channels([hidden.astype(BF16)], 2)
    conv_one, conv_two, bump_c = conv_forward(
        hidden_c,
        seg_column,
        block_first.reshape(KERNEL * width, width),
        block_second.reshape(KERNEL * width, width),
    )
    (bump,) = to_frames([bump_c], 3)
    embedded = hidden + bump.astype(F32)

    normed = modulate(embedded, scale_attn, shift_attn).astype(BF16)
    normed_all = group_gather(normed, 4).reshape(rows, length, D)
    cos, sin = rope_tables(segment_ids, starts, width)
    query, key, value = qkv_forward(normed_all, qkv_t, cos, sin)
    seg_code = segment_ids.astype(F32)
    key_code = jnp.where(key_mask > 0, seg_code, -1.0)
    attended, attended_low, log_lanes = attention_forward(
        query, key, value, seg_code[:, :, None], key_code[:, None, :]
    )
    (attended_own,) = to_frames([attended_low], 5)
    attended_own = attended_own.reshape(tokens, D)

    full_out = late[:, :part].reshape(D, D)
    full_up = late[:, part : 3 * part].reshape(2 * D, D)
    full_down = jnp.concatenate([late[:, 3 * part : 4 * part], late[:, 4 * part :]], axis=2).reshape(
        D, 2 * D
    )

    branch = times_t(attended_own, full_out).reshape(rows, frames, D)
    middle = embedded + gate_attn * branch
    normed_feed = modulate(middle, scale_feed, shift_feed).astype(BF16).reshape(tokens, D)
    up_value = times_t(normed_feed, full_up)
    gelu_low = gelu_curve(up_value).astype(BF16)
    feed_out = times_t(gelu_low, full_down).reshape(rows, frames, D)
    block_out = (middle + gate_feed * feed_out).astype(BF16)

    cotangent = grad_out.astype(F32)
    grad_gate_feed = cotangent * feed_out
    grad_feed = (gate_feed * cotangent).astype(BF16).reshape(tokens, D)
    grad_down = rows_sum(grad_feed, gelu_low).astype(BF16)
    grad_gelu = times(grad_feed, full_down)
    grad_up_value = jax.vjp(gelu_curve, up_value)[1](grad_gelu)[0].astype(BF16)
    grad_up = rows_sum(grad_up_value, normed_feed).astype(BF16)
    grad_normed_feed = times(grad_up_value, full_up).reshape(rows, frames, D)
    grad_mid_part, grad_scale_feed, grad_shift_feed = jax.vjp(
        modulate, middle, scale_feed, shift_feed
    )[1](grad_normed_feed)
    grad_middle = cotangent + grad_mid_part
    grad_gate_attn = grad_middle * branch
    grad_branch = (gate_attn * grad_middle).astype(BF16).reshape(tokens, D)
    grad_out_weights = rows_sum(grad_branch, attended_own).astype(BF16)
    grad_att = times(grad_branch, full_out).astype(BF16).reshape(rows, frames, D)

    late_grads = jnp.concatenate(
        [
            grad_out_weights.reshape(ndev, part, D),
            grad_up.reshape(ndev, 2 * part, D),
            grad_down[:, :D].reshape(ndev, part, D),
            grad_down[:, D:].reshape(ndev, part, D),
        ],
        axis=1,
    )
    late_sum = lax.psum_scatter(
        late_grads, ("batch", "seq"), scatter_dimension=0, tiled=False
    ).astype(F32)

    (grad_att_c,) = to_channels([grad_att], 6)
    heads = width // HEAD
    delta = jnp.sum(
        (grad_att_c.astype(F32) * attended).reshape(rows, length, heads, HEAD), axis=3
    ).transpose(0, 2, 1)
    log_rows = log_lanes.reshape(rows, length, heads, HEAD)[:, :, :, 0].transpose(0, 2, 1)
    block_first_ids = segment_ids[:, ::BLOCK]
    block_last_ids = segment_ids[:, BLOCK - 1 :: BLOCK]
    ends = jnp.sum((segment_ids[:, None, :] <= seg_index[None, :, None]).astype(jnp.int32), axis=2)
    low_edge = (
        jnp.sum(jnp.where(block_first_ids[:, :, None] == seg_index, starts[:, None, :], 0), axis=2)
        // BLOCK
    )
    high_edge = (
        jnp.sum(jnp.where(block_last_ids[:, :, None] == seg_index, ends[:, None, :], 0), axis=2)
        + BLOCK
        - 1
    ) // BLOCK
    grad_projected = attention_backward(
        query,
        key,
        value,
        grad_att_c,
        log_rows,
        delta,
        key_code[:, :, None],
        seg_code[:, None, :],
        cos,
        sin,
        low_edge,
        high_edge,
    ).reshape(rows * length, 3 * width)
    grad_qkv = rows_sum(grad_projected, normed_all.reshape(rows * length, D)).astype(BF16)
    grad_normed = group_sum(
        times(grad_projected, qkv_t).astype(BF16).reshape(rows, n, frames, D), 7
    )

    grad_emb_part, grad_scale_attn, grad_shift_attn = jax.vjp(
        modulate, embedded, scale_attn, shift_attn
    )[1](grad_normed)
    grad_embedded = grad_middle + grad_emb_part

    select = (own_ids[:, :, None] == seg_index).astype(F32)
    grad_frame = jnp.concatenate(
        [
            grad_shift_attn,
            grad_scale_attn,
            grad_gate_attn,
            grad_shift_feed,
            grad_scale_feed,
            grad_gate_feed,
        ],
        axis=2,
    )
    local_sums = jnp.einsum("rfs,rfc->rsc", select, grad_frame, precision=EXACT)
    slots = rows * SEGS
    sums_out = local_sums.reshape(slots, ndev, 6 * part).transpose(1, 0, 2)
    sums_got = spray(sums_out, False, 8).reshape(nb, n, slots, 6 * part)
    grad_mod = jnp.sum(sums_got, axis=1).astype(BF16).reshape(nb * slots, 6 * part)
    grad_adaln = rows_sum(soft_cond, grad_mod)
    soft_part = times_t(grad_mod, adaln_proj)
    soft_got = spray(soft_part.reshape(nb * slots, ndev, part).transpose(1, 0, 2), False, 9)
    grad_soft = jnp.sum(soft_got, axis=0)
    own_cond = times(step_hot, time_table)
    grad_cond = jax.vjp(jax.nn.silu, own_cond)[1](grad_soft)[0]
    grad_time = jnp.dot(step_hot.astype(F32).T, grad_cond, precision=EXACT)

    (grad_emb_c,) = to_channels([grad_embedded.astype(BF16)], 10)
    flip_first = block_first[::-1].transpose(0, 2, 1).reshape(KERNEL * width, width)
    flip_second = block_second[::-1].transpose(0, 2, 1).reshape(KERNEL * width, width)
    grad_hidden_c, sums_first, sums_second = conv_backward(
        grad_emb_c, hidden_c, seg_column, conv_one, conv_two, flip_first, flip_second
    )
    (grad_hidden_conv,) = to_frames([grad_hidden_c], 11)

    def conv_pieces(sums):
        groups = width // CHAN
        own = jnp.stack(
            [
                sums[:, g * CHAN : (g + 1) * CHAN, g * CHAN : (g + 1) * CHAN]
                for g in range(groups)
            ],
            axis=1,
        )
        own = own.transpose(0, 1, 3, 2).reshape(KERNEL, nb, part, CHAN)
        return jnp.moveaxis(own, 1, 0)[None].astype(BF16)

    got = column_grads(
        [
            conv_pieces(sums_first),
            conv_pieces(sums_second),
            grad_qkv.reshape(3, nb, part, D),
        ],
        12,
    )
    grad_first = jnp.sum(got[0].astype(F32), axis=0)[0]
    grad_second = jnp.sum(got[1].astype(F32), axis=0)[0]
    grad_qkv_own = jnp.sum(got[2].astype(F32), axis=0).reshape(3 * part, D).T

    grad_hidden = (grad_embedded + grad_hidden_conv.astype(F32)).astype(BF16).reshape(tokens, D)
    grad_input = rows_sum(grad_hidden, joined).astype(BF16)
    grad_joined = times(grad_hidden, in_t)
    grad_mels = grad_joined[:, : 2 * MEL].reshape(rows, frames, 2 * MEL)
    grad_embed = grad_joined[:, 2 * MEL :].astype(BF16)
    grad_text = rows_sum(grad_embed, text_hot).astype(BF16)
    in_sum, text_sum = scatter_sum(
        [
            grad_input.reshape(nb, n, part, -1),
            grad_text.reshape(nb, n, -1, VOCAB),
        ],
        13,
    )
    grad_input_own = jnp.sum(in_sum.astype(F32), axis=0).T
    grad_text_own = jnp.sum(text_sum.astype(F32), axis=0).T
    grad_down_own = jnp.concatenate([late_sum[3 * part : 4 * part], late_sum[4 * part :]], axis=1)

    return (
        block_out,
        grad_mels,
        grad_input_own,
        grad_first,
        grad_second,
        grad_time,
        grad_adaln,
        grad_qkv_own,
        late_sum[:part].T,
        late_sum[part : 3 * part].T,
        grad_down_own.T,
        grad_text_own,
    )


def solution(mesh):
    frames = P("batch", "seq", None)
    columns = P(None, ("batch", "seq"))
    taps = P(None, ("batch", "seq"), None)
    in_specs = (
        frames,
        P("batch", "seq"),
        P("batch", None),
        P("batch", None),
        P("batch", None),
        columns,
        taps,
        taps,
        columns,
        columns,
        columns,
        columns,
        columns,
        columns,
        columns,
        frames,
    )
    out_specs = (
        frames,
        frames,
        columns,
        taps,
        taps,
        columns,
        columns,
        columns,
        columns,
        columns,
        columns,
        columns,
    )
    return jax.shard_map(
        on_device, mesh=mesh, in_specs=in_specs, out_specs=out_specs, check_vma=False
    )
```

time: 3460 us -> 941 us (0.27)
  waiting for transfers between devices: 1910 us -> 0.06 us
  Pallas kernels: 0 us -> 718 us
  matrix products: 628 us -> 56.4 us
  local copies, waits for them, and re-layouts: 624 us -> 85.7 us
  other arithmetic: 190 us -> 56.9 us
  blocking collectives: 44.2 us -> 0 us
    reduce_scatter x9 -> x1, waiting for transfers between devices: 1440 us -> 0.01 us  [on_device(): lax.psum_scatter(late_grads, ('batch', 'seq'), scatter_dimension=0, tiled...]
    pallas_call x0 -> x19, Pallas kernels: none -> 718 us  [the longest x1 155 us: column_grads(): pl.pallas_call(functools.partial(columns_kernel, nb, n, len(arrays), kind...]
    dot_general x263 -> x22, matrix products: 622 us -> 53.2 us  [the longest x7 18.4 us: times(): lax.dot_general(left, right, (((1,), (0,)), ((), ())), preferred_element_...]
    all_gather x11 -> x1, waiting for transfers between devices: 243 us -> 0.02 us  [on_device(): lax.all_gather(wide_t, ('batch', 'seq'), axis=0, tiled=True)]
    mul x120 -> x1, local copies, waits for them, and re-layouts: 222 us -> 3.04 us  [on_device(): grad_att_c.astype(F32) * attended]
    unnamed x25 -> x2, waiting for transfers between devices: 172 us -> 0.03 us
    dynamic_update_slice x24 -> x0, local copies, waits for them, and re-layouts: 87.3 us -> none  [the longest x16 69.1 us: block_step(): lax.dynamic_update_slice_in_dim(grad_values, value_old + value_term.resha...]
    dynamic_slice x65 -> x0, local copies, waits for them, and re-layouts: 83.7 us -> none  [the longest x16 35.6 us: block_step(): value_old = lax.dynamic_slice_in_dim(grad_values, offset, piece_len, 1)]
  transfers between devices with their start and end apart: 31 -> 2, of which waited for: 21 -> 0; matrix products, arithmetic and copies ran while one was open for 20% -> 15% of each run, Pallas kernels for 0% -> 77%
where the time goes in v1:
time: 941 us; the launch traced here: 934 us
  Pallas kernels  718 us (76%)
  local copies, waits for them, and re-layouts  85.7 us (9%)
  other arithmetic  56.9 us (6%)
  matrix products  56.4 us (6%)
  between operations  16.2 us (2%)
    pallas_call x1, Pallas kernels, column_grads(): pl.pallas_call(functools.partial(columns_kernel, nb, n, len(arrays), kind...  155 us
    pallas_call x1, Pallas kernels, start_gather(): pl.pallas_call(functools.partial(start_kernel, nb, n, wide), out_shape=[j...  120 us
    pallas_call x6, Pallas kernels, swap_call(): pl.pallas_call(functools.partial(swap_kernel, count, n, parts), out_shape...  84.4 us
    pallas_call x1, Pallas kernels, group_sum(): pl.pallas_call(functools.partial(group_sum_kernel, n), out_shape=jax.Shap...  70.4 us
    pallas_call x1, Pallas kernels, conv_backward(): pl.pallas_call(functools.partial(conv_backward_kernel, count, length, wid...  52.5 us
    pallas_call x3, Pallas kernels, spray(): pl.pallas_call(functools.partial(spray_kernel, nb, n, by_batch), out_shap...  50.8 us
    pallas_call x1, Pallas kernels, attention_backward(): pl.pallas_call(functools.partial(attention_backward_kernel, length, width...  43 us
    pallas_call x1, Pallas kernels, group_gather(): pl.pallas_call(functools.partial(group_gather_kernel, n), out_shape=jax.S...  41.5 us
  transfers between devices with their start and end apart: 2, of which 0 were waited for; matrix products, arithmetic and copies ran while one was open for 15% of the time, Pallas kernels for 77%

profile of v1, /device:TPU:1, one launch (start us, length us, event | category | flops | bytes accessed | tf_op | source)
XLA Modules:
  0.0 933.7 jit_solution(7853489872372256097)
XLA Ops:
  22.8 120.4 %shard_map.292 = (bf16[4,8,32,712]{3,2,1,0:T(8,128)(2,1)}, bf16[4,8,16,2546]{3,2,1,0:T(8,128)(2,1)}, bf16[4,8,32,32]{3,2,1,0:T(8,128)(2,1)}, s32[4,8,2,4]{3,2,1,...) custom-call(bf16[32,712]{1,0:T(8,128)(2,1)} %bitcast.392, ...), custom_call_target="tpu_custom_call" | custom-call | tf_op jit(solution)/shard_map/pallas_call | solution.py:460
  146.5 23.0 %shard_map.296 = f32[32,8,192]{2,1,0:T(8,128)} custom-call(f32[4,8,192]{2,1,0:T(8,128)} %convolution_bitcast_fusion.1.x), custom_call_target="tpu_custom_call" | custom-call | tf_op jit(solution)/shard_map/pallas_call | solution.py:509
  191.6 3.1 fusion.14
  196.4 13.2 %shard_map.293.u = bf16[2,1536,128]{2,1,0:T(8,128)(2,1)} custom-call(bf16[2,192,1024]{2,1,0:T(8,128)(2,1)} %get-tuple-element.187.refs_0_), custom_call_target="tpu_custom_call" | custom-call | tf_op jit(solution)/shard_map/pallas_call | solution.py:106
  211.2 28.1 %shard_map.294 = (f32[2,400,512]{2,1,0:T(8,128)}, f32[2,400,512]{2,1,0:T(8,128)}, bf16[2,1536,128]{2,1,0:T(8,128)(2,1)}) custom-call(bf16[2,1536,128]{2,1,0:T(8,128)(2,1)} %shard_map.293.u, s32[2,1536,1]{2,1,0:T(8,128)} %copy.85.seg, bf16[3968,128]{1,0:T(8,128)(2,1)} %get-tuple-element.165.k1, bf16[3968,128]{1,0:T(8,128)(2,1)} %get-tuple-element.164.k2), custom_call_target="tpu_custom_call" | custom-call | tf_op jit(solution)/shard_map/pallas_call | solution.py:818
  239.3 12.3 %shard_map.295 = bf16[2,192,1024]{2,1,0:T(8,128)(2,1)} custom-call(bf16[2,1536,128]{2,1,0:T(8,128)(2,1)} %get-tuple-element.40.refs_0_), custom_call_target="tpu_custom_call" | custom-call | tf_op jit(solution)/shard_map/pallas_call | solution.py:106
  256.6 41.5 %shard_map.297 = bf16[2,8,192,1024]{3,2,1,0:T(8,128)(2,1)} custom-call(bf16[2,192,1024]{2,1,0:T(8,128)(2,1)} %get-tuple-element.182.x), custom_call_target="tpu_custom_call" | custom-call | tf_op jit(solution)/shard_map/pallas_call | solution.py:197
  298.3 4.4 multiply_subtract_fusion
  302.7 9.5 %shard_map.298 = (bf16[2,1536,128]{2,1,0:T(8,128)(2,1)}, bf16[2,1536,128]{2,1,0:T(8,128)(2,1)}, bf16[2,1536,128]{2,1,0:T(8,128)(2,1)}) custom-call(bf16[2,1536,1024]{2,1,0:T(8,128)(2,1)} %bitcast.290, bf16[384,1024]{1,0:T(8,128)(2,1)} %bitcast.332, f32[2,1536,128]{2,1,0:T(8,128)} %get-tuple-element.118.cos, f32[2,1536,128]{2,1,0:T(8,128)} %get-tuple-element.117.sin), custom_call_target="tpu_custom_call" | custom-call | tf_op jit(solution)/shard_map/pallas_call | solution.py:959
  312.2 22.9 %shard_map.299 = (f32[2,1536,128]{2,1,0:T(8,128)}, bf16[2,1536,128]{2,1,0:T(8,128)(2,1)}, f32[2,1536,128]{2,1,0:T(8,128)}) custom-call(bf16[2,1536,128]{2,1,0:T(8,128)(2,1)} %get-tuple-element.44.q, bf16[2,1536,128]{2,1,0:T(8,128)(2,1)} %get-tuple-element.45.k, bf16[2,1536,128]{2,1,0:T(8,128)(2,1)} %get-tuple-element.46.v, f32[2,1536,1]{2,1,0:T(8,128)} %copy.88.q_code, ...), custom_call_target="tpu_custom_call" | custom-call | tf_op jit(solution)/shard_map/pallas_call | solution.py:1003
  335.1 12.3 %shard_map.300 = bf16[2,192,1024]{2,1,0:T(8,128)(2,1)} custom-call(bf16[2,1536,128]{2,1,0:T(8,128)(2,1)} %get-tuple-element.47.refs_0_), custom_call_target="tpu_custom_call" | custom-call | tf_op jit(solution)/shard_map/pallas_call | solution.py:106
  347.4 2.9 slice.302
  350.4 4.2 fusion.57
  363.1 4.2 fusion.7
  374.5 4.7 fusion.53
  384.1 13.3 %pad_maximum_fusion = bf16[32,160,1024]{2,1,0:T(8,128)(2,1)} fusion(bf16[32,32,1024]{2,1,0:T(8,128)(2,1)S(1)} %bitcast.304, bf16[32,32,1024]{2,1,0:T(8,128)(2,1)S(1)} %bitcast.303, bf16[32,64,1024]{2,1,0:T(8,128)(2,1)S(1)} %bitcast.307, bf16[32,32,1024]{2,1,0:T(8,128)(2,1)S(1)} %bitcast.323), kind=kLoop, calls=%fused_computation | loop fusion | flops 41943040 | bytes 20971520 | tf_op jit(solution)/shard_map/concatenate | solution.py:1297
  414.0 3.1 copy.90
  420.1 3.7 convolution_convert_fusion.6
  423.9 20.2 %shard_map.301.g = bf16[2,1536,128]{2,1,0:T(8,128)(2,1)} custom-call(bf16[2,192,1024]{2,1,0:T(8,128)(2,1)} %bitcast.339), custom_call_target="tpu_custom_call" | custom-call | tf_op jit(solution)/shard_map/pallas_call | solution.py:106
  446.5 3.0 copy.92
  451.7 43.0 %shard_map.302 = bf16[2,1536,384]{2,1,0:T(8,128)(2,1)} custom-call(s32[2,6]{1,0:T(2,128)} %and_select_fusion.1.low_edge, s32[2,6]{1,0:T(2,128)} %and_select_fusion.high_edge, bf16[2,1536,128]{2,1,0:T(8,128)(2,1)} %get-tuple-element.44.q, bf16[2,1536,128]{2,1,0:T(8,128)(2,1)} %get-tuple-element.45.k, bf16[2,1536,128]{2,1,0:T(8,128)(2,1)} %get-tuple-element.46.v, ...), custom_call_target="tpu_custom_call" | custom-call | tf_op jit(solution)/shard_map/pallas_call | solution.py:1099
  494.7 7.1 convolution_convert_fusion
  501.8 70.4 %shard_map.303 = f32[2,192,1024]{2,1,0:T(8,128)} custom-call(bf16[2,8,192,1024]{3,2,1,0:T(8,128)(2,1)} %bitcast.306), custom_call_target="tpu_custom_call" | custom-call | tf_op jit(solution)/shard_map/pallas_call | solution.py:281
  581.7 3.2 fusion.44
  585.9 12.0 %shard_map.309 = f32[32,8,192]{2,1,0:T(8,128)} custom-call(f32[32,8,192]{2,1,0:T(8,128)} %bitcast.329), custom_call_target="tpu_custom_call" | custom-call | tf_op jit(solution)/shard_map/pallas_call | solution.py:509
  600.2 15.9 %shard_map.310 = f32[32,32,32]{2,1,0:T(8,128)} custom-call(f32[32,32,32]{2,1,0:T(8,128)} %convolution_bitcast_fusion.x), custom_call_target="tpu_custom_call" | custom-call | tf_op jit(solution)/shard_map/pallas_call | solution.py:509
  616.1 14.1 %shard_map.304.d = bf16[2,1536,128]{2,1,0:T(8,128)(2,1)} custom-call(bf16[2,192,1024]{2,1,0:T(8,128)(2,1)} %get-tuple-element.122.refs_0_), custom_call_target="tpu_custom_call" | custom-call | tf_op jit(solution)/shard_map/pallas_call | solution.py:106
  630.2 52.5 %shard_map.305 = (bf16[2,1536,128]{2,1,0:T(8,128)(2,1)}, f32[31,128,128]{2,1,0:T(8,128)}, f32[31,128,128]{2,1,0:T(8,128)}) custom-call(bf16[2,1536,128]{2,1,0:T(8,128)(2,1)} %shard_map.304.d, bf16[2,1536,128]{2,1,0:T(8,128)(2,1)} %shard_map.293.u, s32[2,1536,1]{2,1,0:T(8,128)} %copy.85.seg, f32[2,400,512]{2,1,0:T(8,128)} %get-tuple-element.50.c1, ...), custom_call_target="tpu_custom_call" | custom-call | tf_op jit(solution)/shard_map/pallas_call | solution.py:902
  682.8 12.3 %shard_map.306 = bf16[2,192,1024]{2,1,0:T(8,128)(2,1)} custom-call(bf16[2,1536,128]{2,1,0:T(8,128)(2,1)} %get-tuple-element.52.refs_0_), custom_call_target="tpu_custom_call" | custom-call | tf_op jit(solution)/shard_map/pallas_call | solution.py:106
  714.6 40.1 %shard_map.307 = (bf16[4,32,712]{2,1,0:T(8,128)(2,1)}, bf16[4,16,2546]{2,1,0:T(8,128)(2,1)}) custom-call(bf16[4,8,32,712]{3,2,1,0:T(8,128)(2,1)} %bitcast.305, bf16[4,8,16,2546]{3,2,1,0:T(8,128)(2,1)} %bitcast.296), custom_call_target="tpu_custom_call" | custom-call | tf_op jit(solution)/shard_map/pallas_call | solution.py:695
  754.6 6.3 convolution_convert_fusion.5
  760.9 154.8 %shard_map.308 = (bf16[4,1,31,32,64]{4,3,2,1,0:T(8,128)(2,1)}, bf16[4,1,31,32,64]{4,3,2,1,0:T(8,128)(2,1)}, bf16[4,3,32,1024]{3,2,1,0:T(8,128)(2,1)}) custom-call(bf16[1,4,31,32,64]{4,3,2,1,0:T(8,128)(2,1)} %bitcast.318, bf16[1,4,31,32,64]{4,3,2,1,0:T(8,128)(2,1)} %bitcast.319, bf16[3,4,32,1024]{3,2,1,0:T(8,128)(2,1)} %bitcast.322), custom_call_target="tpu_custom_call" | custom-call | tf_op jit(solution)/shard_map/pallas_call | solution.py:582
  (381 shorter events, 135.8 us)
Async XLA Ops:
  7.2 13.3 %copy-start.35 = (s32[2,1536]{1,0:T(2,128)S(1)}, s32[2,1536]{1,0:T(2,128)}, u32[]{:S(2)}) copy-start(s32[2,1536]{1,0:T(2,128)} %param.23) | copy-start | bytes 36868
  7.2 340.2 %all-gather.2.cloned.1.call-start = ((), (), s32[]{:S(2)}) async-start(), calls=%async_computation.1 | async-start | bytes 10813440 | tf_op jit(solution)/shard_map/all_gather | solution.py:1203
  9.8 913.5 %reduce-scatter.2.cloned.1.call-start = ((), (), s32[]{:S(2)}) async-start(), calls=%async_computation.2 | async-start | bytes 10813440 | tf_op jit(solution)/shard_map/reduce_scatter | solution.py:1306
  10.6 180.9 %copy-start.106 = (s32[384]{0:T(512)}, s32[384]{0:T(512)S(1)}, u32[]{:S(2)}) copy-start(s32[384]{0:T(512)S(1)} %eq.52) | copy-start | bytes 4612
  144.6 40.9 %copy-start.8 = (bf16[31,4,32,64]{3,2,1,0:T(8,128)(2,1)}, bf16[31,4,32,64]{3,2,1,0:T(8,128)(2,1)S(1)}, u32[]{:S(2)}) copy-start(bf16[31,4,32,64]{3,2,1,0:T(8,128)(2,1)S(1)} %copy.78) | copy-start | bytes 1523716
  145.4 24.1 %copy-start.108 = (s32[32]{0:T(128)}, s32[32]{0:T(128)S(1)}, u32[]{:S(2)}) copy-start(s32[32]{0:T(128)S(1)} %eq.57) | copy-start | bytes 388
  145.6 23.9 %copy-start.37 = (bf16[32,1024]{1,0:T(8,128)(2,1)}, bf16[32,1024]{1,0:T(8,128)(2,1)S(1)}, u32[]{:S(2)}) copy-start(bf16[32,1024]{1,0:T(8,128)(2,1)S(1)} %multiply_convert_fusion.2) | copy-start | bytes 196612
  196.4 13.3 %copy-start.15 = (bf16[3968,128]{1,0:T(8,128)(2,1)S(1)}, bf16[3968,128]{1,0:T(8,128)(2,1)}, u32[]{:S(2)}) copy-start(bf16[3968,128]{1,0:T(8,128)(2,1)} %copy.81) | copy-start | bytes 3047428
  196.4 13.3 %copy-start.51 = (bf16[128,128]{1,0:T(8,128)(2,1)S(1)}, bf16[128,128]{1,0:T(8,128)(2,1)}, u32[]{:S(2)}) copy-start(bf16[128,128]{1,0:T(8,128)(2,1)} %copy.140) | copy-start | bytes 98308
  256.5 41.5 %copy-start.102 = (f32[2,4]{0,1:T(4,128)S(1)}, f32[2,4]{0,1:T(4,128)}, u32[]{:S(2)}) copy-start(f32[2,4]{0,1:T(4,128)} %copy.87) | copy-start | bytes 100
  256.5 41.5 %copy-start.110 = (f32[128]{0:T(128)S(1)}, f32[128]{0:T(128)}, u32[]{:S(2)}) copy-start(f32[128]{0:T(128)} %constant.90.clone) | copy-start | bytes 1540
  256.5 41.7 %copy-start.31 = (f32[1536,128]{1,0:T(8,128)S(1)}, f32[1536,128]{1,0:T(8,128)}, u32[]{:S(2)}) copy-start(f32[1536,128]{1,0:T(8,128)} %constant.89.clone) | copy-start | bytes 2359300
  256.5 41.7 %copy-start.32 = (f32[1536,128]{1,0:T(8,128)S(1)}, f32[1536,128]{1,0:T(8,128)}, u32[]{:S(2)}) copy-start(f32[1536,128]{1,0:T(8,128)} %constant.88.clone) | copy-start | bytes 2359300
  357.1 22.0 %copy-start.62 = (f32[2,192]{1,0:T(2,128)}, f32[2,192]{1,0:T(2,128)S(1)}, u32[]{:S(2)}) copy-start(f32[2,192]{1,0:T(2,128)S(1)} %broadcast_multiply_fusion) | copy-start | bytes 4612
  357.4 21.7 %copy-start.77 = (f32[2,192]{1,0:T(2,128)}, f32[2,192]{1,0:T(2,128)S(1)}, u32[]{:S(2)}) copy-start(f32[2,192]{1,0:T(2,128)S(1)} %fusion.47) | copy-start | bytes 4612
  371.9 7.2 copy-start.2
  374.5 4.7 copy-start.12
  399.7 4.7 copy-start.74
  399.7 5.3 copy-start.73
  414.0 4.7 copy-start.103
  414.0 4.7 copy-start.104
  414.0 4.7 copy-start.105
  414.0 5.9 copy-start.101
  414.0 5.9 copy-start.109
  423.9 20.2 %copy-start.24 = (f32[2,1536,128]{2,1,0:T(8,128)S(1)}, f32[2,1536,128]{2,1,0:T(8,128)}, u32[]{:S(2)}) copy-start(f32[2,1536,128]{2,1,0:T(8,128)} %get-tuple-element.49) | copy-start | bytes 4718596
  451.7 43.0 %copy-start.28 = (bf16[3,4,32,1024]{3,2,1,0:T(8,128)(2,1)S(1)}, bf16[3,4,32,1024]{3,2,1,0:T(8,128)(2,1)}, u32[]{:S(2)}) copy-start(bf16[3,4,32,1024]{3,2,1,0:T(8,128)(2,1)} %get-tuple-element.43) | copy-start | bytes 2359300
  584.9 14.0 %copy-start.17 = (bf16[1024,192]{1,0:T(8,128)(2,1)S(1)}, bf16[1024,192]{1,0:T(8,128)(2,1)}, u32[]{:S(2)}) copy-start(bf16[1024,192]{1,0:T(8,128)(2,1)} %copy.104) | copy-start | bytes 1179652
  630.2 64.9 %copy-start.7 = (f32[2,192,1024]{2,1,0:T(8,128)S(1)}, f32[2,192,1024]{2,1,0:T(8,128)}, u32[]{:S(2)}) copy-start(f32[2,192,1024]{2,1,0:T(8,128)} %copy-done.6) | copy-start | bytes 4718596
  682.8 12.3 %copy-start.5 = (f32[2,192,1024]{2,1,0:T(8,128)S(1)}, f32[2,192,1024]{2,1,0:T(8,128)}, u32[]{:S(2)}) copy-start(f32[2,192,1024]{2,1,0:T(8,128)} %get-tuple-element.101) | copy-start | bytes 4718596
  714.5 40.1 %copy-start.1 = (bf16[2,1536,384]{2,1,0:T(8,128)(2,1)S(1)}, bf16[2,1536,384]{2,1,0:T(8,128)(2,1)}, u32[]{:S(2)}) copy-start(bf16[2,1536,384]{2,1,0:T(8,128)(2,1)} %shard_map.302) | copy-start | bytes 7077892
  760.9 154.9 %copy-start.41 = (bf16[4,32,712]{2,1,0:T(8,128)(2,1)S(1)}, bf16[4,32,712]{2,1,0:T(8,128)(2,1)}, u32[]{:S(2)}) copy-start(bf16[4,32,712]{2,1,0:T(8,128)(2,1)} %get-tuple-element.53) | copy-start | bytes 546820
  760.9 155.5 %copy-start.36 = (bf16[4,16,2546]{2,1,0:T(8,128)(2,1)S(1)}, bf16[4,16,2546]{2,1,0:T(8,128)(2,1)}, u32[]{:S(2)}) copy-start(bf16[4,16,2546]{2,1,0:T(8,128)(2,1)} %get-tuple-element.59) | copy-start | bytes 977668
  (82 other events, 176.5 us)
Sparse Core Ops, SparseCore 0:
  11.4 141.9 all-gather.1
  397.6 165.6 reduce-scatter.1

commit v2 on v1

v2 whole, which is shorter than its diff:
```python
import functools

import jax
import jax.numpy as jnp
import numpy as np
from jax import lax
from jax.experimental import pallas as pl
from jax.experimental.pallas import tpu as pltpu
from jax.sharding import PartitionSpec as P

D = 1024
HEADS = 16
HEAD = 64
MEL = 100
VOCAB = 2546
KERNEL = 31
HALF = KERNEL // 2
CHAN = 64
STEPS = 32
SEGS = 4
GAP = 16
FOLD = 4
TAPS = KERNEL + FOLD - 1

EPSILON = 1e-06
MASKED = -1e30
EXACT = lax.Precision.HIGHEST
MESH = pl.DeviceIdType.MESH
ANY = pl.BlockSpec(memory_space=pl.ANY)
VMEM_LIMIT = 56 * 1024 * 1024
F32 = jnp.float32
BF16 = jnp.bfloat16


def dims():
    return lax.axis_size("batch"), lax.axis_size("seq")


def params(cid=None):
    if cid is None:
        return pltpu.CompilerParams(vmem_limit_bytes=VMEM_LIMIT)
    return pltpu.CompilerParams(
        collective_id=cid, has_side_effects=True, vmem_limit_bytes=VMEM_LIMIT
    )


def greet_all(nb, n, b, s):
    sem = pltpu.get_barrier_semaphore()
    me = b * n + s
    for d in range(1, nb * n):
        other = lax.rem(me + d, nb * n)
        pl.semaphore_signal(
            sem,
            inc=1,
            device_id={"batch": other // n, "seq": lax.rem(other, n)},
            device_id_type=MESH,
        )
    pl.semaphore_wait(sem, nb * n - 1)


def greet_group(n, s):
    sem = pltpu.get_barrier_semaphore()
    for d in range(1, n):
        pl.semaphore_signal(
            sem, inc=1, device_id={"seq": lax.rem(s + d, n)}, device_id_type=MESH
        )
    pl.semaphore_wait(sem, n - 1)


def block_of(b, s, n):
    chips, core = n // 2, lax.rem(s, 2)
    return 2 * lax.rem(s // 2 + b + (chips // 2) * core, chips) + core


def holder_of(b, m, n, nb):
    chips, core = n // 2, lax.rem(m, 2)
    turned = m // 2 + (nb + chips) * chips - b - (chips // 2) * core
    return 2 * lax.rem(turned, chips) + core


def remote(src, dst, send, recv, **where):
    return pltpu.make_async_remote_copy(
        src_ref=src,
        dst_ref=dst,
        send_sem=send,
        recv_sem=recv,
        device_id=where,
        device_id_type=MESH,
    )


class Task:
    def __init__(self, operands, outs, scratch, body, everyone=False):
        self.operands, self.outs, self.scratch = list(operands), list(outs), list(scratch)
        self.body, self.everyone = body, everyone


def transfer_kernel(bodies, sizes, everyone, nb, n, *refs):
    b, s = lax.axis_index("batch"), lax.axis_index("seq")
    counts = [sum(size[i] for size in sizes) for i in range(3)]
    pools = [
        list(refs[: counts[0]]),
        list(refs[counts[0] : counts[0] + counts[1]]),
        list(refs[counts[0] + counts[1] :]),
    ]
    running = []
    for body, size in zip(bodies, sizes):
        taken = []
        for i in range(3):
            taken.append(pools[i][: size[i]])
            pools[i] = pools[i][size[i] :]
        running.append(body(*taken, b, s, nb, n))
    if everyone:
        greet_all(nb, n, b, s)
    else:
        greet_group(n, s)
    while running:
        left = []
        for task in running:
            try:
                next(task)
                left.append(task)
            except StopIteration:
                pass
        running = left


def transfer(tasks, cid):
    nb, n = dims()
    operands = [x for task in tasks for x in task.operands]
    outs = [x for task in tasks for x in task.outs]
    sizes = [(len(t.operands), len(t.outs), len(t.scratch)) for t in tasks]
    got = pl.pallas_call(
        functools.partial(
            transfer_kernel,
            [t.body for t in tasks],
            sizes,
            any(t.everyone for t in tasks),
            nb,
            n,
        ),
        out_shape=outs,
        in_specs=[ANY] * len(operands),
        out_specs=[ANY] * len(outs),
        scratch_shapes=[x for task in tasks for x in task.scratch],
        compiler_params=params(cid),
    )(*operands)
    got = list(got)
    result = []
    for size in sizes:
        result.append(got[: size[1]])
        got = got[size[1] :]
    return result


DMA = pltpu.SemaphoreType.DMA


def like(x, shape, dtype=None):
    return jax.ShapeDtypeStruct(tuple(shape), dtype or x.dtype)


def swap_task(x, shape, parts):
    n = dims()[1]

    def body(ins, outs, scratch, b, s, nb, n):
        send, recv, local = scratch
        src, dst = parts(ins[0], outs[0], b, s)
        copies = []
        for d in range(1, n):
            t = lax.rem(s + d, n)
            copy = remote(src(t), dst, send.at[d], recv.at[d], seq=t)
            copy.start()
            copies.append(copy)
        own = pltpu.make_async_copy(src(s), dst, local)
        own.start()
        copies.append(own)
        yield
        yield
        for copy in copies:
            copy.wait()

    return Task([x], [like(x, shape)], [DMA((n,)), DMA((n,)), DMA], body)


def to_channels(x):
    n = dims()[1]
    rows, frames = x.shape[:2]
    width = x.shape[2] // n
    if width % 128 == 0:

        def parts(x, o, b, s):
            first = pl.multiple_of(s * frames, 16)
            return (
                lambda t: x.at[
                    :, :, pl.ds(pl.multiple_of(block_of(b, t, n) * width, 128), width)
                ]
            ), o.at[:, pl.ds(first, frames), :]

        return swap_task(x, (rows, n * frames, width), parts), lambda got: got[0]

    def split_parts(x, o, b, s):
        return (lambda t: x.at[block_of(b, t, n)]), o.at[s]

    split = x.reshape(rows, frames, n, width).transpose(2, 0, 1, 3)
    return (
        swap_task(split, split.shape, split_parts),
        lambda got: got[0].transpose(1, 0, 2, 3).reshape(rows, n * frames, width),
    )


def to_frames(x):
    n = dims()[1]
    rows, length, width = x.shape
    frames = length // n
    if width % 128 == 0:

        def parts(x, o, b, s):
            first = pl.multiple_of(block_of(b, s, n) * width, 128)
            return (
                lambda t: x.at[:, pl.ds(pl.multiple_of(t * frames, 16), frames), :]
            ), o.at[:, :, pl.ds(first, width)]

        return swap_task(x, (rows, frames, n * width), parts), lambda got: got[0]

    def split_parts(x, o, b, s):
        return (lambda t: x.at[t]), o.at[block_of(b, s, n)]

    split = x.reshape(rows, n, frames, width).transpose(1, 0, 2, 3)
    return (
        swap_task(split, split.shape, split_parts),
        lambda got: got[0].transpose(1, 2, 0, 3).reshape(rows, frames, n * width),
    )


def spray_task(x, by_batch):
    nb, n = dims()
    ndev = nb * n

    def body(ins, outs, scratch, b, s, nb, n):
        send, recv, local = scratch
        x, o = ins[0], outs[0]
        me = b * n + s
        own = pltpu.make_async_copy(x.at[b if by_batch else me], o.at[me], local)
        own.start()
        copies = [own]
        for d in range(1, ndev):
            other = lax.rem(me + d, ndev)
            plane, where = other // n, lax.rem(other, n)
            copy = remote(
                x.at[plane if by_batch else other],
                o.at[me],
                send.at[d],
                recv.at[d],
                batch=plane,
                seq=where,
            )
            copy.start()
            copies.append(copy)
        yield
        yield
        for copy in copies:
            copy.wait()

    return Task(
        [x], [like(x, (ndev,) + x.shape[1:])], [DMA((ndev,)), DMA((ndev,)), DMA], body, True
    )


def gather_task(x):
    n = dims()[1]

    def body(ins, outs, scratch, b, s, nb, n):
        send, recv, local = scratch
        x, o = ins[0], outs[0]
        core = lax.rem(s, 2)
        sibling = s + 1 - 2 * core
        chips = n // 2
        far, near = [], []
        for d in range(1, chips):
            copy = remote(x, o.at[:, s], send.at[d], recv.at[d], seq=lax.rem(s + 2 * d, n))
            copy.start()
            far.append(copy)
        copy = remote(x, o.at[:, s], send.at[0], recv.at[0], seq=sibling)
        copy.start()
        near.append(copy)
        own = pltpu.make_async_copy(x, o.at[:, s], local)
        own.start()
        yield
        for d in range(1, chips):
            far[d - 1].wait_recv()
            source = lax.rem(s - 2 * d + n, n)
            copy = remote(
                o.at[:, source],
                o.at[:, source],
                send.at[chips + d],
                recv.at[chips + d],
                seq=sibling,
            )
            copy.start()
            near.append(copy)
        yield
        own.wait()
        for copy in far:
            copy.wait_send()
        for copy in near:
            copy.wait()

    out = like(x, (x.shape[0], n) + x.shape[1:])
    return Task([x], [out], [DMA((n,)), DMA((n,)), DMA], body)


def quad_gather_task(x):
    n = dims()[1]
    frames = x.shape[1]
    half = frames // 2

    def body(ins, outs, scratch, b, s, nb, n):
        send, recv, local = scratch
        x, o = ins[0], outs[0]
        core, chip = lax.rem(s, 2), s // 2
        sibling = s + 1 - 2 * core
        flip_x = chip + 1 - 2 * lax.rem(chip, 2)
        flip_y = lax.rem(chip + 2, 4)
        diagonal = lax.rem(flip_x + 2, 4)
        seat = lambda c: 2 * c + core
        parts = (pl.ds(0, half), pl.ds(half, half))
        k = iter(range(16))

        def push(piece, source, target):
            i = next(k)
            where = o.at[:, source, parts[piece]]
            copy = remote(
                x.at[:, parts[piece]] if source is s else where,
                where,
                send.at[i],
                recv.at[i],
                seq=target,
            )
            copy.start()
            return copy

        to_x = [push(p, s, seat(flip_x)) for p in (0, 1)]
        to_y = [push(p, s, seat(flip_y)) for p in (1, 0)]
        near = [push(p, s, sibling) for p in (0, 1)]
        own = pltpu.make_async_copy(x, o.at[:, s], local)
        own.start()
        yield
        far = []
        to_x[0].wait_recv()
        far.append(push(0, seat(flip_x), seat(flip_y)))
        near.append(push(0, seat(flip_x), sibling))
        to_y[0].wait_recv()
        far.append(push(1, seat(flip_y), seat(flip_x)))
        near.append(push(1, seat(flip_y), sibling))
        to_x[1].wait_recv()
        near.append(push(1, seat(flip_x), sibling))
        to_y[1].wait_recv()
        near.append(push(0, seat(flip_y), sibling))
        far[0].wait_recv()
        near.append(push(0, seat(diagonal), sibling))
        far[1].wait_recv()
        near.append(push(1, seat(diagonal), sibling))
        yield
        own.wait()
        for copy in to_x + to_y + far:
            copy.wait_send()
        for copy in near:
            copy.wait()

    out = like(x, (x.shape[0], n) + x.shape[1:])
    return Task([x], [out], [DMA((16,)), DMA((16,)), DMA], body)


def sum_task(x):
    n = dims()[1]
    rows, _, frames, width = x.shape
    chips = n // 2
    step = 16

    def body(ins, outs, scratch, b, s, nb, n):
        mine, first, passed, second, total, send, recv, local, out_sem = scratch
        x, o = ins[0], outs[0]
        core = lax.rem(s, 2)
        sibling = s + 1 - 2 * core
        chip = s // 2
        order = [lax.rem(chip + d, chips) for d in list(range(1, chips)) + [0]]
        pair, own, far = [], [], []
        for k, c in enumerate(order):
            copy = remote(
                x.at[:, 2 * c + 1 - core], first.at[k], send.at[k], recv.at[k], seq=sibling
            )
            copy.start()
            pair.append(copy)
            copy = pltpu.make_async_copy(x.at[:, 2 * c + core], mine.at[k], local.at[k])
            copy.start()
            own.append(copy)
        yield
        for k in range(chips):
            pair[k].wait_recv()
            own[k].wait()
            if k < chips - 1:

                def add(i, carry, k=k):
                    at = pl.ds(pl.multiple_of(i * step, step), step)
                    for r in range(rows):
                        passed[k, r, at, :] = (
                            mine[k, r, at, :].astype(F32) + first[k, r, at, :].astype(F32)
                        ).astype(BF16)
                    return carry

                lax.fori_loop(0, frames // step, add, 0)
                copy = remote(
                    passed.at[k],
                    second.at[k],
                    send.at[chips + k],
                    recv.at[chips + k],
                    seq=2 * order[k] + core,
                )
                copy.start()
                far.append(copy)
        yield
        for copy in far:
            copy.wait_recv()

        def finish(i, carry):
            at = pl.ds(pl.multiple_of(i * step, step), step)
            for r in range(rows):
                value = mine[chips - 1, r, at, :].astype(F32) + first[chips - 1, r, at, :].astype(F32)
                for k in range(chips - 1):
                    value = value + second[k, r, at, :].astype(F32)
                total[r, at, :] = value
            return carry

        lax.fori_loop(0, frames // step, finish, 0)
        out = pltpu.make_async_copy(total, o, out_sem)
        out.start()
        for copy in pair + far:
            copy.wait_send()
        out.wait()

    slots = pltpu.VMEM((chips, rows, frames, width), BF16)
    fewer = pltpu.VMEM((chips - 1, rows, frames, width), BF16)
    return Task(
        [x],
        [like(x, (rows, frames, width), F32)],
        [
            slots,
            slots,
            fewer,
            fewer,
            pltpu.VMEM((rows, frames, width), F32),
            DMA((n,)),
            DMA((n,)),
            DMA((chips,)),
            DMA,
        ],
        body,
    )


def spread_task(x):
    nb, n = dims()
    chips = n // 2

    def body(ins, outs, scratch, b, s, nb, n):
        z_send, z_recv, p_send, p_recv, c_send, c_recv, local = scratch
        x, o = ins[0], outs[0]
        core = lax.rem(s, 2)
        sibling = s + 1 - 2 * core
        own = pltpu.make_async_copy(x, o.at[b, s], local)
        own.start()
        along = []
        for d in range(1, nb):
            copy = remote(
                x, o.at[b, s], z_send.at[d], z_recv.at[d], batch=lax.rem(b + d, nb), seq=s
            )
            copy.start()
            along.append(copy)
        far, near = [], []

        def onward(d):
            plane = lax.rem(b - d + nb, nb)
            source = x if d == 0 else o.at[plane, s]
            for c in range(1, chips):
                copy = remote(
                    source,
                    o.at[plane, s],
                    p_send.at[d, c],
                    p_recv.at[d, c],
                    seq=lax.rem(s + 2 * c, n),
                )
                copy.start()
                far.append((d, c, plane, copy))
            copy = remote(source, o.at[plane, s], c_send.at[d, 0], c_recv.at[d, 0], seq=sibling)
            copy.start()
            near.append(copy)

        onward(0)
        yield
        for d in range(1, nb):
            along[d - 1].wait_recv()
            onward(d)
        yield
        for d, c, plane, copy in far:
            copy.wait_recv()
            source = lax.rem(s - 2 * c + n, n)
            last = remote(
                o.at[plane, source],
                o.at[plane, source],
                c_send.at[d, c],
                c_recv.at[d, c],
                seq=sibling,
            )
            last.start()
            near.append(last)
        yield
        own.wait()
        for copy in along:
            copy.wait_send()
        for entry in far:
            entry[3].wait_send()
        for copy in near:
            copy.wait()

    square = DMA((nb, chips))
    return Task(
        [x],
        [like(x, (nb, n) + x.shape)],
        [DMA((nb,)), DMA((nb,)), square, square, square, square, DMA],
        body,
        True,
    )


def columns_out_task(x):
    nb, n = dims()
    ndev = nb * n
    kinds = x.shape[0]

    def body(ins, outs, scratch, b, s, nb, n):
        send, recv = scratch
        x, o = ins[0], outs[0]
        me = b * n + s
        pieces = []
        for j in range(kinds):
            piece = kinds * me + j
            column = lax.rem(piece, ndev)
            pieces.append((j, piece // ndev, column // nb, lax.rem(column, nb)))
        sent = []
        for j, part, block, slot in pieces:
            source, target, arrived = x.at[j], o.at[part, slot], recv.at[part, slot]
            for d in range(nb):
                plane = lax.rem(b + d, nb)
                owner = holder_of(plane, block, n, nb)
                if d == 0:

                    @pl.when(owner == s)
                    def _(source=source, target=target, arrived=arrived):
                        pltpu.make_async_copy(source, target, arrived).start()

                    @pl.when(owner != s)
                    def _(source=source, target=target, arrived=arrived, j=j, owner=owner):
                        remote(
                            source, target, send.at[j, 0], arrived, batch=b, seq=owner
                        ).start()
                else:
                    copy = remote(
                        source, target, send.at[j, d], arrived, batch=plane, seq=owner
                    )
                    copy.start()
                    sent.append(copy)
        yield
        yield
        yield
        for copy in sent:
            copy.wait_send()
        for j, part, block, slot in pieces:
            owner = holder_of(b, block, n, nb)

            @pl.when(owner != s)
            def _(j=j, part=part, slot=slot, owner=owner):
                remote(
                    x.at[j], o.at[part, slot], send.at[j, 0], recv.at[part, slot], batch=b, seq=owner
                ).wait_send()

        for p in range(kinds):
            for j in range(nb):
                pltpu.make_async_copy(x.at[0], o.at[p, j], recv.at[p, j]).wait()

    return Task(
        [x],
        [like(x, (kinds, nb) + x.shape[1:])],
        [DMA((kinds, nb)), DMA((kinds, nb))],
        body,
        True,
    )


def columns_back_task(x):
    nb, n = dims()
    ndev = nb * n
    kinds = x.shape[0]

    def body(ins, outs, scratch, b, s, nb, n):
        send, recv = scratch
        x, o = ins[0], outs[0]
        me = b * n + s
        pieces = []
        for p in range(kinds):
            for j in range(nb):
                column = p * ndev + block_of(b, s, n) * nb + j
                part = lax.rem(column, kinds)
                pieces.append(
                    (x.at[p, j], o.at[b, part], column // kinds, send.at[p, j], recv.at[b, part])
                )
        for source, target, owner, sent, arrived in pieces:

            @pl.when(owner == me)
            def _(source=source, target=target, arrived=arrived):
                pltpu.make_async_copy(source, target, arrived).start()

            @pl.when(owner != me)
            def _(source=source, target=target, owner=owner, sent=sent, arrived=arrived):
                remote(
                    source, target, sent, arrived, batch=owner // n, seq=lax.rem(owner, n)
                ).start()

        yield
        yield
        yield
        for source, target, owner, sent, arrived in pieces:

            @pl.when(owner != me)
            def _(source=source, target=target, owner=owner, sent=sent, arrived=arrived):
                remote(
                    source, target, sent, arrived, batch=owner // n, seq=lax.rem(owner, n)
                ).wait_send()

        for p in range(kinds):
            for j in range(nb):
                pltpu.make_async_copy(x.at[0, 0], o.at[j, p], recv.at[j, p]).wait()

    return Task(
        [x],
        [like(x, (nb, kinds) + x.shape[2:])],
        [DMA((kinds, nb)), DMA((nb, kinds))],
        body,
        True,
    )


def scatter_task(x):
    nb, n = dims()
    chips = n // 2

    def body(ins, outs, scratch, b, s, nb, n):
        mine, first, passed, second, total, send, recv, local, z_send, z_recv, z_local = scratch
        x, o = ins[0], outs[0]
        core = lax.rem(s, 2)
        sibling = s + 1 - 2 * core
        chip = s // 2
        order = [lax.rem(chip + d, chips) for d in list(range(1, chips)) + [0]]
        pair, own, far, last = [], [], [], []
        for k, c in enumerate(order):
            copy = remote(
                x.at[:, 2 * c + 1 - core], first.at[k], send.at[k], recv.at[k], seq=sibling
            )
            copy.start()
            pair.append(copy)
            copy = pltpu.make_async_copy(x.at[:, 2 * c + core], mine.at[k], local.at[k])
            copy.start()
            own.append(copy)
        yield
        for k in range(chips - 1):
            pair[k].wait_recv()
            own[k].wait()

            def add(i, carry, k=k):
                passed[k, i] = (mine[k, i].astype(F32) + first[k, i].astype(F32)).astype(BF16)
                return carry

            lax.fori_loop(0, nb, add, 0)
            copy = remote(
                passed.at[k],
                second.at[k],
                send.at[chips + k],
                recv.at[chips + k],
                seq=2 * order[k] + core,
            )
            copy.start()
            far.append(copy)
        yield
        pair[chips - 1].wait_recv()
        own[chips - 1].wait()
        for copy in far:
            copy.wait_recv()

        def finish(i, carry):
            value = mine[chips - 1, i].astype(F32) + first[chips - 1, i].astype(F32)
            for k in range(chips - 1):
                value = value + second[k, i].astype(F32)
            total[i] = value.astype(BF16)
            return carry

        lax.fori_loop(0, nb, finish, 0)
        for d in range(1, nb):
            plane = lax.rem(b + d, nb)
            copy = remote(
                total.at[plane], o.at[b], z_send.at[d], z_recv.at[d], batch=plane, seq=s
            )
            copy.start()
            last.append(copy)
        copy = pltpu.make_async_copy(total.at[b], o.at[b], z_local)
        copy.start()
        last.append(copy)
        yield
        for copy in pair + far:
            copy.wait_send()
        for copy in last:
            copy.wait()

    block = (nb,) + x.shape[2:]
    return Task(
        [x],
        [like(x, block)],
        [
            pltpu.VMEM((chips,) + block, BF16),
            pltpu.VMEM((chips,) + block, BF16),
            pltpu.VMEM((chips - 1,) + block, BF16),
            pltpu.VMEM((chips - 1,) + block, BF16),
            pltpu.VMEM(block, BF16),
            DMA((n,)),
            DMA((n,)),
            DMA((chips,)),
            DMA((nb,)),
            DMA((nb,)),
            DMA,
        ],
        body,
        True,
    )


def times(left, right):
    return lax.dot_general(left, right, (((1,), (0,)), ((), ())), preferred_element_type=F32)


def times_t(left, right):
    return lax.dot_general(left, right, (((1,), (1,)), ((), ())), preferred_element_type=F32)


def rows_sum(left, right):
    return lax.dot_general(left, right, (((0,), (0,)), ((), ())), preferred_element_type=F32)


def mish_parts(v):
    e = jnp.exp(jnp.minimum(v, 20.0))
    n = e * (e + 2.0)
    inverse = 1.0 / (n + 2.0)
    return e, n, inverse


def mish(v):
    e, n, inverse = mish_parts(v)
    return v * (n * inverse)


def mish_slope(v):
    e, n, inverse = mish_parts(v)
    return n * inverse + v * (4.0 * e * (1.0 + e)) * inverse * inverse


CHUNK = 128


def interleave(even, odd):
    low = lax.broadcasted_iota(jnp.int32, even.shape, 1) < CHAN
    return (
        jnp.where(low, even, pltpu.roll(odd, CHAN, 1)),
        jnp.where(low, pltpu.roll(even, CHAN, 1), odd),
    )


def to_groups(even, odd):
    if even.shape[1] == CHAN:
        return (jnp.concatenate([even, odd], axis=1),)
    return interleave(even, odd)


def to_pair(blocks):
    if len(blocks) == 1:
        return blocks[0][:, :CHAN], blocks[0][:, CHAN:]
    return interleave(*blocks)


def place(buf, source, seg, length):
    rows = buf.shape[0]

    def clear(i, carry):
        buf[pl.ds(pl.multiple_of(i * 16, 16), 16), :] = jnp.zeros((16, buf.shape[1]), F32)
        return carry

    lax.fori_loop(0, rows // 16, clear, 0)

    def move(i, carry):
        at = pl.multiple_of(i * CHUNK, CHUNK)
        value = source(at)
        ids = seg[0, pl.ds(at, CHUNK), :] & 7
        for u in range(SEGS):
            to = pl.ds(at + GAP * (u + 1), CHUNK)
            buf[to, :] = buf[to, :] + jnp.where(ids == u, value, 0.0)
        return carry

    lax.fori_loop(0, length // CHUNK, move, 0)


def unplace(buf, sink, seg, length):
    def move(i, carry):
        at = pl.multiple_of(i * CHUNK, CHUNK)
        ids = seg[0, pl.ds(at, CHUNK), :] & 7
        value = buf[pl.ds(at + GAP, CHUNK), :]
        for u in range(1, SEGS):
            value = jnp.where(ids == u, buf[pl.ds(at + GAP * (u + 1), CHUNK), :], value)
        sink[0, pl.ds(at, CHUNK), :] = value.astype(sink.dtype)
        return carry

    lax.fori_loop(0, length // CHUNK, move, 0)


def folded(buf, count, first):
    return buf[pl.ds(first, count, stride=FOLD), :]


def spread_taps(x, buf, count):
    for t in range(TAPS // 2):
        blocks = to_groups(folded(buf, count, 2 * t + 1), folded(buf, count, 2 * t + 2))
        for g, block in enumerate(blocks):
            x[g, :, 2 * CHAN * t : 2 * CHAN * (t + 1)] = block.astype(BF16)


def write_folded(buf, count, groups, value, live=None):
    for w in range(FOLD // 2):
        lanes = slice(2 * CHAN * w, 2 * CHAN * (w + 1))
        for half, part in enumerate(to_pair([value(g, lanes) for g in range(groups)])):
            at = pl.ds(GAP + 2 * w + half, count, stride=FOLD)
            buf[at, :] = part if live is None else part * live[at, :]


def fill_bands(bands, taps, groups, back):
    low = lax.broadcasted_iota(jnp.int32, (CHAN, 2 * CHAN), 1) < CHAN
    zero = jnp.zeros((CHAN, 2 * CHAN), F32)
    width = groups * CHAN

    def forms(k):
        if not 0 <= k < KERNEL:
            return None
        full = taps[:, KERNEL - 1 - k if back else k].astype(F32).reshape(width, 2 * CHAN)
        if back:
            full = full.T
            if groups == 1:
                full = jnp.concatenate([full, full], axis=1)
        turned = pltpu.roll(full, CHAN, 1)
        result = {}
        for c in range(2):
            for g in range(groups):
                if back:
                    rows, own = slice(c * CHAN, (c + 1) * CHAN), g
                else:
                    rows, own = slice(g * CHAN, (g + 1) * CHAN), c
                pair = (full[rows], turned[rows])
                result[c, g] = pair if own == 0 else pair[::-1]
        return result

    known = {}
    for tap in range(TAPS):
        known[tap] = forms(tap)
        known.pop(tap - FOLD, None)
        for w in range(FOLD // 2):
            left, right = known.get(tap - 2 * w), known.get(tap - 2 * w - 1)
            for c in range(2):
                for g in range(groups):
                    a = zero if left is None else left[c, g][0]
                    b = zero if right is None else right[c, g][1]
                    bands[
                        c, g, tap * CHAN : (tap + 1) * CHAN, 2 * CHAN * w : 2 * CHAN * (w + 1)
                    ] = jnp.where(low, a, b).astype(BF16)


FOLDED = FOLD * CHAN
DEPTH = TAPS * CHAN


def conv_forward_kernel(count, length, groups, u, seg, taps, c1, c2, out, buf, live, x, bands):
    @pl.when(pl.program_id(0) == 0)
    def _():
        fill_bands(bands, taps, groups, False)

    width = groups * CHAN
    place(live, lambda at: jnp.ones((CHUNK, width), F32), seg, length)
    place(buf, lambda at: u[0, pl.ds(at, CHUNK), :].astype(F32), seg, length)
    spread_taps(x, buf, count)
    for g in range(groups):
        c1[0, g] = times(x[g], bands[0, g])
    write_folded(buf, count, groups, lambda g, lanes: mish(c1[0, g, :, lanes]), live)
    spread_taps(x, buf, count)
    for g in range(groups):
        c2[0, g] = times(x[g], bands[1, g])
    write_folded(buf, count, groups, lambda g, lanes: mish(c2[0, g, :, lanes]))
    unplace(buf, out, seg, length)


def conv_sizes(length):
    count = -(-(length + GAP * (SEGS - 1)) // FOLD)
    count = -(-count // 16) * 16
    return count, FOLD * count + 48


def whole(shape):
    zeros = (0,) * len(shape)
    return pl.BlockSpec(shape, lambda *i: zeros)


def by_row(shape):
    return pl.BlockSpec((1,) + tuple(shape[1:]), lambda r: (r,) + (0,) * (len(shape) - 1))


def conv_forward(u, seg, taps):
    rows, length, width = u.shape
    groups = width // CHAN
    count, buffer = conv_sizes(length)
    kept = (rows, groups, count, FOLDED)
    return pl.pallas_call(
        functools.partial(conv_forward_kernel, count, length, groups),
        grid=(rows,),
        in_specs=[by_row(u.shape), by_row(seg.shape), whole(taps.shape)],
        out_specs=[by_row(kept), by_row(kept), by_row(u.shape)],
        out_shape=[
            jax.ShapeDtypeStruct(kept, F32),
            jax.ShapeDtypeStruct(kept, F32),
            jax.ShapeDtypeStruct(u.shape, BF16),
        ],
        scratch_shapes=[
            pltpu.VMEM((buffer, width), F32),
            pltpu.VMEM((buffer, width), F32),
            pltpu.VMEM((groups, count, DEPTH), BF16),
            pltpu.VMEM((2, groups, DEPTH, FOLDED), BF16),
        ],
        compiler_params=params(),
    )(u, seg, taps)


def weight_sums(even, odd, c, turned, x, groups):
    rows = slice(c * CHAN, (c + 1) * CHAN)
    blocks = TAPS // 2
    pair = 2 * CHAN
    for g in range(groups):
        for start in range(0, blocks, 2):
            stop = min(start + 2, blocks)
            product = times(turned[g], x[g, :, start * pair : stop * pair])
            for t in range(start, stop):
                part = product[:, (t - start) * pair : (t - start + 1) * pair]
                for m in range(FOLD):
                    to = t - m // 2
                    if 0 <= to < 16:
                        sums = odd if m % 2 else even
                        sums[g, to, rows] = sums[g, to, rows] + part[m * CHAN : (m + 1) * CHAN]


def conv_backward_kernel(
    count, length, groups, nb, d, u, seg, c1, c2, taps, dh, pieces, buf, grads, live, x, turned, bands, even, odd
):
    width = groups * CHAN
    row = pl.program_id(0)

    @pl.when(row == 0)
    def _():
        fill_bands(bands, taps, groups, True)
        even[...] = jnp.zeros_like(even)
        odd[...] = jnp.zeros_like(odd)

    place(live, lambda at: jnp.ones((CHUNK, width), F32), seg, length)
    place(grads, lambda at: d[0, pl.ds(at, CHUNK), :].astype(F32), seg, length)

    def slope(kept, scaled):
        values = {}
        for w in range(FOLD // 2):
            lanes = slice(2 * CHAN * w, 2 * CHAN * (w + 1))
            for g in range(groups):
                value = scaled(g, w, lanes) * mish_slope(kept[0, g, :, lanes])
                values[g, w] = value
                turned[g, lanes, :] = value.T.astype(BF16)
        return values

    def loaded(g, w, lanes):
        return to_groups(
            folded(grads, count, GAP + 2 * w), folded(grads, count, GAP + 2 * w + 1)
        )[g]

    values = slope(c2, loaded)
    write_folded(grads, count, groups, lambda g, lanes: values[g, lanes.start // (2 * CHAN)])
    for i in range(0, GAP, 8):
        buf[i : i + 8, :] = jnp.zeros((8, width), F32)
    for i in range(GAP + FOLD * count, buf.shape[0], 8):
        buf[i : i + 8, :] = jnp.zeros((8, width), F32)
    write_folded(buf, count, groups, lambda g, lanes: mish(c1[0, g, :, lanes]), live)
    spread_taps(x, buf, count)
    weight_sums(even, odd, 1, turned, x, groups)
    spread_taps(x, grads, count)
    back = [times(x[g], bands[1, g]) for g in range(groups)]

    def masked(g, w, lanes):
        alive = to_groups(
            folded(live, count, GAP + 2 * w), folded(live, count, GAP + 2 * w + 1)
        )[g]
        return back[g][:, lanes] * alive

    values = slope(c1, masked)
    write_folded(grads, count, groups, lambda g, lanes: values[g, lanes.start // (2 * CHAN)])
    place(buf, lambda at: u[0, pl.ds(at, CHUNK), :].astype(F32), seg, length)
    spread_taps(x, buf, count)
    weight_sums(even, odd, 0, turned, x, groups)
    spread_taps(x, grads, count)
    last = [times(x[g], bands[0, g]) for g in range(groups)]
    write_folded(buf, count, groups, lambda g, lanes: last[g][:, lanes])
    unplace(buf, dh, seg, length)

    @pl.when(row == pl.num_programs(0) - 1)
    def _():
        low = lax.broadcasted_iota(jnp.int32, (2 * CHAN, 2 * CHAN), 1) < CHAN
        part = width // nb
        each = CHAN // part
        for g in range(groups):
            for p in range(16):
                left = pltpu.roll(odd[g, p], CHAN, 1)
                right = pltpu.roll(odd[g, p + 1], CHAN, 1) if p < 15 else left
                total = (even[g, p] + jnp.where(low, left, right)).T.astype(BF16)
                for half in range(2):
                    k = 2 * p + half
                    if k < KERNEL:
                        for j in range(each):
                            first = half * CHAN + j * part
                            pieces[0, g * each + j, k] = total[first : first + part]


def conv_backward(d, u, seg, c1, c2, taps, nb):
    rows, length, width = u.shape
    groups = width // CHAN
    count, buffer = conv_sizes(length)
    pieces = (1, nb, KERNEL, width // nb, 2 * CHAN)
    sums = pltpu.VMEM((groups, 16, 2 * CHAN, 2 * CHAN), F32)
    frames = pltpu.VMEM((buffer, width), F32)
    return pl.pallas_call(
        functools.partial(conv_backward_kernel, count, length, groups, nb),
        grid=(rows,),
        in_specs=[
            by_row(d.shape),
            by_row(u.shape),
            by_row(seg.shape),
            by_row(c1.shape),
            by_row(c2.shape),
            whole(taps.shape),
        ],
        out_specs=[by_row(u.shape), whole(pieces)],
        out_shape=[
            jax.ShapeDtypeStruct(u.shape, BF16),
            jax.ShapeDtypeStruct(pieces, BF16),
        ],
        scratch_shapes=[
            frames,
            frames,
            frames,
            pltpu.VMEM((groups, count, DEPTH), BF16),
            pltpu.VMEM((groups, FOLDED, count), BF16),
            pltpu.VMEM((2, groups, DEPTH, FOLDED), BF16),
            sums,
            sums,
        ],
        compiler_params=params(),
    )(d, u, seg, c1, c2, taps)


def pair_swap(x):
    width = x.shape[1]
    if width % 128:
        x = jnp.concatenate([x, x], axis=1)
    lane = lax.broadcasted_iota(jnp.int32, x.shape, 1)
    after = pltpu.roll(x, x.shape[1] - 1, 1)
    before = pltpu.roll(x, 1, 1)
    return jnp.where(lax.rem(lane, 2) == 0, -after, before)[:, :width]


def qkv_kernel(width, x, w, cos, sin, q, k, v):
    got = lax.dot_general(
        x[0], w[...], (((1,), (1,)), ((), ())), preferred_element_type=F32
    )
    for p, out in enumerate((q, k)):
        part = got[:, p * width : (p + 1) * width]
        out[0] = (part * cos[0] + pair_swap(part) * sin[0]).astype(BF16)
    v[0] = got[:, 2 * width :].astype(BF16)


def qkv_forward(x, w, cos, sin):
    rows, length, depth = x.shape
    width = w.shape[0] // 3
    block = 512
    spec = pl.BlockSpec((1, block, width), lambda r, i: (r, i, 0))
    shape = jax.ShapeDtypeStruct((rows, length, width), BF16)
    return pl.pallas_call(
        functools.partial(qkv_kernel, width),
        grid=(rows, length // block),
        in_specs=[
            pl.BlockSpec((1, block, depth), lambda r, i: (r, i, 0)),
            whole(w.shape),
            spec,
            spec,
        ],
        out_specs=[spec] * 3,
        out_shape=[shape] * 3,
        compiler_params=params(),
    )(x, w, cos, sin)


def attention_forward_kernel(width, q, k, v, q_code, k_code, out, low, log_sum):
    heads = width // HEAD
    lane = lax.broadcasted_iota(jnp.int32, q.shape[1:], 1) // HEAD
    allowed = (q_code[0] & 7) == k_code[0]
    queries = q[0] * 0.125
    result, logs = None, None
    for h in range(heads):
        chosen = jnp.where(lane == h, queries, jnp.zeros_like(queries))
        scores = lax.dot_general(
            chosen, k[0], (((1,), (1,)), ((), ())), preferred_element_type=F32
        )
        scores = jnp.where(allowed, scores, MASKED)
        peak = jnp.max(scores, axis=1, keepdims=True)
        weights = jnp.exp(scores - peak)
        total = jnp.sum(weights, axis=1, keepdims=True)
        value = jnp.dot(weights.astype(BF16), v[0], preferred_element_type=F32) / total
        log = jnp.broadcast_to(peak + jnp.log(total), value.shape)
        result = value if h == 0 else jnp.where(lane == h, value, result)
        logs = log if h == 0 else jnp.where(lane == h, log, logs)
    out[0] = result
    low[0] = result.astype(BF16)
    log_sum[0] = logs


def attention_forward(q, k, v, q_code, k_code):
    rows, length, width = q.shape
    block = 256
    spec = pl.BlockSpec((1, block, width), lambda r, i: (r, i, 0))
    row = pl.BlockSpec((1, length, width), lambda r, i: (r, 0, 0))
    return pl.pallas_call(
        functools.partial(attention_forward_kernel, width),
        grid=(rows, length // block),
        in_specs=[
            spec,
            row,
            row,
            pl.BlockSpec((1, block, 1), lambda r, i: (r, i, 0)),
            pl.BlockSpec((1, 1, length), lambda r, i: (r, 0, 0)),
        ],
        out_specs=[spec] * 3,
        out_shape=[
            jax.ShapeDtypeStruct(q.shape, F32),
            jax.ShapeDtypeStruct(q.shape, BF16),
            jax.ShapeDtypeStruct(q.shape, F32),
        ],
        compiler_params=params(),
    )(q, k, v, q_code, k_code)


BLOCK = 256


def attention_backward_kernel(
    length, width, low_edge, high_edge, q, k, v, g, log_sum, delta, k_code, q_code, cos, sin, out, dq, dk, dv
):
    heads = width // HEAD
    row = pl.program_id(0)
    lane = lax.broadcasted_iota(jnp.int32, (BLOCK, width), 1) // HEAD
    dk[...] = jnp.zeros_like(dk)
    dv[...] = jnp.zeros_like(dv)

    def outer(i, carry):
        at = pl.ds(pl.multiple_of(i * BLOCK, BLOCK), BLOCK)
        queries = q[0, at, :] * 0.125
        grads = g[0, at, :]
        zero = jnp.zeros_like(queries)
        queries_of = [jnp.where(lane == h, queries, zero) for h in range(heads)]
        grads_of = [jnp.where(lane == h, grads, zero) for h in range(heads)]
        dq[...] = jnp.zeros_like(dq)

        def inner(j, carry):
            to = pl.ds(pl.multiple_of(j * BLOCK, BLOCK), BLOCK)
            keys, values = k[0, to, :], v[0, to, :]
            allowed = k_code[0, to, :] == q_code[0, :, at]
            dk_part, dv_part, dq_part = None, None, None
            for h in range(heads):
                keys_of = jnp.where(lane == h, keys, zero)
                scores = lax.dot_general(
                    keys, queries_of[h], (((1,), (1,)), ((), ())), preferred_element_type=F32
                )
                probs = jnp.where(allowed, jnp.exp(scores - log_sum[0, h : h + 1, at]), 0.0)
                grad_probs = lax.dot_general(
                    values, grads_of[h], (((1,), (1,)), ((), ())), preferred_element_type=F32
                )
                grad_scores = (probs * (grad_probs - delta[0, h : h + 1, at])).astype(BF16)
                a = jnp.dot(probs.astype(BF16), grads_of[h], preferred_element_type=F32)
                c = jnp.dot(grad_scores, queries_of[h], preferred_element_type=F32)
                e = lax.dot_general(
                    grad_scores, keys_of, (((0,), (0,)), ((), ())), preferred_element_type=F32
                )
                dv_part = a if h == 0 else dv_part + a
                dk_part = c if h == 0 else dk_part + c
                dq_part = e if h == 0 else dq_part + e
            dv[to, :] = dv[to, :] + dv_part
            dk[to, :] = dk[to, :] + dk_part
            dq[...] = dq[...] + dq_part
            return carry

        lax.fori_loop(low_edge[row, i], high_edge[row, i], inner, 0)
        grad = dq[...] * 0.125
        turned = grad * cos[0, at, :] - pair_swap(grad) * sin[0, at, :]
        out[0, at, 0:width] = turned.astype(BF16)
        return carry

    lax.fori_loop(0, length // BLOCK, outer, 0)

    def finish(i, carry):
        at = pl.ds(pl.multiple_of(i * BLOCK, BLOCK), BLOCK)
        grad = dk[at, :]
        turned = grad * cos[0, at, :] - pair_swap(grad) * sin[0, at, :]
        out[0, at, width : 2 * width] = turned.astype(BF16)
        out[0, at, 2 * width : 3 * width] = dv[at, :].astype(BF16)
        return carry

    lax.fori_loop(0, length // BLOCK, finish, 0)


def attention_backward(q, k, v, g, log_sum, delta, k_code, q_code, cos, sin, low_edge, high_edge):
    rows, length, width = q.shape

    def spec(shape):
        return pl.BlockSpec((1,) + tuple(shape[1:]), lambda r, *_: (r,) + (0,) * (len(shape) - 1))

    arrays = (q, k, v, g, log_sum, delta, k_code, q_code, cos, sin)
    out = (rows, length, 3 * width)
    return pl.pallas_call(
        functools.partial(attention_backward_kernel, length, width),
        grid_spec=pltpu.PrefetchScalarGridSpec(
            num_scalar_prefetch=2,
            grid=(rows,),
            in_specs=[spec(a.shape) for a in arrays],
            out_specs=spec(out),
            scratch_shapes=[
                pltpu.VMEM((BLOCK, width), F32),
                pltpu.VMEM((length, width), F32),
                pltpu.VMEM((length, width), F32),
            ],
        ),
        out_shape=jax.ShapeDtypeStruct(out, BF16),
        compiler_params=params(),
    )(low_edge, high_edge, *arrays)


def pick(ids, table, rows):
    value = table[SEGS - 1 : SEGS, :]
    for u in range(SEGS - 2, -1, -1):
        value = jnp.where(ids == u, table[u : u + 1, :], value)
    return jnp.broadcast_to(value, (rows, table.shape[1]))


def gelu_parts(v):
    c = 0.7978845608
    t = jnp.tanh(c * (v + 0.044715 * v * v * v))
    half = 0.5 * (1.0 + t)
    return v * half, half + 0.5 * v * (1.0 - t * t) * c * (1.0 + 0.134145 * v * v)


STEP = 32


def feed_kernel(
    rows,
    frames,
    part,
    att,
    embedded,
    late,
    ids,
    mod,
    cotangent,
    block_out,
    grad_att,
    late_grads,
    grad_middle,
    sums,
    branch,
    middle,
    scale,
    normed,
    bend,
    low,
    grad_up,
    feed,
    grad_feed,
    grad_normed,
    grad_branch,
):
    tokens = rows * frames
    wide = 256
    per = wide // part

    def each_step(body):
        for r in range(rows):

            def step(i, carry, r=r):
                at = pl.ds(pl.multiple_of(r * frames + i * STEP, STEP), STEP)
                body(r, at)
                return carry

            lax.fori_loop(0, frames // STEP, step, 0)

    def gate(r, at, which):
        return pick(ids[at, :], mod[r, which], STEP)

    def columns(first, count, j):
        n = wide // count
        return late[j * n : (j + 1) * n, first : first + count, :].reshape(wide, D)

    for j in range(D // wide):
        branch[:, j * wide : (j + 1) * wide] = times_t(att[...], columns(0, part, j))

    def to_normed(r, at):
        value = embedded[at, :] + gate(r, at, 2) * branch[at, :]
        middle[at, :] = value
        centre = value - jnp.mean(value, axis=1, keepdims=True)
        factor = lax.rsqrt(jnp.mean(centre * centre, axis=1, keepdims=True) + EPSILON)
        hat = centre * factor
        scale[at, :] = jnp.broadcast_to(factor, (STEP, 128))
        normed[at, :] = (hat * (1.0 + gate(r, at, 4)) + gate(r, at, 3)).astype(BF16)

    each_step(to_normed)
    for j in range(2 * D // wide):
        lanes = slice(j * wide, (j + 1) * wide)
        value, slope = gelu_parts(times_t(normed[...], columns(part, 2 * part, j)))
        low[:, lanes] = value.astype(BF16)
        bend[:, lanes] = slope
    for j in range(D // wide):
        feed[:, j * wide : (j + 1) * wide] = times_t(
            low[:, :D], columns(3 * part, part, j)
        ) + times_t(low[:, D:], columns(4 * part, part, j))

    def to_out(r, at):
        gate_feed = gate(r, at, 5)
        block_out[at, :] = (middle[at, :] + gate_feed * feed[at, :]).astype(BF16)
        grad_feed[at, :] = (gate_feed * cotangent[at, :].astype(F32)).astype(BF16)

    each_step(to_out)

    def inner(first, count, lanes):
        return late[:, first : first + count, lanes].reshape(-1, wide)

    for half in range(2):
        for j in range(D // wide):
            lanes = slice(half * D + j * wide, half * D + (j + 1) * wide)
            weights = inner((3 + half) * part, part, slice(j * wide, (j + 1) * wide))
            grad_up[:, lanes] = (times(grad_feed[...], weights) * bend[:, lanes]).astype(BF16)
    for j in range(D // wide):
        lanes = slice(j * wide, (j + 1) * wide)
        grad_normed[:, lanes] = times(grad_up[...], inner(part, 2 * part, lanes))

    sums[...] = jnp.zeros_like(sums)

    def back(r, at):
        value = middle[at, :]
        factor = scale[at, 0:1]
        hat = (value - jnp.mean(value, axis=1, keepdims=True)) * factor
        grad = grad_normed[at, :]
        e = grad * (1.0 + gate(r, at, 4))
        out = cotangent[at, :].astype(F32)
        total = out + factor * (
            e
            - jnp.mean(e, axis=1, keepdims=True)
            - hat * jnp.mean(e * hat, axis=1, keepdims=True)
        )
        grad_middle[at, :] = total
        grad_branch[at, :] = (gate(r, at, 2) * total).astype(BF16)
        first = ids[at, :] == ids[r * frames : r * frames + 1, :]
        for k, part_sum in enumerate(
            (total * branch[at, :], grad, grad * hat, out * feed[at, :])
        ):
            kept = jnp.where(first, part_sum, 0.0)
            other = part_sum - kept
            for side, piece in enumerate((kept, other)):
                folded = piece[0:8]
                for q in range(1, STEP // 8):
                    folded = folded + piece[8 * q : 8 * q + 8]
                sums[r, side, k] = sums[r, side, k] + folded

    each_step(back)
    for j in range(D // wide):
        lanes = slice(j * wide, (j + 1) * wide)
        grad_att[:, lanes] = times(grad_branch[...], inner(0, part, lanes)).astype(BF16)
        late_grads[j * per : (j + 1) * per, 0:part, :] = (
            rows_sum(grad_branch[:, lanes], att[...]).astype(BF16).reshape(per, part, D)
        )
        for half in range(2):
            late_grads[j * per : (j + 1) * per, (3 + half) * part : (4 + half) * part, :] = (
                rows_sum(grad_feed[:, lanes], low[:, half * D : (half + 1) * D])
                .astype(BF16)
                .reshape(per, part, D)
            )
    for j in range(2 * D // wide):
        lanes = slice(j * wide, (j + 1) * wide)
        late_grads[j * per // 2 : (j + 1) * per // 2, part : 3 * part, :] = (
            rows_sum(grad_up[:, lanes], normed[...]).astype(BF16).reshape(per // 2, 2 * part, D)
        )


def feed_both(att, embedded, late, ids, mod, cotangent, rows, frames, part):
    tokens = rows * frames
    vmem = pl.BlockSpec(memory_space=pltpu.VMEM)

    def scratch(width, dtype):
        return pltpu.VMEM((tokens, width), dtype)

    return pl.pallas_call(
        functools.partial(feed_kernel, rows, frames, part),
        in_specs=[vmem] * 6,
        out_specs=[vmem] * 5,
        out_shape=[
            jax.ShapeDtypeStruct((tokens, D), BF16),
            jax.ShapeDtypeStruct((tokens, D), BF16),
            jax.ShapeDtypeStruct(late.shape, BF16),
            jax.ShapeDtypeStruct((tokens, D), F32),
            jax.ShapeDtypeStruct((rows, 2, 4, 8, D), F32),
        ],
        scratch_shapes=[
            scratch(D, F32),
            scratch(D, F32),
            scratch(128, F32),
            scratch(D, BF16),
            scratch(2 * D, F32),
            scratch(2 * D, BF16),
            scratch(2 * D, BF16),
            scratch(D, F32),
            scratch(D, BF16),
            scratch(D, F32),
            scratch(D, BF16),
        ],
        compiler_params=params(),
    )(att, embedded, late, ids, mod, cotangent)


def layer_norm(field):
    centre = field - jnp.mean(field, axis=-1, keepdims=True)
    return centre * lax.rsqrt(jnp.mean(centre * centre, axis=-1, keepdims=True) + EPSILON)


def modulate(field, scaling, shifting):
    return layer_norm(field) * (1.0 + scaling) + shifting


def gelu_curve(inputs):
    return jax.nn.gelu(inputs, approximate=True)


def by_segment(ids, table):
    value = table[:, SEGS - 1][:, None, :]
    for u in range(SEGS - 2, -1, -1):
        value = jnp.where(ids[:, :, None] == u, table[:, u][:, None, :], value)
    return value


def rope_tables(segment_ids, starts, width):
    length = segment_ids.shape[1]
    pairs = (np.arange(width) % HEAD) // 2
    freq = 10000.0 ** (-2.0 * pairs / HEAD)
    angle = np.arange(length)[:, None] * freq[None, :]
    cos_t = jnp.asarray(np.cos(angle).astype(np.float32))[None]
    sin_t = jnp.asarray(np.sin(angle).astype(np.float32))[None]
    offset = starts.astype(F32)[:, :, None] * jnp.asarray(freq.astype(np.float32))
    cos_o = by_segment(segment_ids, jnp.cos(offset))
    sin_o = by_segment(segment_ids, jnp.sin(offset))
    return cos_t * cos_o + sin_t * sin_o, sin_t * cos_o - cos_t * sin_o


def on_device(
    mel_inputs,
    text_ids,
    segment_ids,
    key_mask,
    time_index,
    input_proj,
    conv_first,
    conv_second,
    time_table,
    adaln_proj,
    qkv_proj,
    out_proj,
    up_proj,
    down_proj,
    text_table,
    grad_out,
):
    nb, n = dims()
    ndev = nb * n
    rows, frames = mel_inputs.shape[:2]
    tokens = rows * frames
    length = frames * n
    width = D // n
    part = D // ndev
    mine = lax.axis_index("seq")
    first_frame = mine * frames

    out_t, up_t, down_t = out_proj.T, up_proj.T, down_proj.T
    wide_t = jnp.concatenate([out_t, up_t, down_t[:, :D], down_t[:, D:]], axis=0)
    per = wide_t.shape[0]
    (
        (full_in,),
        (full_text,),
        (full_time,),
        (all_index,),
        (got_convs,),
    ) = transfer(
        [
            spread_task(input_proj.T),
            spread_task(text_table.T),
            spread_task(time_table.T),
            spread_task(time_index),
            columns_out_task(jnp.concatenate([conv_first, conv_second], axis=2)[None]),
        ],
        0,
    )
    got_convs = got_convs[0]
    wide_t, _ = lax.optimization_barrier((wide_t, all_index))
    late = lax.all_gather(wide_t, ("batch", "seq"), axis=0, tiled=True).reshape(ndev, per, D)
    in_t = full_in.reshape(D, input_proj.shape[0])
    text_t = full_text.reshape(-1, VOCAB)
    time_t = full_time.reshape(D, STEPS)
    slot_steps = all_index[:, 0].reshape(nb * rows * SEGS)

    own_ids = lax.dynamic_slice_in_dim(segment_ids, first_frame, frames, 1)
    key_code = segment_ids + jnp.where(key_mask > 0, 0, 8)
    seg_column = key_code[:, :, None]
    seg_index = jnp.arange(SEGS, dtype=jnp.int32)
    starts = jnp.sum((segment_ids[:, None, :] < seg_index[None, :, None]).astype(jnp.int32), axis=2)

    text_hot = (
        text_ids.reshape(-1)[:, None] == jnp.arange(VOCAB, dtype=jnp.int32)[None, :]
    ).astype(BF16)
    text_embed = times_t(text_hot, text_t).astype(BF16)
    joined = jnp.concatenate([mel_inputs.reshape(tokens, 2 * MEL), text_embed], axis=1)
    hidden = times_t(joined, in_t).reshape(rows, frames, D)

    step_hot = (
        slot_steps[:, None] == jnp.arange(STEPS, dtype=jnp.int32)[None, :]
    ).astype(BF16)
    cond_value = times_t(step_hot, time_t)
    soft_cond = jax.nn.silu(cond_value).astype(BF16)
    own_mod = times(soft_cond, adaln_proj)
    task, arrange = to_channels(hidden.astype(BF16))
    got, (mod_got,) = transfer(
        [task, spray_task(own_mod.reshape(nb, rows * SEGS, 6 * part), True)], 2
    )
    hidden_c = arrange(got)
    modulation = mod_got.transpose(1, 0, 2).reshape(rows, SEGS, 6, D)
    shift_attn, scale_attn = (by_segment(own_ids, modulation[:, :, i]) for i in range(2))

    conv_one, conv_two, bump_c = conv_forward(hidden_c, seg_column, got_convs)
    task, arrange = to_frames(bump_c)
    bump = arrange(transfer([task], 3)[0])
    embedded = hidden + bump.astype(F32)

    normed = modulate(embedded, scale_attn, shift_attn).astype(BF16)
    gather = quad_gather_task if n == 8 else gather_task
    (normed_all,), (got_qkv,) = transfer(
        [gather(normed), columns_out_task(qkv_proj.T.reshape(3, part, D))], 4
    )
    normed_all = normed_all.reshape(rows, length, D)
    qkv_t = got_qkv.reshape(3 * width, D)
    cos, sin = rope_tables(segment_ids, starts, width)
    query, key, value = qkv_forward(normed_all, qkv_t, cos, sin)
    attended, attended_low, log_lanes = attention_forward(
        query, key, value, seg_column, key_code[:, None, :]
    )
    task, arrange = to_frames(attended_low)
    attended_own = arrange(transfer([task], 5)[0])
    attended_own = attended_own.reshape(tokens, D)

    block_out, grad_att, late_grads, grad_middle, feed_sums = feed_both(
        attended_own,
        embedded.reshape(tokens, D),
        late,
        own_ids.reshape(tokens, 1),
        modulation.transpose(0, 2, 1, 3),
        grad_out.reshape(tokens, D),
        rows,
        frames,
        part,
    )
    block_out = block_out.reshape(rows, frames, D)
    grad_att = grad_att.reshape(rows, frames, D)
    grad_middle = grad_middle.reshape(rows, frames, D)
    task, arrange = to_channels(grad_att)
    grad_att_c = arrange(transfer([task], 6)[0])
    heads = width // HEAD
    delta = jnp.sum(
        (grad_att_c.astype(F32) * attended).reshape(rows, length, heads, HEAD), axis=3
    ).transpose(0, 2, 1)
    log_rows = log_lanes.reshape(rows, length, heads, HEAD)[:, :, :, 0].transpose(0, 2, 1)
    block_first_ids = segment_ids[:, ::BLOCK]
    block_last_ids = segment_ids[:, BLOCK - 1 :: BLOCK]
    ends = jnp.sum((segment_ids[:, None, :] <= seg_index[None, :, None]).astype(jnp.int32), axis=2)
    low_edge = (
        jnp.sum(jnp.where(block_first_ids[:, :, None] == seg_index, starts[:, None, :], 0), axis=2)
        // BLOCK
    )
    high_edge = (
        jnp.sum(jnp.where(block_last_ids[:, :, None] == seg_index, ends[:, None, :], 0), axis=2)
        + BLOCK
        - 1
    ) // BLOCK
    grad_projected = attention_backward(
        query,
        key,
        value,
        grad_att_c,
        log_rows,
        delta,
        seg_column,
        segment_ids[:, None, :],
        cos,
        sin,
        low_edge,
        high_edge,
    ).reshape(rows * length, 3 * width)
    grad_qkv = rows_sum(grad_projected, normed_all.reshape(rows * length, D)).astype(BF16)
    partial = times(grad_projected, qkv_t).astype(BF16).reshape(rows, n, frames, D)
    (grad_normed,), (got_qkv_grads,) = transfer(
        [sum_task(partial), columns_back_task(grad_qkv.reshape(3, nb, part, D))], 7
    )
    late_grads, grad_normed = lax.optimization_barrier((late_grads, grad_normed))
    late_sum = lax.psum_scatter(
        late_grads, ("batch", "seq"), scatter_dimension=0, tiled=False
    ).astype(F32)

    grad_emb_part, grad_scale_attn, grad_shift_attn = jax.vjp(
        modulate, embedded, scale_attn, shift_attn
    )[1](grad_normed)
    grad_embedded = grad_middle + grad_emb_part

    first_ids, last_ids = own_ids[:, 0], own_ids[:, -1]
    first = (own_ids == first_ids[:, None])[:, :, None]
    attn_sums = [
        jnp.stack([jnp.sum(jnp.where(first, g, 0.0), axis=1), jnp.sum(jnp.where(first, 0.0, g), axis=1)], axis=1)
        for g in (grad_shift_attn, grad_scale_attn)
    ]
    feed_sums = jnp.sum(feed_sums, axis=3)
    sides = jnp.concatenate(
        [attn_sums[0], attn_sums[1]] + [feed_sums[:, :, i] for i in range(4)], axis=2
    )
    is_first = (first_ids[:, None] == seg_index).astype(F32)
    is_last = (last_ids[:, None] == seg_index).astype(F32)
    local_sums = is_first[:, :, None] * sides[:, :1] + is_last[:, :, None] * sides[:, 1:]
    slots = rows * SEGS
    sums_out = local_sums.reshape(slots, ndev, 6 * part).transpose(1, 0, 2)
    task, arrange = to_channels(grad_embedded.astype(BF16))
    got, (sums_got,) = transfer([task, spray_task(sums_out, False)], 10)
    grad_emb_c = arrange(got)
    sums_got = sums_got.reshape(nb, n, slots, 6 * part)
    grad_mod = jnp.sum(sums_got, axis=1).astype(BF16).reshape(nb * slots, 6 * part)
    grad_adaln = rows_sum(soft_cond, grad_mod)
    soft_part = times_t(grad_mod, adaln_proj)
    soft_out = soft_part.reshape(nb * slots, ndev, part).transpose(1, 0, 2)
    grad_hidden_c, conv_sums = conv_backward(
        grad_emb_c, hidden_c, seg_column, conv_one, conv_two, got_convs, nb
    )
    task, arrange = to_frames(grad_hidden_c)
    got, (soft_got,), (got_conv_grads,) = transfer(
        [task, spray_task(soft_out, False), columns_back_task(conv_sums)], 11
    )
    grad_hidden_conv = arrange(got)
    grad_soft = jnp.sum(soft_got, axis=0)
    own_cond = times(step_hot, time_table)
    grad_cond = jax.vjp(jax.nn.silu, own_cond)[1](grad_soft)[0]
    grad_time = jnp.dot(step_hot.astype(F32).T, grad_cond, precision=EXACT)
    grad_convs = jnp.sum(got_conv_grads.astype(F32), axis=0)[0]
    grad_first, grad_second = grad_convs[..., :CHAN], grad_convs[..., CHAN:]
    grad_qkv_own = jnp.sum(got_qkv_grads.astype(F32), axis=0).reshape(3 * part, D).T

    grad_hidden = (grad_embedded + grad_hidden_conv.astype(F32)).astype(BF16).reshape(tokens, D)
    grad_input = rows_sum(grad_hidden, joined).astype(BF16)
    grad_joined = times(grad_hidden, in_t)
    grad_mels = grad_joined[:, : 2 * MEL].reshape(rows, frames, 2 * MEL)
    grad_embed = grad_joined[:, 2 * MEL :].astype(BF16)
    grad_text = rows_sum(grad_embed, text_hot).astype(BF16)
    (in_sum,), (text_sum,) = transfer(
        [
            scatter_task(grad_input.reshape(nb, n, part, -1)),
            scatter_task(grad_text.reshape(nb, n, -1, VOCAB)),
        ],
        13,
    )
    grad_input_own = jnp.sum(in_sum.astype(F32), axis=0).T
    grad_text_own = jnp.sum(text_sum.astype(F32), axis=0).T
    grad_down_own = jnp.concatenate([late_sum[3 * part : 4 * part], late_sum[4 * part :]], axis=1)

    return (
        block_out,
        grad_mels,
        grad_input_own,
        grad_first,
        grad_second,
        grad_time,
        grad_adaln,
        grad_qkv_own,
        late_sum[:part].T,
        late_sum[part : 3 * part].T,
        grad_down_own.T,
        grad_text_own,
    )


def solution(mesh):
    frames = P("batch", "seq", None)
    columns = P(None, ("batch", "seq"))
    taps = P(None, ("batch", "seq"), None)
    in_specs = (
        frames,
        P("batch", "seq"),
        P("batch", None),
        P("batch", None),
        P("batch", None),
        columns,
        taps,
        taps,
        columns,
        columns,
        columns,
        columns,
        columns,
        columns,
        columns,
        frames,
    )
    out_specs = (
        frames,
        frames,
        columns,
        taps,
        taps,
        columns,
        columns,
        columns,
        columns,
        columns,
        columns,
        columns,
    )
    return jax.shard_map(
        on_device, mesh=mesh, in_specs=in_specs, out_specs=out_specs, check_vma=False
    )
```

time: 941 us -> 626 us (0.67)
  Pallas kernels: 718 us -> 512 us
  local copies, waits for them, and re-layouts: 85.7 us -> 27 us
  matrix products: 56.4 us -> 27.7 us
  other arithmetic: 56.9 us -> 37.6 us
    pallas_call x16 -> x13, Pallas kernels: 643 us -> 432 us  [the longest x10 332 us: transfer(): pl.pallas_call(functools.partial(transfer_kernel, [t.body for t in tasks]...]
    unnamed x260 -> x130, local copies, waits for them, and re-layouts: 31.7 us -> 6.76 us
    concatenate x3 -> x0, other arithmetic: 14 us -> none  [the longest x1 13.3 us: on_device(): jnp.concatenate([grad_out_weights.reshape(ndev, part, D), grad_up.reshape...]
    dot_general x7 -> x4, matrix products: 17.6 us -> 6.39 us  [times_t(): lax.dot_general(left, right, (((1,), (1,)), ((), ())), preferred_element_...]
    another operation x10 -> x4, local copies, waits for them, and re-layouts: 10 us -> 0.03 us  [on_device(): jnp.stack([jnp.sum(jnp.where(first, g, 0.0), axis=1), jnp.sum(jnp.where(f...]
  transfers between devices with their start and end apart: 2 -> 2, of which waited for: 0 -> 0; matrix products, arithmetic and copies ran while one was open for 15% -> 11% of each run, Pallas kernels for 77% -> 51%
where the time goes in v2:
time: 626 us; the launch traced here: 619 us
  Pallas kernels  512 us (82%)
  other arithmetic  37.6 us (6%)
  matrix products  27.7 us (4%)
  local copies, waits for them, and re-layouts  27 us (4%)
  between operations  15.3 us (2%)
    pallas_call x10, Pallas kernels, transfer(): pl.pallas_call(functools.partial(transfer_kernel, [t.body for t in tasks]...  332 us
    pallas_call x1, Pallas kernels, attention_backward(): pl.pallas_call(functools.partial(attention_backward_kernel, length, width...  46.8 us
    pallas_call x1, Pallas kernels, conv_backward(): pl.pallas_call(functools.partial(conv_backward_kernel, count, length, gro...  43.4 us
    pallas_call x1, Pallas kernels, feed_both(): pl.pallas_call(functools.partial(feed_kernel, rows, frames, part), in_spe...  32.8 us
    pallas_call x1, Pallas kernels, conv_forward(): pl.pallas_call(functools.partial(conv_forward_kernel, count, length, grou...  23.8 us
    pallas_call x1, Pallas kernels, attention_forward(): pl.pallas_call(functools.partial(attention_forward_kernel, width), grid=(...  23.4 us
  transfers between devices with their start and end apart: 2, of which 0 were waited for; matrix products, arithmetic and copies ran while one was open for 11% of the time, Pallas kernels for 51%

profile of v2, /device:TPU:1, one launch (start us, length us, event | category | flops | bytes accessed | tf_op | source)
XLA Modules:
  0.0 619.1 jit_solution(14517531189261053732)
XLA Ops:
  9.5 1.9 maximum_bitcast_fusion.1.refs_4_
  13.1 53.1 %shard_map.274 = (bf16[4,8,32,712]{3,2,1,0:T(8,128)(2,1)}, bf16[4,8,16,2546]{3,2,1,0:T(8,128)(2,1)}, bf16[4,8,32,32]{3,2,1,0:T(8,128)(2,1)}, s32[4,8,2,4]{3,2,1,0:T(2,128)}, bf16[1,4,31,32,128]{4,3,2,1,0:T(8,128)(2,1)}) custom-call(bf16[32,712]{1,0:T(8,128)(2,1)} %bitcast.221, bf16[16,2546]{1,0:T(8,128)(2,1)} %bitcast.219, bf16[32,32]{1,0:T(8,128)(2,1)} %bitcast.226, ...), custom_call_target="tpu_custom_call" | custom-call | tf_op jit(solution)/shard_map/pallas_call | solution.py:133
  73.3 1.7 copy.82.seg.q_code.k_code
  76.2 3.1 fusion.4
  79.4 1.7 fusion.53
  81.1 20.2 %shard_map.275 = (bf16[2,1536,128]{2,1,0:T(8,128)(2,1)}, f32[32,8,192]{2,1,0:T(8,128)}) custom-call(bf16[2,192,1024]{2,1,0:T(8,128)(2,1)} %get-tuple-element.190.refs_0_, f32[4,8,192]{2,1,0:T(8,128)} %convolution_bitcast_fusion.1.refs_1_), custom_call_target="tpu_custom_call" | custom-call | tf_op jit(solution)/shard_map/pallas_call | solution.py:133
  103.6 23.8 %shard_map.276 = (f32[2,2,400,256]{3,2,1,0:T(8,128)}, f32[2,2,400,256]{3,2,1,0:T(8,128)}, bf16[2,1536,128]{2,1,0:T(8,128)(2,1)}) custom-call(bf16[2,1536,128]{2,1,0:T(8,128)(2,1)} %get-tuple-element.53.u, s32[2,1536,1]{2,1,0:T(8,128)} %copy.82.seg.q_code.k_code, bf16[4,31,32,128]{3,2,1,0:T(8,128)(2,1)} %bitcast.177), custom_call_target="tpu_custom_call" | custom-call | tf_op jit(solution)/shard_map/pallas_call | solution.py:933
  127.4 19.7 %shard_map.277 = bf16[2,192,1024]{2,1,0:T(8,128)(2,1)} custom-call(bf16[2,1536,128]{2,1,0:T(8,128)(2,1)} %get-tuple-element.55.refs_0_), custom_call_target="tpu_custom_call" | custom-call | tf_op jit(solution)/shard_map/pallas_call | solution.py:133
  149.1 3.5 add_convert_fusion.1.refs_0_
  152.6 42.7 %shard_map.278 = (bf16[2,8,192,1024]{3,2,1,0:T(8,128)(2,1)}, bf16[3,4,32,1024]{3,2,1,0:T(8,128)(2,1)}) custom-call(bf16[2,192,1024]{2,1,0:T(8,128)(2,1)} %add_convert_fusion.1.refs_0_, bf16[3,32,1024]{2,1,0:T(8,128)(2,1)} %bitcast.199), custom_call_target="tpu_custom_call" | custom-call | tf_op jit(solution)/shard_map/pallas_call | solution.py:133
  195.6 4.2 multiply_subtract_fusion
  199.8 9.4 %shard_map.279 = (bf16[2,1536,128]{2,1,0:T(8,128)(2,1)}, bf16[2,1536,128]{2,1,0:T(8,128)(2,1)}, bf16[2,1536,128]{2,1,0:T(8,128)(2,1)}) custom-call(bf16[2,1536,1024]{2,1,0:T(8,128)(2,1)} %bitcast.165, bf16[384,1024]{1,0:T(8,128)(2,1)} %bitcast.185, f32[2,1536,128]{2,1,0:T(8,128)} %get-tuple-element.150.cos, f32[2,1536,128]{2,1,0:T(8,128)} %get-tuple-element.149.sin), custom_call_target="tpu_custom_call" | custom-call | tf_op jit(solution)/shard_map/pallas_call | solution.py:1109
  209.3 23.4 %shard_map.280 = (f32[2,1536,128]{2,1,0:T(8,128)}, bf16[2,1536,128]{2,1,0:T(8,128)(2,1)}, f32[2,1536,128]{2,1,0:T(8,128)}) custom-call(bf16[2,1536,128]{2,1,0:T(8,128)(2,1)} %get-tuple-element.59.q, bf16[2,1536,128]{2,1,0:T(8,128)(2,1)} %get-tuple-element.60.k, bf16[2,1536,128]{2,1,0:T(8,128)(2,1)} %get-tuple-element.61.v, ...), custom_call_target="tpu_custom_call" | custom-call | tf_op jit(solution)/shard_map/pallas_call | solution.py:1153
  232.7 12.2 %shard_map.281 = bf16[2,192,1024]{2,1,0:T(8,128)(2,1)} custom-call(bf16[2,1536,128]{2,1,0:T(8,128)(2,1)} %get-tuple-element.62.refs_0_), custom_call_target="tpu_custom_call" | custom-call | tf_op jit(solution)/shard_map/pallas_call | solution.py:133
  248.1 32.8 %shard_map.282 = (bf16[384,1024]{1,0:T(8,128)(2,1)}, bf16[384,1024]{1,0:T(8,128)(2,1)}, bf16[32,160,1024]{2,1,0:T(8,128)(2,1)}, f32[384,1024]{1,0:T(8,128)}, f32[2,2,4,8,1024]{4,3,2,1,0:T(8,128)}) custom-call(bf16[384,1024]{1,0:T(8,128)(2,1)} %bitcast.180, f32[384,1024]{1,0:T(8,128)} %bitcast.164, bf16[32,160,1024]{2,1,0:T(8,128)(2,1)} %bitcast.172, ...), custom_call_target="tpu_custom_call" | custom-call | tf_op jit(solution)/shard_map/pallas_call | solution.py:1429
  280.8 12.2 %shard_map.283.g = bf16[2,1536,128]{2,1,0:T(8,128)(2,1)} custom-call(bf16[2,192,1024]{2,1,0:T(8,128)(2,1)} %bitcast.187), custom_call_target="tpu_custom_call" | custom-call | tf_op jit(solution)/shard_map/pallas_call | solution.py:133
  295.6 46.8 %shard_map.284 = bf16[2,1536,384]{2,1,0:T(8,128)(2,1)} custom-call(s32[2,6]{1,0:T(2,128)} %get-tuple-element.195.low_edge, s32[2,6]{1,0:T(2,128)} %get-tuple-element.194.high_edge, bf16[2,1536,128]{2,1,0:T(8,128)(2,1)} %get-tuple-element.59.q, bf16[2,1536,128]{2,1,0:T(8,128)(2,1)} %get-tuple-element.60.k, bf16[2,1536,128]{2,1,0:T(8,128)(2,1)} %get-tuple-element.61.v, ...), custom_call_target="tpu_custom_call" | custom-call | tf_op jit(solution)/shard_map/pallas_call | solution.py:1249
  342.4 7.3 %convolution_convert_fusion = bf16[3072,1024]{1,0:T(8,128)(2,1)} fusion(bf16[3072,384]{1,0:T(8,128)(2,1)} %bitcast.169, bf16[384,1024]{1,0:T(8,128)(2,1)S(1)} %bitcast.186), kind=kOutput, calls=%fused_computation | convolution fusion | flops 2419064832 | bytes 9437184 | tf_op jit(solution)/shard_map/dot_general | solution.py:746
  349.8 3.5 convolution_convert_fusion.3
  353.3 49.3 %shard_map.285 = (f32[2,192,1024]{2,1,0:T(8,128)}, bf16[4,3,32,1024]{3,2,1,0:T(8,128)(2,1)}) custom-call(bf16[2,8,192,1024]{3,2,1,0:T(8,128)(2,1)} %bitcast.173, bf16[3,4,32,1024]{3,2,1,0:T(8,128)(2,1)} %bitcast.179), custom_call_target="tpu_custom_call" | custom-call | tf_op jit(solution)/shard_map/pallas_call | solution.py:133
  407.2 2.8 select_reduce_fusion.1
  412.8 2.3 fusion.44
  417.3 32.1 %shard_map.286 = (bf16[2,1536,128]{2,1,0:T(8,128)(2,1)}, f32[32,8,192]{2,1,0:T(8,128)}) custom-call(bf16[2,192,1024]{2,1,0:T(8,128)(2,1)} %fusion.5.refs_0_, f32[32,8,192]{2,1,0:T(8,128)} %fusion.14.refs_1_), custom_call_target="tpu_custom_call" | custom-call | tf_op jit(solution)/shard_map/pallas_call | solution.py:133
  449.4 43.4 %shard_map.287 = (bf16[2,1536,128]{2,1,0:T(8,128)(2,1)}, bf16[1,4,31,32,128]{4,3,2,1,0:T(8,128)(2,1)}) custom-call(bf16[2,1536,128]{2,1,0:T(8,128)(2,1)} %get-tuple-element.73.d, bf16[2,1536,128]{2,1,0:T(8,128)(2,1)} %get-tuple-element.53.u, s32[2,1536,1]{2,1,0:T(8,128)} %copy.82.seg.q_code.k_code, f32[2,2,400,256]{3,2,1,0:T(8,128)} %get-tuple-element.74.c1, ...), custom_call_target="tpu_custom_call" | custom-call | tf_op jit(solution)/shard_map/pallas_call | solution.py:1053
  494.1 44.4 %shard_map.288 = (bf16[2,192,1024]{2,1,0:T(8,128)(2,1)}, f32[32,32,32]{2,1,0:T(8,128)}, bf16[4,1,31,32,128]{4,3,2,1,0:T(8,128)(2,1)}) custom-call(bf16[2,1536,128]{2,1,0:T(8,128)(2,1)} %get-tuple-element.76.refs_0_, f32[32,32,32]{2,1,0:T(8,128)} %convolution_bitcast_fusion.refs_1_, bf16[1,4,31,32,128]{4,3,2,1,0:T(8,128)(2,1)} %get-tuple-element.78.refs_2_), custom_call_target="tpu_custom_call" | custom-call | tf_op jit(solution)/shard_map/pallas_call | solution.py:133
  538.6 1.7 reduce_sum.213
  545.5 2.1 fusion.54
  549.5 2.8 convolution_convert_fusion.1
  552.3 2.9 copy.100
  555.2 46.0 %shard_map.289 = (bf16[4,32,712]{2,1,0:T(8,128)(2,1)}, bf16[4,16,2546]{2,1,0:T(8,128)(2,1)}) custom-call(bf16[4,8,32,712]{3,2,1,0:T(8,128)(2,1)} %bitcast.176, bf16[4,8,16,2546]{3,2,1,0:T(8,128)(2,1)} %bitcast.171), custom_call_target="tpu_custom_call" | custom-call | tf_op jit(solution)/shard_map/pallas_call | solution.py:133
  601.3 1.7 convert_reduce_fusion.3
  603.0 1.7 convert_reduce_fusion.2
  (214 shorter events, 47.2 us)
Async XLA Ops:
  7.2 59.1 %copy-start.24 = (s32[2,1536]{1,0:T(2,128)S(1)}, s32[2,1536]{1,0:T(2,128)}, u32[]{:S(2)}) copy-start(s32[2,1536]{1,0:T(2,128)} %param.21) | copy-start | bytes 36868
  7.2 61.7 %copy-start.44 = (s32[2,192]{1,0:T(2,128)S(1)}, s32[2,192]{1,0:T(2,128)}, u32[]{:S(2)}) copy-start(s32[2,192]{1,0:T(2,128)} %param.20) | copy-start | bytes 4612
  7.2 63.2 %copy-start.40 = (s32[2,1536]{1,0:T(2,128)S(1)}, s32[2,1536]{1,0:T(2,128)}, u32[]{:S(2)}) copy-start(s32[2,1536]{1,0:T(2,128)} %param.22) | copy-start | bytes 36868
  7.2 240.9 %all-gather.2.cloned.1.call-start = ((), (), s32[]{:S(2)}) async-start(), calls=%async_computation.1 | async-start | bytes 10813440 | tf_op jit(solution)/shard_map/all_gather | solution.py:1539
  66.2 8.9 %copy-start.52 = (bf16[4,8,32,32]{3,2,1,0:T(8,128)(2,1)S(1)}, bf16[4,8,32,32]{3,2,1,0:T(8,128)(2,1)}, u32[]{:S(2)}) copy-start(bf16[4,8,32,32]{3,2,1,0:T(8,128)(2,1)} %get-tuple-element.52) | copy-start | bytes 196612
  66.2 9.1 %copy-start.10 = (bf16[1024,192]{0,1:T(8,128)(2,1)S(1)}, bf16[1024,192]{0,1:T(8,128)(2,1)}, u32[]{:S(2)}) copy-start(bf16[1024,192]{0,1:T(8,128)(2,1)} %param.28) | copy-start | bytes 1179652
  66.2 542.7 %reduce-scatter.2.cloned.1.call-start = ((), (), s32[]{:S(2)}) async-start(), calls=%async_computation.2 | async-start | bytes 10813440 | tf_op jit(solution)/shard_map/reduce_scatter | solution.py:1646
  69.0 10.3 %copy-start.45 = (s32[384]{0:T(512)}, s32[384]{0:T(512)S(1)}, u32[]{:S(2)}) copy-start(s32[384]{0:T(512)S(1)} %eq.134) | copy-start | bytes 4612
  71.8 7.6 %copy-start.43 = (s32[2]{0:T(128)}, s32[2]{0:T(128)S(1)}, u32[]{:S(2)}) copy-start(s32[2]{0:T(128)S(1)} %get-tuple-element.140) | copy-start | bytes 28
  103.6 45.4 %copy-start.27 = (f32[2,1,1024]{2,0,1:T(2,128)}, f32[2,1,1024]{2,0,1:T(2,128)S(1)}, u32[]{:S(2)}) copy-start(f32[2,1,1024]{2,0,1:T(2,128)S(1)} %copy.163) | copy-start | bytes 24580
  103.6 45.4 %copy-start.29 = (f32[2,1,1024]{2,0,1:T(2,128)}, f32[2,1,1024]{2,0,1:T(2,128)S(1)}, u32[]{:S(2)}) copy-start(f32[2,1,1024]{2,0,1:T(2,128)S(1)} %copy.164) | copy-start | bytes 24580
  148.9 46.4 %copy-start.34 = (f32[2,192]{1,0:T(2,128)}, f32[2,192]{1,0:T(2,128)S(1)}, u32[]{:S(2)}) copy-start(f32[2,192]{1,0:T(2,128)S(1)} %multiply_reduce_fusion.1) | copy-start | bytes 4612
  149.0 46.4 %copy-start.33 = (f32[2,192]{1,0:T(2,128)}, f32[2,192]{1,0:T(2,128)S(1)}, u32[]{:S(2)}) copy-start(f32[2,192]{1,0:T(2,128)S(1)} %fusion.40) | copy-start | bytes 4612
  149.0 46.3 %copy-start.36 = (pred[2,192]{1,0:T(4,128)(4,1)}, pred[2,192]{1,0:T(4,128)(4,1)S(1)}, u32[]{:S(2)}) copy-start(pred[2,192]{1,0:T(4,128)(4,1)S(1)} %get-tuple-element.187) | copy-start | bytes 1156
  149.0 46.3 %copy-start.37 = (pred[2,192]{1,0:T(4,128)(4,1)}, pred[2,192]{1,0:T(4,128)(4,1)S(1)}, u32[]{:S(2)}) copy-start(pred[2,192]{1,0:T(4,128)(4,1)S(1)} %get-tuple-element.188) | copy-start | bytes 1156
  149.0 46.3 %copy-start.38 = (pred[2,192]{1,0:T(4,128)(4,1)}, pred[2,192]{1,0:T(4,128)(4,1)S(1)}, u32[]{:S(2)}) copy-start(pred[2,192]{1,0:T(4,128)(4,1)S(1)} %get-tuple-element.189) | copy-start | bytes 1156
  149.0 46.3 %copy-start.51 = (f32[128]{0:T(128)S(1)}, f32[128]{0:T(128)}, u32[]{:S(2)}) copy-start(f32[128]{0:T(128)} %constant.71.clone) | copy-start | bytes 1540
  149.1 46.5 %copy-start.16 = (f32[1536,128]{1,0:T(8,128)S(1)}, f32[1536,128]{1,0:T(8,128)}, u32[]{:S(2)}) copy-start(f32[1536,128]{1,0:T(8,128)} %constant.70.clone) | copy-start | bytes 2359300
  149.1 46.5 %copy-start.17 = (f32[1536,128]{1,0:T(8,128)S(1)}, f32[1536,128]{1,0:T(8,128)}, u32[]{:S(2)}) copy-start(f32[1536,128]{1,0:T(8,128)} %constant.69.clone) | copy-start | bytes 2359300
  232.7 12.2 %copy-start.9 = (f32[2,1536,128]{2,1,0:T(8,128)S(1)}, f32[2,1536,128]{2,1,0:T(8,128)}, u32[]{:S(2)}) copy-start(f32[2,1536,128]{2,1,0:T(8,128)} %get-tuple-element.68) | copy-start | bytes 4718596
  280.8 12.3 %copy-start.11 = (f32[2,1536,128]{2,1,0:T(8,128)S(1)}, f32[2,1536,128]{2,1,0:T(8,128)}, u32[]{:S(2)}) copy-start(f32[2,1536,128]{2,1,0:T(8,128)} %get-tuple-element.69) | copy-start | bytes 4718596
  295.6 46.8 %copy-start.14 = (bf16[3,4,32,1024]{3,2,1,0:T(8,128)(2,1)S(1)}, bf16[3,4,32,1024]{3,2,1,0:T(8,128)(2,1)}, u32[]{:S(2)}) copy-start(bf16[3,4,32,1024]{3,2,1,0:T(8,128)(2,1)} %get-tuple-element.58) | copy-start | bytes 2359300
  295.6 54.1 %slice-start = ((s8[6291456]{0:T(1024)(128)(4,1)}), s8[2097152]{0:T(1024)(128)(4,1)S(1)}, s32[]{:S(2)}) async-start(s8[6291456]{0:T(1024)(128)(4,1)} %bitcast.166), calls=%async_computation.3 | async-start | bytes 4194304
  342.4 7.4 %slice-start.1 = ((s8[6291456]{0:T(1024)(128)(4,1)}), s8[4194304]{0:T(1024)(128)(4,1)S(1)}, s32[]{:S(2)}) async-start(s8[6291456]{0:T(1024)(128)(4,1)} %bitcast.166), calls=%async_computation.4 | async-start | bytes 8388608
  342.4 7.4 %copy-start.2 = (bf16[2,1536,384]{2,1,0:T(8,128)(2,1)S(1)}, bf16[2,1536,384]{2,1,0:T(8,128)(2,1)}, u32[]{:S(2)}) copy-start(bf16[2,1536,384]{2,1,0:T(8,128)(2,1)} %shard_map.284) | copy-start | bytes 7077892
  402.6 4.5 copy-start.1
  402.6 4.5 copy-start.5
  449.4 43.4 %copy-start.21 = (f32[32,8,192]{2,1,0:T(8,128)S(1)}, f32[32,8,192]{2,1,0:T(8,128)}, u32[]{:S(2)}) copy-start(f32[32,8,192]{2,1,0:T(8,128)} %get-tuple-element.77) | copy-start | bytes 589828
  449.4 43.4 %copy-start.6 = (bf16[1024,192]{1,0:T(8,128)(2,1)S(1)}, bf16[1024,192]{1,0:T(8,128)(2,1)}, u32[]{:S(2)}) copy-start(bf16[1024,192]{1,0:T(8,128)(2,1)} %copy.98) | copy-start | bytes 1179652
  494.1 46.1 %copy-start.4 = (f32[384,1024]{1,0:T(8,128)S(1)}, f32[384,1024]{1,0:T(8,128)}, u32[]{:S(2)}) copy-start(f32[384,1024]{1,0:T(8,128)} %get-tuple-element.65) | copy-start | bytes 4718596
  555.2 49.5 %copy-start.15 = (bf16[4,3,32,1024]{3,2,1,0:T(8,128)(2,1)S(1)}, bf16[4,3,32,1024]{3,2,1,0:T(8,128)(2,1)}, u32[]{:S(2)}) copy-start(bf16[4,3,32,1024]{3,2,1,0:T(8,128)(2,1)} %get-tuple-element.83) | copy-start | bytes 2359300
  601.3 4.3 copy-start.13
  (26 other events, 67.7 us)
Sparse Core Ops, SparseCore 0:
  66.4 100.2 all-gather.1
  402.8 178.2 reduce-scatter.1

commit v3 on v2

--- a/solution.py
+++ b/solution.py
@@ -90,9 +90,13 @@
 
 
 class Task:
-    def __init__(self, operands, outs, scratch, body, everyone=False):
+    def __init__(
+        self, operands, outs, scratch, body, everyone=False, in_specs=None, out_specs=None
+    ):
         self.operands, self.outs, self.scratch = list(operands), list(outs), list(scratch)
         self.body, self.everyone = body, everyone
+        self.in_specs = in_specs or [ANY] * len(self.operands)
+        self.out_specs = out_specs or [ANY] * len(self.outs)
 
 
 def transfer_kernel(bodies, sizes, everyone, nb, n, *refs):
@@ -140,8 +144,8 @@
             n,
         ),
         out_shape=outs,
-        in_specs=[ANY] * len(operands),
-        out_specs=[ANY] * len(outs),
+        in_specs=[x for task in tasks for x in task.in_specs],
+        out_specs=[x for task in tasks for x in task.out_specs],
         scratch_shapes=[x for task in tasks for x in task.scratch],
         compiler_params=params(cid),
     )(*operands)
@@ -459,6 +463,213 @@
     )
 
 
+def quad_stages(s, x, mine, first, out, one, got_one, two, got_two, sems, add, total):
+    send, recv, local = sems
+    core, chip = lax.rem(s, 2), s // 2
+    sibling = s + 1 - 2 * core
+    flip_x = chip + 1 - 2 * lax.rem(chip, 2)
+    flip_y = lax.rem(chip + 2, 4)
+    places = [flip_x, flip_y, lax.rem(flip_x + 2, 4), chip]
+    sent, own = {}, {}
+    for k in (2, 0, 1, 3):
+        copy = remote(
+            out(x, 2 * places[k] + 1 - core), first.at[k], send.at[k], recv.at[k], seq=sibling
+        )
+        copy.start()
+        sent[k] = copy
+        copy = pltpu.make_async_copy(out(x, 2 * places[k] + core), mine.at[k], local.at[k])
+        copy.start()
+        own[k] = copy
+    yield
+    across = (2 * flip_x + core, 2 * flip_y + core)
+    stage = {}
+    waited = set()
+
+    def ready(k):
+        if k not in waited:
+            waited.add(k)
+            sent[k].wait_recv()
+            own[k].wait()
+
+    for half, i, k in ((0, 1, 2), (1, 1, 2), (0, 0, 0), (1, 0, 1)):
+        ready(k)
+        add(one.at[half, i], half, [mine.at[k], first.at[k]], [])
+        q = 4 + 2 * half + i
+        copy = remote(
+            one.at[half, i], got_one.at[half, i], send.at[q], recv.at[q], seq=across[half]
+        )
+        copy.start()
+        stage[half, i] = copy
+    yield
+    for half in (0, 1):
+        k = 1 - half
+        ready(k)
+        stage[half, 1].wait_recv()
+        add(two.at[half], half, [mine.at[k], first.at[k]], [got_one.at[half, 1]])
+        q = 8 + half
+        copy = remote(two.at[half], got_two.at[half], send.at[q], recv.at[q], seq=across[1 - half])
+        copy.start()
+        stage[half, 2] = copy
+    yield
+    ready(3)
+    for half in (0, 1):
+        stage[half, 0].wait_recv()
+        stage[half, 2].wait_recv()
+        total(half, [mine.at[3], first.at[3]], [got_one.at[half, 0], got_two.at[half]])
+    for copy in list(sent.values()) + list(stage.values()):
+        copy.wait_send()
+
+
+def quad_scratch(block, half):
+    return [
+        pltpu.VMEM((4,) + block, BF16),
+        pltpu.VMEM((4,) + block, BF16),
+        pltpu.VMEM((2, 2) + half, BF16),
+        pltpu.VMEM((2, 2) + half, BF16),
+        pltpu.VMEM((2,) + half, BF16),
+        pltpu.VMEM((2,) + half, BF16),
+        DMA((10,)),
+        DMA((10,)),
+        DMA((4,)),
+    ]
+
+
+def quad_sum_task(x):
+    rows, _, frames, width = x.shape
+    half_len = frames // 2
+    step = 16
+
+    def body(ins, outs, scratch, b, s, nb, n):
+        mine, first, one, got_one, two, got_two, send, recv, local, total, out_sem = scratch
+
+        def each(work):
+            def move(i, carry):
+                at = pl.multiple_of(i * step, step)
+                for r in range(rows):
+                    work(r, at)
+                return carry
+
+            lax.fori_loop(0, half_len // step, move, 0)
+
+        def value(half, whole_refs, half_refs, r, at):
+            parts = [ref[r, pl.ds(half * half_len + at, step), :] for ref in whole_refs]
+            parts += [ref[r, pl.ds(at, step), :] for ref in half_refs]
+            result = parts[0].astype(F32)
+            for p in parts[1:]:
+                result = result + p.astype(F32)
+            return result
+
+        def add(target, half, whole_refs, half_refs):
+            def work(r, at):
+                target[r, pl.ds(at, step), :] = value(half, whole_refs, half_refs, r, at).astype(BF16)
+
+            each(work)
+
+        def finish(half, whole_refs, half_refs):
+            def work(r, at):
+                total[r, pl.ds(half * half_len + at, step), :] = value(
+                    half, whole_refs, half_refs, r, at
+                )
+
+            each(work)
+
+        yield from quad_stages(
+            s,
+            ins[0],
+            mine,
+            first,
+            lambda ref, i: ref.at[:, i],
+            one,
+            got_one,
+            two,
+            got_two,
+            (send, recv, local),
+            add,
+            finish,
+        )
+        out = pltpu.make_async_copy(total, outs[0], out_sem)
+        out.start()
+        out.wait()
+
+    return Task(
+        [x],
+        [like(x, (rows, frames, width), F32)],
+        quad_scratch((rows, frames, width), (rows, half_len, width))
+        + [pltpu.VMEM((rows, frames, width), F32), DMA],
+        body,
+    )
+
+
+def quad_scatter_task(x):
+    nb, n = dims()
+    block = (nb,) + x.shape[2:]
+
+    def body(ins, outs, scratch, b, s, nb, n):
+        mine, first, one, got_one, two, got_two, send, recv, local = scratch[:9]
+        total, z_send, z_recv, z_local = scratch[9:]
+        o = outs[0]
+
+        def value(half, whole_refs, half_refs, i):
+            parts = [ref[half * (nb // 2) + i] for ref in whole_refs]
+            parts += [ref[i] for ref in half_refs]
+            result = parts[0].astype(F32)
+            for p in parts[1:]:
+                result = result + p.astype(F32)
+            return result.astype(BF16)
+
+        def add(target, half, whole_refs, half_refs):
+            def work(i, carry):
+                target[i] = value(half, whole_refs, half_refs, i)
+                return carry
+
+            lax.fori_loop(0, nb // 2, work, 0)
+
+        def finish(half, whole_refs, half_refs):
+            def work(i, carry):
+                total[half * (nb // 2) + i] = value(half, whole_refs, half_refs, i)
+                return carry
+
+            lax.fori_loop(0, nb // 2, work, 0)
+
+        yield from quad_stages(
+            s,
+            ins[0],
+            mine,
+            first,
+            lambda ref, i: ref.at[:, i],
+            one,
+            got_one,
+            two,
+            got_two,
+            (send, recv, local),
+            add,
+            finish,
+        )
+        last = []
+        for d in range(1, nb):
+            plane = lax.rem(b + d, nb)
+            copy = remote(
+                total.at[plane], o.at[b], z_send.at[d], z_recv.at[d], batch=plane, seq=s
+            )
+            copy.start()
+            last.append(copy)
+        copy = pltpu.make_async_copy(total.at[b], o.at[b], z_local)
+        copy.start()
+        last.append(copy)
+        yield
+        for copy in last:
+            copy.wait()
+
+    return Task(
+        [x],
+        [like(x, block)],
+        quad_scratch(block, (nb // 2,) + x.shape[2:])
+        + [pltpu.VMEM(block, BF16), DMA((nb,)), DMA((nb,)), DMA],
+        body,
+        True,
+    )
+
+
 def spread_task(x):
     nb, n = dims()
     chips = n // 2
@@ -533,7 +744,7 @@
     )
 
 
-def columns_out_task(x):
+def columns_out_task(x, late=False):
     nb, n = dims()
     ndev = nb * n
     kinds = x.shape[0]
@@ -547,6 +758,8 @@
             piece = kinds * me + j
             column = lax.rem(piece, ndev)
             pieces.append((j, piece // ndev, column // nb, lax.rem(column, nb)))
+        if late:
+            yield
         sent = []
         for j, part, block, slot in pieces:
             source, target, arrived = x.at[j], o.at[part, slot], recv.at[part, slot]
@@ -1293,20 +1506,19 @@
     cotangent,
     block_out,
     grad_att,
-    late_grads,
     grad_middle,
     sums,
+    normed,
+    low,
+    grad_up,
+    grad_feed,
+    grad_branch,
     branch,
     middle,
     scale,
-    normed,
     bend,
-    low,
-    grad_up,
     feed,
-    grad_feed,
     grad_normed,
-    grad_branch,
 ):
     tokens = rows * frames
     wide = 256
@@ -1403,55 +1615,338 @@
     for j in range(D // wide):
         lanes = slice(j * wide, (j + 1) * wide)
         grad_att[:, lanes] = times(grad_branch[...], inner(0, part, lanes)).astype(BF16)
-        late_grads[j * per : (j + 1) * per, 0:part, :] = (
+
+
+def feed_both(att, embedded, late, ids, mod, cotangent, rows, frames, part):
+    tokens = rows * frames
+    vmem = pl.BlockSpec(memory_space=pltpu.VMEM)
+
+    def scratch(width):
+        return pltpu.VMEM((tokens, width), F32)
+
+    def out(width, dtype=BF16):
+        return jax.ShapeDtypeStruct((tokens, width), dtype)
+
+    return pl.pallas_call(
+        functools.partial(feed_kernel, rows, frames, part),
+        in_specs=[vmem] * 6,
+        out_specs=[vmem] * 9,
+        out_shape=[
+            out(D),
+            out(D),
+            out(D, F32),
+            jax.ShapeDtypeStruct((rows, 2, 4, 8, D), F32),
+            out(D),
+            out(2 * D),
+            out(2 * D),
+            out(D),
+            out(D),
+        ],
+        scratch_shapes=[
+            scratch(D),
+            scratch(D),
+            scratch(128),
+            scratch(2 * D),
+            scratch(D),
+            scratch(D),
+        ],
+        compiler_params=params(),
+    )(att, embedded, late, ids, mod, cotangent)
+
+
+def lane_block(b, s, n, width):
+    return pl.ds(pl.multiple_of(block_of(b, s, n) * width, 128), width)
+
+
+def seat_rows(s, frames, first, count):
+    return pl.ds(pl.multiple_of(s * frames + first, 16), count)
+
+
+def norm_gather_task(bump_c, hidden, ids, mod, rows, frames):
+    n = dims()[1]
+    width = D // n
+    half = frames // 2
+
+    def body(ins, outs, scratch, b, s, nb, n):
+        bump_in, hidden, ids, mod = ins
+        embedded, o = outs
+        bump, normed, send, recv, local, g_send, g_recv, g_local = scratch
+        core, chip = lax.rem(s, 2), s // 2
+        sibling = s + 1 - 2 * core
+        flip_x = chip + 1 - 2 * lax.rem(chip, 2)
+        flip_y = lax.rem(chip + 2, 4)
+        seat_x, seat_y = 2 * flip_x + core, 2 * flip_y + core
+        diagonal = 2 * lax.rem(flip_x + 2, 4) + core
+        lanes = lane_block(b, s, n, width)
+        swaps = {}
+        for r in range(rows):
+            for d in range(1, n):
+                t = lax.rem(s + d, n)
+                copy = remote(
+                    bump_in.at[r, seat_rows(t, frames, 0, frames), :],
+                    bump.at[r, :, lanes],
+                    send.at[r, d],
+                    recv.at[r, d],
+                    seq=t,
+                )
+                copy.start()
+                swaps[r, d] = copy
+            copy = pltpu.make_async_copy(
+                bump_in.at[r, seat_rows(s, frames, 0, frames), :], bump.at[r, :, lanes], local.at[r]
+            )
+            copy.start()
+            swaps[r, 0] = copy
+        yield
+        parts = (pl.ds(0, half), pl.ds(half, half))
+        pushes, near, far = {}, [], []
+
+        def push(r, i, piece, source, target, fresh=False):
+            where = o.at[r, source, parts[piece]]
+            copy = remote(
+                normed.at[r, parts[piece]] if fresh else where,
+                where,
+                g_send.at[r, i],
+                g_recv.at[r, i],
+                seq=target,
+            )
+            copy.start()
+            return copy
+
+        for r in range(rows):
+            swaps[r, 0].wait()
+            for d in range(1, n):
+                swaps[r, d].wait_recv()
+
+            def step(i, carry, r=r):
+                inside = pl.ds(pl.multiple_of(i * STEP, STEP), STEP)
+                at = pl.ds(pl.multiple_of(r * frames + i * STEP, STEP), STEP)
+                value = hidden[at, :] + bump[r, inside, :].astype(F32)
+                embedded[at, :] = value
+                centre = value - jnp.mean(value, axis=1, keepdims=True)
+                hat = centre * lax.rsqrt(
+                    jnp.mean(centre * centre, axis=1, keepdims=True) + EPSILON
+                )
+                scale = pick(ids[at, :], mod[r, 1], STEP)
+                shift = pick(ids[at, :], mod[r, 0], STEP)
+                normed[r, inside, :] = (hat * (1.0 + scale) + shift).astype(BF16)
+                return carry
+
+            lax.fori_loop(0, frames // STEP, step, 0)
+            pushes[r, "x0"] = push(r, 0, 0, s, seat_x, True)
+            pushes[r, "y1"] = push(r, 1, 1, s, seat_y, True)
+            pushes[r, "x1"] = push(r, 2, 1, s, seat_x, True)
+            pushes[r, "y0"] = push(r, 3, 0, s, seat_y, True)
+            near += [push(r, 4, 0, s, sibling, True), push(r, 5, 1, s, sibling, True)]
+            copy = pltpu.make_async_copy(normed.at[r], o.at[r, s], g_local.at[r])
+            copy.start()
+            pushes[r, "own"] = copy
+            yield
+        for r in range(rows):
+            pushes[r, "x0"].wait_recv()
+            far.append(push(r, 6, 0, seat_x, seat_y))
+            near.append(push(r, 7, 0, seat_x, sibling))
+            pushes[r, "y1"].wait_recv()
+            far.append(push(r, 8, 1, seat_y, seat_x))
+            near.append(push(r, 9, 1, seat_y, sibling))
+            pushes[r, "x1"].wait_recv()
+            near.append(push(r, 10, 1, seat_x, sibling))
+            pushes[r, "y0"].wait_recv()
+            near.append(push(r, 11, 0, seat_y, sibling))
+        for r in range(rows):
+            far[2 * r].wait_recv()
+            near.append(push(r, 12, 0, diagonal, sibling))
+            far[2 * r + 1].wait_recv()
+            near.append(push(r, 13, 1, diagonal, sibling))
+        yield
+        for r in range(rows):
+            pushes[r, "own"].wait()
+            for d in range(1, n):
+                swaps[r, d].wait_send()
+            for name in ("x0", "x1", "y0", "y1"):
+                pushes[r, name].wait_send()
+        for copy in far:
+            copy.wait_send()
+        for copy in near:
+            copy.wait()
+
+    vmem = pl.BlockSpec(memory_space=pltpu.VMEM)
+    tokens = rows * frames
+    return Task(
+        [bump_c, hidden, ids, mod],
+        [
+            jax.ShapeDtypeStruct((tokens, D), F32),
+            jax.ShapeDtypeStruct((rows, n, frames, D), BF16),
+        ],
+        [
+            pltpu.VMEM((rows, frames, D), BF16),
+            pltpu.VMEM((rows, frames, D), BF16),
+            DMA((rows, n)),
+            DMA((rows, n)),
+            DMA((rows,)),
+            DMA((rows, 14)),
+            DMA((rows, 14)),
+            DMA((rows,)),
+        ],
+        body,
+        in_specs=[ANY, vmem, vmem, vmem],
+        out_specs=[vmem, ANY],
+    )
+
+
+def fold_rows(piece):
+    total = piece[0:8]
+    for q in range(1, piece.shape[0] // 8):
+        total = total + piece[8 * q : 8 * q + 8]
+    return total
+
+
+def sum_norm_task(partial, embedded, grad_middle, ids, mod, rows, frames):
+    n = dims()[1]
+    width = D // n
+    half_len = frames // 2
+    step = 16
+
+    def body(ins, outs, scratch, b, s, nb, n):
+        x, embedded, middle, ids, mod = ins
+        grad, o, sums = outs
+        mine, first, one, got_one, two, got_two, send, recv, local, low, c_send, c_recv, c_local = scratch
+        copies = []
+        sums[...] = jnp.zeros_like(sums)
+
+        def value(half, whole_refs, half_refs, r, at):
+            parts = [ref[r, pl.ds(half * half_len + at, step), :] for ref in whole_refs]
+            parts += [ref[r, pl.ds(at, step), :] for ref in half_refs]
+            result = parts[0].astype(F32)
+            for p in parts[1:]:
+                result = result + p.astype(F32)
+            return result
+
+        def each(work):
+            def move(i, carry):
+                at = pl.multiple_of(i * step, step)
+                for r in range(rows):
+                    work(r, at)
+                return carry
+
+            lax.fori_loop(0, half_len // step, move, 0)
+
+        def add(target, half, whole_refs, half_refs):
+            def work(r, at):
+                target[r, pl.ds(at, step), :] = value(half, whole_refs, half_refs, r, at).astype(BF16)
+
+            each(work)
+
+        def finish(half, whole_refs, half_refs):
+            def work(r, at):
+                down = value(half, whole_refs, half_refs, r, at)
+                where = pl.ds(pl.multiple_of(r * frames + half * half_len + at, step), step)
+                field = embedded[where, :]
+                centre = field - jnp.mean(field, axis=1, keepdims=True)
+                factor = lax.rsqrt(jnp.mean(centre * centre, axis=1, keepdims=True) + EPSILON)
+                hat = centre * factor
+                e = down * (1.0 + pick(ids[where, :], mod[r, 1], step))
+                result = middle[where, :] + factor * (
+                    e
+                    - jnp.mean(e, axis=1, keepdims=True)
+                    - hat * jnp.mean(e * hat, axis=1, keepdims=True)
+                )
+                grad[where, :] = result
+                low[r, pl.ds(half * half_len + at, step), :] = result.astype(BF16)
+                begin = ids[where, :] == ids[r * frames : r * frames + 1, :]
+                for k, part_sum in enumerate((down, down * hat)):
+                    kept = jnp.where(begin, part_sum, 0.0)
+                    sums[r, 0, k] = sums[r, 0, k] + fold_rows(kept)
+                    sums[r, 1, k] = sums[r, 1, k] + fold_rows(part_sum - kept)
+
+            each(work)
+            rows_at = pl.ds(half * half_len, half_len)
+            target = o.at[:, seat_rows(s, frames, half * half_len, half_len), :]
+            for d in range(1, n):
+                t = lax.rem(s + d, n)
+                copy = remote(
+                    low.at[:, rows_at, lane_block(b, t, n, width)],
+                    target,
+                    c_send.at[half, d],
+                    c_recv.at[half, d],
+                    seq=t,
+                )
+                copy.start()
+                copies.append(copy)
+            copy = pltpu.make_async_copy(
+                low.at[:, rows_at, lane_block(b, s, n, width)], target, c_local.at[half]
+            )
+            copy.start()
+            copies.append(copy)
+
+        yield from quad_stages(
+            s,
+            x,
+            mine,
+            first,
+            lambda ref, i: ref.at[:, i],
+            one,
+            got_one,
+            two,
+            got_two,
+            (send, recv, local),
+            add,
+            finish,
+        )
+        for copy in copies:
+            copy.wait()
+
+    vmem = pl.BlockSpec(memory_space=pltpu.VMEM)
+    tokens = rows * frames
+    return Task(
+        [partial, embedded, grad_middle, ids, mod],
+        [
+            jax.ShapeDtypeStruct((tokens, D), F32),
+            jax.ShapeDtypeStruct((rows, n * frames, width), BF16),
+            jax.ShapeDtypeStruct((rows, 2, 2, 8, D), F32),
+        ],
+        quad_scratch((rows, frames, D), (rows, half_len, D))
+        + [pltpu.VMEM((rows, frames, D), BF16), DMA((2, n)), DMA((2, n)), DMA((2,))],
+        body,
+        in_specs=[ANY] + [vmem] * 4,
+        out_specs=[vmem, ANY, vmem],
+    )
+
+
+def late_grads_task(att, grad_branch, grad_feed, low, grad_up, normed, ndev, part):
+    def body(ins, outs, scratch, b, s, nb, n):
+        yield
+        late_work(*ins, outs[0], part)
+
+    vmem = pl.BlockSpec(memory_space=pltpu.VMEM)
+    return Task(
+        [att, grad_branch, grad_feed, low, grad_up, normed],
+        [jax.ShapeDtypeStruct((ndev, 5 * part, D), BF16)],
+        [],
+        body,
+        in_specs=[vmem] * 6,
+        out_specs=[vmem],
+    )
+
+
+def late_work(att, grad_branch, grad_feed, low, grad_up, normed, out, part):
+    wide = 256
+    per = wide // part
+    for j in range(D // wide):
+        lanes = slice(j * wide, (j + 1) * wide)
+        out[j * per : (j + 1) * per, 0:part, :] = (
             rows_sum(grad_branch[:, lanes], att[...]).astype(BF16).reshape(per, part, D)
         )
         for half in range(2):
-            late_grads[j * per : (j + 1) * per, (3 + half) * part : (4 + half) * part, :] = (
+            out[j * per : (j + 1) * per, (3 + half) * part : (4 + half) * part, :] = (
                 rows_sum(grad_feed[:, lanes], low[:, half * D : (half + 1) * D])
                 .astype(BF16)
                 .reshape(per, part, D)
             )
     for j in range(2 * D // wide):
         lanes = slice(j * wide, (j + 1) * wide)
-        late_grads[j * per // 2 : (j + 1) * per // 2, part : 3 * part, :] = (
+        out[j * per // 2 : (j + 1) * per // 2, part : 3 * part, :] = (
             rows_sum(grad_up[:, lanes], normed[...]).astype(BF16).reshape(per // 2, 2 * part, D)
         )
-
-
-def feed_both(att, embedded, late, ids, mod, cotangent, rows, frames, part):
-    tokens = rows * frames
-    vmem = pl.BlockSpec(memory_space=pltpu.VMEM)
-
-    def scratch(width, dtype):
-        return pltpu.VMEM((tokens, width), dtype)
-
-    return pl.pallas_call(
-        functools.partial(feed_kernel, rows, frames, part),
-        in_specs=[vmem] * 6,
-        out_specs=[vmem] * 5,
-        out_shape=[
-            jax.ShapeDtypeStruct((tokens, D), BF16),
-            jax.ShapeDtypeStruct((tokens, D), BF16),
-            jax.ShapeDtypeStruct(late.shape, BF16),
-            jax.ShapeDtypeStruct((tokens, D), F32),
-            jax.ShapeDtypeStruct((rows, 2, 4, 8, D), F32),
-        ],
-        scratch_shapes=[
-            scratch(D, F32),
-            scratch(D, F32),
-            scratch(128, F32),
-            scratch(D, BF16),
-            scratch(2 * D, F32),
-            scratch(2 * D, BF16),
-            scratch(2 * D, BF16),
-            scratch(D, F32),
-            scratch(D, BF16),
-            scratch(D, F32),
-            scratch(D, BF16),
-        ],
-        compiler_params=params(),
-    )(att, embedded, late, ids, mod, cotangent)
 
 
 def layer_norm(field):
@@ -1530,7 +2025,7 @@
             spread_task(text_table.T),
             spread_task(time_table.T),
             spread_task(time_index),
-            columns_out_task(jnp.concatenate([conv_first, conv_second], axis=2)[None]),
+            columns_out_task(jnp.concatenate([conv_first, conv_second], axis=2)[None], True),
         ],
         0,
     )
@@ -1567,18 +2062,30 @@
     )
     hidden_c = arrange(got)
     modulation = mod_got.transpose(1, 0, 2).reshape(rows, SEGS, 6, D)
+    mod_table = modulation.transpose(0, 2, 1, 3)
+    ids_column = own_ids.reshape(tokens, 1)
+    fused = n == 8 and width % 128 == 0
     shift_attn, scale_attn = (by_segment(own_ids, modulation[:, :, i]) for i in range(2))
 
     conv_one, conv_two, bump_c = conv_forward(hidden_c, seg_column, got_convs)
-    task, arrange = to_frames(bump_c)
-    bump = arrange(transfer([task], 3)[0])
-    embedded = hidden + bump.astype(F32)
-
-    normed = modulate(embedded, scale_attn, shift_attn).astype(BF16)
-    gather = quad_gather_task if n == 8 else gather_task
-    (normed_all,), (got_qkv,) = transfer(
-        [gather(normed), columns_out_task(qkv_proj.T.reshape(3, part, D))], 4
-    )
+    qkv_task = columns_out_task(qkv_proj.T.reshape(3, part, D))
+    if fused:
+        (embedded, normed_all), (got_qkv,) = transfer(
+            [
+                norm_gather_task(
+                    bump_c, hidden.reshape(tokens, D), ids_column, mod_table, rows, frames
+                ),
+                qkv_task,
+            ],
+            3,
+        )
+        embedded = embedded.reshape(rows, frames, D)
+    else:
+        task, arrange = to_frames(bump_c)
+        bump = arrange(transfer([task], 3)[0])
+        embedded = hidden + bump.astype(F32)
+        normed = modulate(embedded, scale_attn, shift_attn).astype(BF16)
+        (normed_all,), (got_qkv,) = transfer([gather_task(normed), qkv_task], 4)
     normed_all = normed_all.reshape(rows, length, D)
     qkv_t = got_qkv.reshape(3 * width, D)
     cos, sin = rope_tables(segment_ids, starts, width)
@@ -1590,16 +2097,29 @@
     attended_own = arrange(transfer([task], 5)[0])
     attended_own = attended_own.reshape(tokens, D)
 
-    block_out, grad_att, late_grads, grad_middle, feed_sums = feed_both(
+    (
+        block_out,
+        grad_att,
+        grad_middle,
+        feed_sums,
+        normed_feed,
+        gelu_low,
+        grad_up,
+        grad_feed,
+        grad_branch,
+    ) = feed_both(
         attended_own,
         embedded.reshape(tokens, D),
         late,
-        own_ids.reshape(tokens, 1),
-        modulation.transpose(0, 2, 1, 3),
+        ids_column,
+        mod_table,
         grad_out.reshape(tokens, D),
         rows,
         frames,
         part,
+    )
+    late_task = late_grads_task(
+        attended_own, grad_branch, grad_feed, gelu_low, grad_up, normed_feed, ndev, part
     )
     block_out = block_out.reshape(rows, frames, D)
     grad_att = grad_att.reshape(rows, frames, D)
@@ -1639,25 +2159,51 @@
     ).reshape(rows * length, 3 * width)
     grad_qkv = rows_sum(grad_projected, normed_all.reshape(rows * length, D)).astype(BF16)
     partial = times(grad_projected, qkv_t).astype(BF16).reshape(rows, n, frames, D)
-    (grad_normed,), (got_qkv_grads,) = transfer(
-        [sum_task(partial), columns_back_task(grad_qkv.reshape(3, nb, part, D))], 7
-    )
-    late_grads, grad_normed = lax.optimization_barrier((late_grads, grad_normed))
+    qkv_back = columns_back_task(grad_qkv.reshape(3, nb, part, D))
+    if fused:
+        (grad_embedded, grad_emb_c, attn_sums), (got_qkv_grads,), (late_grads,) = transfer(
+            [
+                sum_norm_task(
+                    partial,
+                    embedded.reshape(tokens, D),
+                    grad_middle.reshape(tokens, D),
+                    ids_column,
+                    mod_table,
+                    rows,
+                    frames,
+                ),
+                qkv_back,
+                late_task,
+            ],
+            7,
+        )
+        grad_embedded = grad_embedded.reshape(rows, frames, D)
+        attn_sums = jnp.sum(attn_sums, axis=3)
+        attn_sums = [attn_sums[:, :, 0], attn_sums[:, :, 1]]
+    else:
+        (grad_normed,), (got_qkv_grads,), (late_grads,) = transfer(
+            [sum_task(partial), qkv_back, late_task], 7
+        )
+        grad_emb_part, grad_scale_attn, grad_shift_attn = jax.vjp(
+            modulate, embedded, scale_attn, shift_attn
+        )[1](grad_normed)
+        grad_embedded = grad_middle + grad_emb_part
+        task, arrange = to_channels(grad_embedded.astype(BF16))
+        grad_emb_c = arrange(transfer([task], 10)[0])
     late_sum = lax.psum_scatter(
         late_grads, ("batch", "seq"), scatter_dimension=0, tiled=False
     ).astype(F32)
 
-    grad_emb_part, grad_scale_attn, grad_shift_attn = jax.vjp(
-        modulate, embedded, scale_attn, shift_attn
-    )[1](grad_normed)
-    grad_embedded = grad_middle + grad_emb_part
-
     first_ids, last_ids = own_ids[:, 0], own_ids[:, -1]
-    first = (own_ids == first_ids[:, None])[:, :, None]
-    attn_sums = [
-        jnp.stack([jnp.sum(jnp.where(first, g, 0.0), axis=1), jnp.sum(jnp.where(first, 0.0, g), axis=1)], axis=1)
-        for g in (grad_shift_attn, grad_scale_attn)
-    ]
+    if not fused:
+        first = (own_ids == first_ids[:, None])[:, :, None]
+        attn_sums = [
+            jnp.stack(
+                [jnp.sum(jnp.where(first, g, 0.0), axis=1), jnp.sum(jnp.where(first, 0.0, g), axis=1)],
+                axis=1,
+            )
+            for g in (grad_shift_attn, grad_scale_attn)
+        ]
     feed_sums = jnp.sum(feed_sums, axis=3)
     sides = jnp.concatenate(
         [attn_sums[0], attn_sums[1]] + [feed_sums[:, :, i] for i in range(4)], axis=2
@@ -1667,26 +2213,19 @@
     local_sums = is_first[:, :, None] * sides[:, :1] + is_last[:, :, None] * sides[:, 1:]
     slots = rows * SEGS
     sums_out = local_sums.reshape(slots, ndev, 6 * part).transpose(1, 0, 2)
-    task, arrange = to_channels(grad_embedded.astype(BF16))
-    got, (sums_got,) = transfer([task, spray_task(sums_out, False)], 10)
-    grad_emb_c = arrange(got)
+    grad_hidden_c, conv_sums = conv_backward(
+        grad_emb_c, hidden_c, seg_column, conv_one, conv_two, got_convs, nb
+    )
+    task, arrange = to_frames(grad_hidden_c)
+    got, (sums_got,), (got_conv_grads,) = transfer(
+        [task, spray_task(sums_out, False), columns_back_task(conv_sums)], 11
+    )
+    grad_hidden_conv = arrange(got)
     sums_got = sums_got.reshape(nb, n, slots, 6 * part)
     grad_mod = jnp.sum(sums_got, axis=1).astype(BF16).reshape(nb * slots, 6 * part)
     grad_adaln = rows_sum(soft_cond, grad_mod)
     soft_part = times_t(grad_mod, adaln_proj)
     soft_out = soft_part.reshape(nb * slots, ndev, part).transpose(1, 0, 2)
-    grad_hidden_c, conv_sums = conv_backward(
-        grad_emb_c, hidden_c, seg_column, conv_one, conv_two, got_convs, nb
-    )
-    task, arrange = to_frames(grad_hidden_c)
-    got, (soft_got,), (got_conv_grads,) = transfer(
-        [task, spray_task(soft_out, False), columns_back_task(conv_sums)], 11
-    )
-    grad_hidden_conv = arrange(got)
-    grad_soft = jnp.sum(soft_got, axis=0)
-    own_cond = times(step_hot, time_table)
-    grad_cond = jax.vjp(jax.nn.silu, own_cond)[1](grad_soft)[0]
-    grad_time = jnp.dot(step_hot.astype(F32).T, grad_cond, precision=EXACT)
     grad_convs = jnp.sum(got_conv_grads.astype(F32), axis=0)[0]
     grad_first, grad_second = grad_convs[..., :CHAN], grad_convs[..., CHAN:]
     grad_qkv_own = jnp.sum(got_qkv_grads.astype(F32), axis=0).reshape(3 * part, D).T
@@ -1697,13 +2236,19 @@
     grad_mels = grad_joined[:, : 2 * MEL].reshape(rows, frames, 2 * MEL)
     grad_embed = grad_joined[:, 2 * MEL :].astype(BF16)
     grad_text = rows_sum(grad_embed, text_hot).astype(BF16)
-    (in_sum,), (text_sum,) = transfer(
+    scatter = quad_scatter_task if n == 8 and nb % 2 == 0 else scatter_task
+    (in_sum,), (text_sum,), (soft_got,) = transfer(
         [
-            scatter_task(grad_input.reshape(nb, n, part, -1)),
-            scatter_task(grad_text.reshape(nb, n, -1, VOCAB)),
+            scatter(grad_input.reshape(nb, n, part, -1)),
+            scatter(grad_text.reshape(nb, n, -1, VOCAB)),
+            spray_task(soft_out, False),
         ],
         13,
     )
+    grad_soft = jnp.sum(soft_got, axis=0)
+    own_cond = times(step_hot, time_table)
+    grad_cond = jax.vjp(jax.nn.silu, own_cond)[1](grad_soft)[0]
+    grad_time = jnp.dot(step_hot.astype(F32).T, grad_cond, precision=EXACT)
     grad_input_own = jnp.sum(in_sum.astype(F32), axis=0).T
     grad_text_own = jnp.sum(text_sum.astype(F32), axis=0).T
     grad_down_own = jnp.concatenate([late_sum[3 * part : 4 * part], late_sum[4 * part :]], axis=1)

time: 626 us -> 594 us (0.949)
  other arithmetic: 37.6 us -> 22.1 us
  Pallas kernels: 512 us -> 497 us
    reduce_sum x4 -> x1, other arithmetic: 6.88 us -> 0.08 us  [on_device(): attn_sums = jnp.sum(attn_sums, axis=3)]
    pallas_call x1, Pallas kernels: 32.8 us -> 26 us  [feed_both(): pl.pallas_call(functools.partial(feed_kernel, rows, frames, part), in_spe...]
    pallas_call x10 -> x8, Pallas kernels: 332 us -> 329 us  [transfer(): pl.pallas_call(functools.partial(transfer_kernel, [t.body for t in tasks]...]
  transfers between devices with their start and end apart: 2 -> 2, of which waited for: 0 -> 1; matrix products, arithmetic and copies ran while one was open for 11% -> 8% of each run, Pallas kernels for 51% -> 52%
where the time goes in v3:
time: 594 us; the launch traced here: 583 us
  Pallas kernels  497 us (84%)
  matrix products  25.9 us (4%)
  other arithmetic  22.1 us (4%)
  local copies, waits for them, and re-layouts  21.5 us (4%)
  between operations  15.1 us (3%)
    pallas_call x8, Pallas kernels, transfer(): pl.pallas_call(functools.partial(transfer_kernel, [t.body for t in tasks]...  329 us
    pallas_call x1, Pallas kernels, conv_backward(): pl.pallas_call(functools.partial(conv_backward_kernel, count, length, gro...  43.5 us
    pallas_call x1, Pallas kernels, attention_backward(): pl.pallas_call(functools.partial(attention_backward_kernel, length, width...  43.2 us
    pallas_call x1, Pallas kernels, feed_both(): pl.pallas_call(functools.partial(feed_kernel, rows, frames, part), in_spe...  26 us
    pallas_call x1, Pallas kernels, conv_forward(): pl.pallas_call(functools.partial(conv_forward_kernel, count, length, grou...  23.7 us
    pallas_call x1, Pallas kernels, attention_forward(): pl.pallas_call(functools.partial(attention_forward_kernel, width), grid=(...  22.9 us
  transfers between devices with their start and end apart: 2, of which 1 were waited for; matrix products, arithmetic and copies ran while one was open for 8% of the time, Pallas kernels for 52%

profile of v3, /device:TPU:1, one launch (start us, length us, event | category | flops | bytes accessed | tf_op | source)
XLA Modules:
  0.0 583.0 jit_solution(13356970665714971665)
XLA Ops:
  7.3 1.4 copy.84
  9.5 1.9 maximum_bitcast_fusion.1.refs_4_
  11.4 1.7 pad_maximum_fusion.3
  13.1 48.6 %shard_map.274 = (bf16[4,8,32,712]{3,2,1,0:T(8,128)(2,1)}, bf16[4,8,16,2546]{3,2,1,0:T(8,128)(2,1)}, bf16[4,8,32,32]{3,2,1,0:T(8,128)(2,1)}, s32[4,8,2,4]{3,2,1,0:T(2,128)}, bf16[1,4,31,32,128]{4,3,2,1,0:T(8,128)(2,1)}) custom-call(bf16[32,712]{1,0:T(8,128)(2,1)} %bitcast.188, bf16[16,2546]{1,0:T(8,128)(2,1)} %bitcast.186, bf16[32,32]{1,0:T(8,128)(2,1)} %bitcast.189, ...), custom_call_target="tpu_custom_call" | custom-call | tf_op jit(solution)/shard_map/pallas_call | solution.py:137
  66.0 1.7 copy.85.seg.q_code.k_code
  68.9 3.1 fusion.3
  72.0 2.2 fusion.42
  74.2 21.1 %shard_map.275 = (bf16[2,1536,128]{2,1,0:T(8,128)(2,1)}, f32[32,8,192]{2,1,0:T(8,128)}) custom-call(bf16[2,192,1024]{2,1,0:T(8,128)(2,1)} %bitcast.159, f32[4,8,192]{2,1,0:T(8,128)} %convolution_bitcast_fusion.1.refs_1_), custom_call_target="tpu_custom_call" | custom-call | tf_op jit(solution)/shard_map/pallas_call | solution.py:137
  98.3 23.7 %shard_map.276 = (f32[2,2,400,256]{3,2,1,0:T(8,128)}, f32[2,2,400,256]{3,2,1,0:T(8,128)}, bf16[2,1536,128]{2,1,0:T(8,128)(2,1)}) custom-call(bf16[2,1536,128]{2,1,0:T(8,128)(2,1)} %get-tuple-element.58.u, s32[2,1536,1]{2,1,0:T(8,128)} %copy.85.seg.q_code.k_code, bf16[4,31,32,128]{3,2,1,0:T(8,128)(2,1)} %bitcast.153), custom_call_target="tpu_custom_call" | custom-call | tf_op jit(solution)/shard_map/pallas_call | solution.py:1146
  122.1 63.2 %shard_map.277 = (f32[384,1024]{1,0:T(8,128)}, bf16[2,8,192,1024]{3,2,1,0:T(8,128)(2,1)}, bf16[3,4,32,1024]{3,2,1,0:T(8,128)(2,1)}) custom-call(bf16[2,1536,128]{2,1,0:T(8,128)(2,1)} %get-tuple-element.60.refs_0_, f32[384,1024]{1,0:T(8,128)} %get-tuple-element.179.refs_1_, s32[384,1]{1,0:T(8,128)} %reshape.226.refs_2_.ids.refs_3_, ...), custom_call_target="tpu_custom_call" | custom-call | tf_op jit(solution)/shard_map/pallas_call | solution.py:137
  185.5 4.2 multiply_subtract_fusion
  189.6 9.5 %shard_map.278 = (bf16[2,1536,128]{2,1,0:T(8,128)(2,1)}, bf16[2,1536,128]{2,1,0:T(8,128)(2,1)}, bf16[2,1536,128]{2,1,0:T(8,128)(2,1)}) custom-call(bf16[2,1536,1024]{2,1,0:T(8,128)(2,1)} %bitcast.141, bf16[384,1024]{1,0:T(8,128)(2,1)} %bitcast.165, f32[2,1536,128]{2,1,0:T(8,128)} %get-tuple-element.149.cos, f32[2,1536,128]{2,1,0:T(8,128)} %get-tuple-element.148.sin), custom_call_target="tpu_custom_call" | custom-call | tf_op jit(solution)/shard_map/pallas_call | solution.py:1322
  199.1 22.9 %shard_map.279 = (f32[2,1536,128]{2,1,0:T(8,128)}, bf16[2,1536,128]{2,1,0:T(8,128)(2,1)}, f32[2,1536,128]{2,1,0:T(8,128)}) custom-call(bf16[2,1536,128]{2,1,0:T(8,128)(2,1)} %get-tuple-element.64.q, bf16[2,1536,128]{2,1,0:T(8,128)(2,1)} %get-tuple-element.65.k, bf16[2,1536,128]{2,1,0:T(8,128)(2,1)} %get-tuple-element.66.v, ...), custom_call_target="tpu_custom_call" | custom-call | tf_op jit(solution)/shard_map/pallas_call | solution.py:1366
  222.0 12.3 %shard_map.280 = bf16[2,192,1024]{2,1,0:T(8,128)(2,1)} custom-call(bf16[2,1536,128]{2,1,0:T(8,128)(2,1)} %get-tuple-element.67.refs_0_), custom_call_target="tpu_custom_call" | custom-call | tf_op jit(solution)/shard_map/pallas_call | solution.py:137
  237.5 26.0 %shard_map.281 = (bf16[384,1024]{1,0:T(8,128)(2,1)}, bf16[384,1024]{1,0:T(8,128)(2,1)}, f32[384,1024]{1,0:T(8,128)}, f32[2,2,4,8,1024]{4,3,2,1,0:T(8,128)}, bf16...) custom-call(bf16[384,1024]{1,0:T(8,128)(2,1)} %bitcast.149, ...), custom_call_target="tpu_custom_call" | custom-call | tf_op jit(solution)/shard_map/pallas_call | solution.py:1630
  263.6 12.1 %shard_map.282.g = bf16[2,1536,128]{2,1,0:T(8,128)(2,1)} custom-call(bf16[2,192,1024]{2,1,0:T(8,128)(2,1)} %bitcast.167), custom_call_target="tpu_custom_call" | custom-call | tf_op jit(solution)/shard_map/pallas_call | solution.py:137
  275.7 1.3 convert_multiply_fusion
  278.3 43.2 %shard_map.283 = bf16[2,1536,384]{2,1,0:T(8,128)(2,1)} custom-call(s32[2,6]{1,0:T(2,128)} %get-tuple-element.181.low_edge, s32[2,6]{1,0:T(2,128)} %get-tuple-element.180.high_edge, bf16[2,1536,128]{2,1,0:T(8,128)(2,1)} %get-tuple-element.64.q, bf16[2,1536,128]{2,1,0:T(8,128)(2,1)} %get-tuple-element.65.k, bf16[2,1536,128]{2,1,0:T(8,128)(2,1)} %get-tuple-element.66.v, ...), custom_call_target="tpu_custom_call" | custom-call | tf_op jit(solution)/shard_map/pallas_call | solution.py:1462
  321.5 7.4 %convolution_convert_fusion = bf16[3072,1024]{1,0:T(8,128)(2,1)} fusion(bf16[3072,384]{1,0:T(8,128)(2,1)} %bitcast.145, bf16[384,1024]{1,0:T(8,128)(2,1)S(1)} %bitcast.166), kind=kOutput, calls=%fused_computation | convolution fusion | flops 2419064832 | bytes 9437184 | tf_op jit(solution)/shard_map/dot_general | solution.py:959
  329.0 3.5 convolution_convert_fusion.3
  332.5 65.9 %shard_map.284 = (f32[384,1024]{1,0:T(8,128)}, bf16[2,1536,128]{2,1,0:T(8,128)(2,1)}, f32[2,2,2,8,1024]{4,3,2,1,0:T(8,128)}, bf16[4,3,32,1024]{3,2,1,0:T(8,128)(2,1)}, bf16[32,160,1024]{2,1,0:T(8,128)(2,1)}) custom-call(bf16[2,8,192,1024]{3,2,1,0:T(8,128)(2,1)} %bitcast.151, f32[384,1024]{1,0:T(8,128)} %get-tuple-element.68.embedded.refs_1_, ...), custom_call_target="tpu_custom_call" | custom-call | tf_op jit(solution)/shard_map/pallas_call | solution.py:137
  400.5 43.5 %shard_map.285 = (bf16[2,1536,128]{2,1,0:T(8,128)(2,1)}, bf16[1,4,31,32,128]{4,3,2,1,0:T(8,128)(2,1)}) custom-call(bf16[2,1536,128]{2,1,0:T(8,128)(2,1)} %get-tuple-element.81.d, bf16[2,1536,128]{2,1,0:T(8,128)(2,1)} %get-tuple-element.58.u, s32[2,1536,1]{2,1,0:T(8,128)} %copy.85.seg.q_code.k_code, f32[2,2,400,256]{3,2,1,0:T(8,128)} %get-tuple-element.82.c1, ...), custom_call_target="tpu_custom_call" | custom-call | tf_op jit(solution)/shard_map/pallas_call | solution.py:1266
  445.0 39.9 %shard_map.286 = (bf16[2,192,1024]{2,1,0:T(8,128)(2,1)}, f32[32,8,192]{2,1,0:T(8,128)}, bf16[4,1,31,32,128]{4,3,2,1,0:T(8,128)(2,1)}) custom-call(bf16[2,1536,128]{2,1,0:T(8,128)(2,1)} %get-tuple-element.84.refs_0_, f32[32,8,192]{2,1,0:T(8,128)} %fusion.6.refs_1_, bf16[1,4,31,32,128]{4,3,2,1,0:T(8,128)(2,1)} %get-tuple-element.87.refs_2_), custom_call_target="tpu_custom_call" | custom-call | tf_op jit(solution)/shard_map/pallas_call | solution.py:137
  485.0 1.5 add_convert_fusion
  487.7 1.6 convolution_convert_fusion.1
  489.3 2.9 copy.106
  492.2 2.4 convolution_convert_fusion.2
  494.6 1.6 copy.105
  496.3 1.3 convolution_bitcast_fusion.refs_2_
  497.6 65.5 %shard_map.287 = (bf16[4,32,712]{2,1,0:T(8,128)(2,1)}, bf16[4,16,2546]{2,1,0:T(8,128)(2,1)}, f32[32,32,32]{2,1,0:T(8,128)}) custom-call(bf16[4,8,32,712]{3,2,1,0:T(8,128)(2,1)} %bitcast.152, bf16[4,8,16,2546]{3,2,1,0:T(8,128)(2,1)} %bitcast.147, f32[32,32,32]{2,1,0:T(8,128)} %convolution_bitcast_fusion.refs_2_), custom_call_target="tpu_custom_call" | custom-call | tf_op jit(solution)/shard_map/pallas_call | solution.py:137
  563.1 1.3 reduce_sum.127
  565.3 1.6 convert_reduce_fusion.3
  (141 shorter events, 27.7 us)
Async XLA Ops:
  7.2 55.3 %copy-start.20 = (s32[2,1536]{1,0:T(2,128)S(1)}, s32[2,1536]{1,0:T(2,128)}, u32[]{:S(2)}) copy-start(s32[2,1536]{1,0:T(2,128)} %param.21) | copy-start | bytes 36868
  7.2 58.0 %copy-start.24 = (s32[2,192]{1,0:T(2,128)S(1)}, s32[2,192]{1,0:T(2,128)}, u32[]{:S(2)}) copy-start(s32[2,192]{1,0:T(2,128)} %param.20) | copy-start | bytes 4612
  7.2 58.2 %copy-start.22 = (s32[2,1536]{1,0:T(2,128)S(1)}, s32[2,1536]{1,0:T(2,128)}, u32[]{:S(2)}) copy-start(s32[2,1536]{1,0:T(2,128)} %param.22) | copy-start | bytes 36868
  7.2 230.3 %all-gather.2.cloned.1.call-start = ((), (), s32[]{:S(2)}) async-start(), calls=%async_computation.1 | async-start | bytes 10813440 | tf_op jit(solution)/shard_map/all_gather | solution.py:2034
  13.1 54.9 %copy-start.5 = (bf16[1024,192]{0,1:T(8,128)(2,1)S(1)}, bf16[1024,192]{0,1:T(8,128)(2,1)}, u32[]{:S(2)}) copy-start(bf16[1024,192]{0,1:T(8,128)(2,1)} %param.28) | copy-start | bytes 1179652
  61.7 6.0 %copy-start.30 = (bf16[4,8,32,32]{3,2,1,0:T(8,128)(2,1)S(1)}, bf16[4,8,32,32]{3,2,1,0:T(8,128)(2,1)}, u32[]{:S(2)}) copy-start(bf16[4,8,32,32]{3,2,1,0:T(8,128)(2,1)} %get-tuple-element.57) | copy-start | bytes 196612
  61.8 510.8 %reduce-scatter.2.cloned.1.call-start = ((), (), s32[]{:S(2)}) async-start(), calls=%async_computation.2 | async-start | bytes 10813440 | tf_op jit(solution)/shard_map/reduce_scatter | solution.py:2193
  65.3 6.6 %copy-start.25 = (s32[384]{0:T(512)}, s32[384]{0:T(512)S(1)}, u32[]{:S(2)}) copy-start(s32[384]{0:T(512)S(1)} %eq.111) | copy-start | bytes 4612
  65.4 6.6 %copy-start.27 = (s32[32]{0:T(128)}, s32[32]{0:T(128)S(1)}, u32[]{:S(2)}) copy-start(s32[32]{0:T(128)S(1)} %eq.115) | copy-start | bytes 388
  68.9 3.1 copy-start.1
  68.9 3.1 copy-start.21
  72.0 2.3 copy-start.14
  122.0 63.2 %copy-start.29 = (f32[128]{0:T(128)S(1)}, f32[128]{0:T(128)}, u32[]{:S(2)}) copy-start(f32[128]{0:T(128)} %constant.57.clone) | copy-start | bytes 1540
  122.0 63.4 %copy-start.11 = (f32[1536,128]{1,0:T(8,128)S(1)}, f32[1536,128]{1,0:T(8,128)}, u32[]{:S(2)}) copy-start(f32[1536,128]{1,0:T(8,128)} %constant.55.clone) | copy-start | bytes 2359300
  122.0 63.4 %copy-start.12 = (f32[1536,128]{1,0:T(8,128)S(1)}, f32[1536,128]{1,0:T(8,128)}, u32[]{:S(2)}) copy-start(f32[1536,128]{1,0:T(8,128)} %constant.56.clone) | copy-start | bytes 2359300
  222.0 12.3 %copy-start.4 = (f32[2,1536,128]{2,1,0:T(8,128)S(1)}, f32[2,1536,128]{2,1,0:T(8,128)}, u32[]{:S(2)}) copy-start(f32[2,1536,128]{2,1,0:T(8,128)} %get-tuple-element.72) | copy-start | bytes 4718596
  263.6 12.1 %copy-start.6 = (f32[2,1536,128]{2,1,0:T(8,128)S(1)}, f32[2,1536,128]{2,1,0:T(8,128)}, u32[]{:S(2)}) copy-start(f32[2,1536,128]{2,1,0:T(8,128)} %get-tuple-element.73) | copy-start | bytes 4718596
  278.3 43.3 %copy-start.8 = (bf16[3,4,32,1024]{3,2,1,0:T(8,128)(2,1)S(1)}, bf16[3,4,32,1024]{3,2,1,0:T(8,128)(2,1)}, u32[]{:S(2)}) copy-start(bf16[3,4,32,1024]{3,2,1,0:T(8,128)(2,1)} %get-tuple-element.63) | copy-start | bytes 2359300
  278.3 50.7 %slice-start = ((s8[6291456]{0:T(1024)(128)(4,1)}), s8[2097152]{0:T(1024)(128)(4,1)S(1)}, s32[]{:S(2)}) async-start(s8[6291456]{0:T(1024)(128)(4,1)} %bitcast.142), calls=%async_computation.3 | async-start | bytes 4194304
  321.5 7.4 %slice-start.1 = ((s8[6291456]{0:T(1024)(128)(4,1)}), s8[4194304]{0:T(1024)(128)(4,1)S(1)}, s32[]{:S(2)}) async-start(s8[6291456]{0:T(1024)(128)(4,1)} %bitcast.142), calls=%async_computation.4 | async-start | bytes 8388608
  321.5 7.4 %copy-start = (bf16[2,1536,384]{2,1,0:T(8,128)(2,1)S(1)}, bf16[2,1536,384]{2,1,0:T(8,128)(2,1)}, u32[]{:S(2)}) copy-start(bf16[2,1536,384]{2,1,0:T(8,128)(2,1)} %shard_map.283) | copy-start | bytes 7077892
  398.5 1.0 copy-start.16
  398.5 1.1 copy-start.13
  444.0 40.9 %copy-start.3 = (f32[384,1024]{1,0:T(8,128)S(1)}, f32[384,1024]{1,0:T(8,128)}, u32[]{:S(2)}) copy-start(f32[384,1024]{1,0:T(8,128)} %get-tuple-element.80) | copy-start | bytes 4718596
  485.0 1.7 copy-start.2
  486.5 1.1 copy-start.10
  486.6 1.0 copy-start.26
  494.6 1.6 copy-start.17
  563.1 3.8 copy-start.15
  563.1 4.5 copy-start.9
  563.1 5.4 copy-start.7
  566.9 2.6 copy-start.19
  (3 other events, 2.3 us)
Sparse Core Ops, SparseCore 0:
  61.9 115.8 all-gather.1
  398.6 173.8 reduce-scatter.1

commit v4 on v3

--- a/solution.py
+++ b/solution.py
@@ -463,7 +463,7 @@
     )
 
 
-def quad_stages(s, x, mine, first, out, one, got_one, two, got_two, sems, add, total):
+def quad_stages(s, x, mine, first, out, one, got_one, two, got_two, sems, add, total, rests=(0, 0, 0)):
     send, recv, local = sems
     core, chip = lax.rem(s, 2), s // 2
     sibling = s + 1 - 2 * core
@@ -481,6 +481,8 @@
         copy.start()
         own[k] = copy
     yield
+    for _ in range(rests[0]):
+        yield
     across = (2 * flip_x + core, 2 * flip_y + core)
     stage = {}
     waited = set()
@@ -501,6 +503,8 @@
         copy.start()
         stage[half, i] = copy
     yield
+    for _ in range(rests[1]):
+        yield
     for half in (0, 1):
         k = 1 - half
         ready(k)
@@ -511,6 +515,8 @@
         copy.start()
         stage[half, 2] = copy
     yield
+    for _ in range(rests[2]):
+        yield
     ready(3)
     for half in (0, 1):
         stage[half, 0].wait_recv()
@@ -600,43 +606,57 @@
     )
 
 
-def quad_scatter_task(x):
+def quad_scatter_task(x, rests=(0, 0, 0), first_row=0, row_count=None):
     nb, n = dims()
-    block = (nb,) + x.shape[2:]
+    x_rows = row_count or x.shape[2]
+    block = (nb, x_rows, x.shape[3])
+    taken = pl.ds(first_row, x_rows)
 
     def body(ins, outs, scratch, b, s, nb, n):
         mine, first, one, got_one, two, got_two, send, recv, local = scratch[:9]
         total, z_send, z_recv, z_local = scratch[9:]
         o = outs[0]
 
-        def value(half, whole_refs, half_refs, i):
-            parts = [ref[half * (nb // 2) + i] for ref in whole_refs]
-            parts += [ref[i] for ref in half_refs]
+        rows = x_rows
+        step = 16 if rows % 16 == 0 else rows
+
+        def value(half, whole_refs, half_refs, i, at):
+            parts = [ref[half * (nb // 2) + i, at, :] for ref in whole_refs]
+            parts += [ref[i, at, :] for ref in half_refs]
             result = parts[0].astype(F32)
             for p in parts[1:]:
                 result = result + p.astype(F32)
             return result.astype(BF16)
 
+        def each(work):
+            def move(k, carry):
+                if step == rows:
+                    work(k, slice(None))
+                else:
+                    i, j = k // (rows // step), lax.rem(k, rows // step)
+                    work(i, pl.ds(pl.multiple_of(j * step, step), step))
+                return carry
+
+            lax.fori_loop(0, (nb // 2) * (rows // step), move, 0)
+
         def add(target, half, whole_refs, half_refs):
-            def work(i, carry):
-                target[i] = value(half, whole_refs, half_refs, i)
-                return carry
-
-            lax.fori_loop(0, nb // 2, work, 0)
+            def work(i, at):
+                target[i, at, :] = value(half, whole_refs, half_refs, i, at)
+
+            each(work)
 
         def finish(half, whole_refs, half_refs):
-            def work(i, carry):
-                total[half * (nb // 2) + i] = value(half, whole_refs, half_refs, i)
-                return carry
-
-            lax.fori_loop(0, nb // 2, work, 0)
+            def work(i, at):
+                total[half * (nb // 2) + i, at, :] = value(half, whole_refs, half_refs, i, at)
+
+            each(work)
 
         yield from quad_stages(
             s,
             ins[0],
             mine,
             first,
-            lambda ref, i: ref.at[:, i],
+            (lambda ref, i: ref.at[:, i]) if row_count is None else (lambda ref, i: ref.at[:, i, taken]),
             one,
             got_one,
             two,
@@ -644,6 +664,7 @@
             (send, recv, local),
             add,
             finish,
+            rests,
         )
         last = []
         for d in range(1, nb):
@@ -663,7 +684,7 @@
     return Task(
         [x],
         [like(x, block)],
-        quad_scratch(block, (nb // 2,) + x.shape[2:])
+        quad_scratch(block, (nb // 2,) + block[1:])
         + [pltpu.VMEM(block, BF16), DMA((nb,)), DMA((nb,)), DMA],
         body,
         True,
@@ -1180,22 +1201,14 @@
                         sums[g, to, rows] = sums[g, to, rows] + part[m * CHAN : (m + 1) * CHAN]
 
 
-def conv_backward_kernel(
-    count, length, groups, nb, d, u, seg, c1, c2, taps, dh, pieces, buf, grads, live, x, turned, bands, even, odd
+def conv_chain(
+    d, seg, c1, c2, dh, buf, grads, live, x, turned2, turned1, bands, count, length, groups
 ):
     width = groups * CHAN
-    row = pl.program_id(0)
-
-    @pl.when(row == 0)
-    def _():
-        fill_bands(bands, taps, groups, True)
-        even[...] = jnp.zeros_like(even)
-        odd[...] = jnp.zeros_like(odd)
-
     place(live, lambda at: jnp.ones((CHUNK, width), F32), seg, length)
     place(grads, lambda at: d[0, pl.ds(at, CHUNK), :].astype(F32), seg, length)
 
-    def slope(kept, scaled):
+    def slope(kept, turned, scaled):
         values = {}
         for w in range(FOLD // 2):
             lanes = slice(2 * CHAN * w, 2 * CHAN * (w + 1))
@@ -1203,57 +1216,83 @@
                 value = scaled(g, w, lanes) * mish_slope(kept[0, g, :, lanes])
                 values[g, w] = value
                 turned[g, lanes, :] = value.T.astype(BF16)
-        return values
-
-    def loaded(g, w, lanes):
+        write_folded(grads, count, groups, lambda g, lanes: values[g, lanes.start // (2 * CHAN)])
+
+    def both(source, g, w):
         return to_groups(
-            folded(grads, count, GAP + 2 * w), folded(grads, count, GAP + 2 * w + 1)
+            folded(source, count, GAP + 2 * w), folded(source, count, GAP + 2 * w + 1)
         )[g]
 
-    values = slope(c2, loaded)
-    write_folded(grads, count, groups, lambda g, lanes: values[g, lanes.start // (2 * CHAN)])
+    slope(c2, turned2, lambda g, w, lanes: both(grads, g, w))
+    yield
+    spread_taps(x, grads, count)
+    back = [times(x[g], bands[1, g]) for g in range(groups)]
+    slope(c1, turned1, lambda g, w, lanes: back[g][:, lanes] * both(live, g, w))
+    yield
+    spread_taps(x, grads, count)
+    last = [times(x[g], bands[0, g]) for g in range(groups)]
+    write_folded(buf, count, groups, lambda g, lanes: last[g][:, lanes])
+    unplace(buf, dh, seg, length)
+
+
+def conv_weights(
+    u, seg, c1, buf, live, x, turned2, turned1, even, odd, count, length, groups
+):
+    width = groups * CHAN
+    place(live, lambda at: jnp.ones((CHUNK, width), F32), seg, length)
     for i in range(0, GAP, 8):
         buf[i : i + 8, :] = jnp.zeros((8, width), F32)
     for i in range(GAP + FOLD * count, buf.shape[0], 8):
         buf[i : i + 8, :] = jnp.zeros((8, width), F32)
     write_folded(buf, count, groups, lambda g, lanes: mish(c1[0, g, :, lanes]), live)
     spread_taps(x, buf, count)
-    weight_sums(even, odd, 1, turned, x, groups)
-    spread_taps(x, grads, count)
-    back = [times(x[g], bands[1, g]) for g in range(groups)]
-
-    def masked(g, w, lanes):
-        alive = to_groups(
-            folded(live, count, GAP + 2 * w), folded(live, count, GAP + 2 * w + 1)
-        )[g]
-        return back[g][:, lanes] * alive
-
-    values = slope(c1, masked)
-    write_folded(grads, count, groups, lambda g, lanes: values[g, lanes.start // (2 * CHAN)])
+    weight_sums(even, odd, 1, turned2, x, groups)
+    yield
     place(buf, lambda at: u[0, pl.ds(at, CHUNK), :].astype(F32), seg, length)
     spread_taps(x, buf, count)
-    weight_sums(even, odd, 0, turned, x, groups)
-    spread_taps(x, grads, count)
-    last = [times(x[g], bands[0, g]) for g in range(groups)]
-    write_folded(buf, count, groups, lambda g, lanes: last[g][:, lanes])
-    unplace(buf, dh, seg, length)
+    weight_sums(even, odd, 0, turned1, x, groups)
+
+
+def conv_pieces(pieces, even, odd, groups, nb):
+    low = lax.broadcasted_iota(jnp.int32, (2 * CHAN, 2 * CHAN), 1) < CHAN
+    part = groups * CHAN // nb
+    each = CHAN // part
+    for g in range(groups):
+        for p in range(16):
+            left = pltpu.roll(odd[g, p], CHAN, 1)
+            right = pltpu.roll(odd[g, p + 1], CHAN, 1) if p < 15 else left
+            total = (even[g, p] + jnp.where(low, left, right)).T.astype(BF16)
+            for half in range(2):
+                k = 2 * p + half
+                if k < KERNEL:
+                    for j in range(each):
+                        first = half * CHAN + j * part
+                        pieces[0, g * each + j, k] = total[first : first + part]
+
+
+def conv_backward_kernel(
+    count, length, groups, nb, d, u, seg, c1, c2, taps, dh, pieces, buf, grads, live, x, turned2, turned1, bands, even, odd
+):
+    row = pl.program_id(0)
+
+    @pl.when(row == 0)
+    def _():
+        fill_bands(bands, taps, groups, True)
+        even[...] = jnp.zeros_like(even)
+        odd[...] = jnp.zeros_like(odd)
+
+    for _ in conv_chain(
+        d, seg, c1, c2, dh, buf, grads, live, x, turned2, turned1, bands, count, length, groups
+    ):
+        pass
+    for _ in conv_weights(
+        u, seg, c1, buf, live, x, turned2, turned1, even, odd, count, length, groups
+    ):
+        pass
 
     @pl.when(row == pl.num_programs(0) - 1)
     def _():
-        low = lax.broadcasted_iota(jnp.int32, (2 * CHAN, 2 * CHAN), 1) < CHAN
-        part = width // nb
-        each = CHAN // part
-        for g in range(groups):
-            for p in range(16):
-                left = pltpu.roll(odd[g, p], CHAN, 1)
-                right = pltpu.roll(odd[g, p + 1], CHAN, 1) if p < 15 else left
-                total = (even[g, p] + jnp.where(low, left, right)).T.astype(BF16)
-                for half in range(2):
-                    k = 2 * p + half
-                    if k < KERNEL:
-                        for j in range(each):
-                            first = half * CHAN + j * part
-                            pieces[0, g * each + j, k] = total[first : first + part]
+        conv_pieces(pieces, even, odd, groups, nb)
 
 
 def conv_backward(d, u, seg, c1, c2, taps, nb):
@@ -1285,6 +1324,7 @@
             frames,
             pltpu.VMEM((groups, count, DEPTH), BF16),
             pltpu.VMEM((groups, FOLDED, count), BF16),
+            pltpu.VMEM((groups, FOLDED, count), BF16),
             pltpu.VMEM((2, groups, DEPTH, FOLDED), BF16),
             sums,
             sums,
@@ -1492,6 +1532,7 @@
 
 
 STEP = 32
+LATE_RESTS = ((0, 1, 3), (0, 2, 3), (1, 3, 2), (1, 4, 2))
 
 
 def feed_kernel(
@@ -1915,20 +1956,23 @@
 def late_grads_task(att, grad_branch, grad_feed, low, grad_up, normed, ndev, part):
     def body(ins, outs, scratch, b, s, nb, n):
         yield
-        late_work(*ins, outs[0], part)
+        late_work(*ins, *outs, part)
 
     vmem = pl.BlockSpec(memory_space=pltpu.VMEM)
     return Task(
         [att, grad_branch, grad_feed, low, grad_up, normed],
-        [jax.ShapeDtypeStruct((ndev, 5 * part, D), BF16)],
+        [
+            jax.ShapeDtypeStruct((ndev, 3 * part, D), BF16),
+            jax.ShapeDtypeStruct((ndev, 2 * part, D), BF16),
+        ],
         [],
         body,
         in_specs=[vmem] * 6,
-        out_specs=[vmem],
-    )
-
-
-def late_work(att, grad_branch, grad_feed, low, grad_up, normed, out, part):
+        out_specs=[vmem] * 2,
+    )
+
+
+def late_work(att, grad_branch, grad_feed, low, grad_up, normed, out, down, part):
     wide = 256
     per = wide // part
     for j in range(D // wide):
@@ -1937,7 +1981,7 @@
             rows_sum(grad_branch[:, lanes], att[...]).astype(BF16).reshape(per, part, D)
         )
         for half in range(2):
-            out[j * per : (j + 1) * per, (3 + half) * part : (4 + half) * part, :] = (
+            down[j * per : (j + 1) * per, half * part : (half + 1) * part, :] = (
                 rows_sum(grad_feed[:, lanes], low[:, half * D : (half + 1) * D])
                 .astype(BF16)
                 .reshape(per, part, D)
@@ -1947,6 +1991,89 @@
         out[j * per // 2 : (j + 1) * per // 2, part : 3 * part, :] = (
             rows_sum(grad_up[:, lanes], normed[...]).astype(BF16).reshape(per // 2, 2 * part, D)
         )
+
+
+def conv_back_task(d, u, seg, c1, c2, taps, frames):
+    nb, n = dims()
+    rows, length, width = u.shape
+    groups = width // CHAN
+    count, buffer = conv_sizes(length)
+    pieces_shape = (1, nb, KERNEL, width // nb, 2 * CHAN)
+
+    def body(ins, outs, scratch, b, s, nb, n):
+        d, u, seg, c1, c2, taps = ins
+        o, pieces = outs
+        buf, grads, live, x, turned2, turned1, bands, even, odd, dh, send, recv, local = scratch
+        yield
+        fill_bands(bands, taps, groups, True)
+        even[...] = jnp.zeros_like(even)
+        odd[...] = jnp.zeros_like(odd)
+        copies = []
+        for r in range(rows):
+            row = pl.ds(r, 1)
+            yield from conv_chain(
+                d.at[row], seg.at[row], c1.at[row], c2.at[row], dh.at[row], buf, grads, live, x,
+                turned2.at[r], turned1.at[r], bands, count, length, groups,
+            )
+            target = o.at[r, :, lane_block(b, s, n, width)]
+            for k in range(1, n):
+                t = lax.rem(s + k, n)
+                copy = remote(
+                    dh.at[r, seat_rows(t, frames, 0, frames), :],
+                    target,
+                    send.at[r, k],
+                    recv.at[r, k],
+                    seq=t,
+                )
+                copy.start()
+                copies.append(copy)
+            copy = pltpu.make_async_copy(
+                dh.at[r, seat_rows(s, frames, 0, frames), :], target, local.at[r]
+            )
+            copy.start()
+            copies.append(copy)
+            yield
+        for r in range(rows):
+            row = pl.ds(r, 1)
+            yield from conv_weights(
+                u.at[row], seg.at[row], c1.at[row], buf, live, x, turned2.at[r], turned1.at[r],
+                even, odd, count, length, groups,
+            )
+            yield
+        conv_pieces(pieces, even, odd, groups, nb)
+        yield
+        for copy in copies:
+            copy.wait()
+
+    vmem = pl.BlockSpec(memory_space=pltpu.VMEM)
+    frames_buf = pltpu.VMEM((buffer, width), F32)
+    turned = pltpu.VMEM((rows, groups, FOLDED, count), BF16)
+    sums = pltpu.VMEM((groups, 16, 2 * CHAN, 2 * CHAN), F32)
+    return Task(
+        [d, u, seg, c1, c2, taps],
+        [
+            jax.ShapeDtypeStruct((rows, frames, n * width), BF16),
+            jax.ShapeDtypeStruct(pieces_shape, BF16),
+        ],
+        [
+            frames_buf,
+            frames_buf,
+            frames_buf,
+            pltpu.VMEM((groups, count, DEPTH), BF16),
+            turned,
+            turned,
+            pltpu.VMEM((2, groups, DEPTH, FOLDED), BF16),
+            sums,
+            sums,
+            pltpu.VMEM(u.shape, BF16),
+            DMA((rows, n)),
+            DMA((rows, n)),
+            DMA((rows,)),
+        ],
+        body,
+        in_specs=[vmem] * 6,
+        out_specs=[ANY, vmem],
+    )
 
 
 def layer_norm(field):
@@ -2161,7 +2288,7 @@
     partial = times(grad_projected, qkv_t).astype(BF16).reshape(rows, n, frames, D)
     qkv_back = columns_back_task(grad_qkv.reshape(3, nb, part, D))
     if fused:
-        (grad_embedded, grad_emb_c, attn_sums), (got_qkv_grads,), (late_grads,) = transfer(
+        (grad_embedded, grad_emb_c, attn_sums), (got_qkv_grads,), late_grads = transfer(
             [
                 sum_norm_task(
                     partial,
@@ -2181,7 +2308,7 @@
         attn_sums = jnp.sum(attn_sums, axis=3)
         attn_sums = [attn_sums[:, :, 0], attn_sums[:, :, 1]]
     else:
-        (grad_normed,), (got_qkv_grads,), (late_grads,) = transfer(
+        (grad_normed,), (got_qkv_grads,), late_grads = transfer(
             [sum_task(partial), qkv_back, late_task], 7
         )
         grad_emb_part, grad_scale_attn, grad_shift_attn = jax.vjp(
@@ -2190,10 +2317,6 @@
         grad_embedded = grad_middle + grad_emb_part
         task, arrange = to_channels(grad_embedded.astype(BF16))
         grad_emb_c = arrange(transfer([task], 10)[0])
-    late_sum = lax.psum_scatter(
-        late_grads, ("batch", "seq"), scatter_dimension=0, tiled=False
-    ).astype(F32)
-
     first_ids, last_ids = own_ids[:, 0], own_ids[:, -1]
     if not fused:
         first = (own_ids == first_ids[:, None])[:, :, None]
@@ -2213,21 +2336,39 @@
     local_sums = is_first[:, :, None] * sides[:, :1] + is_last[:, :, None] * sides[:, 1:]
     slots = rows * SEGS
     sums_out = local_sums.reshape(slots, ndev, 6 * part).transpose(1, 0, 2)
-    grad_hidden_c, conv_sums = conv_backward(
-        grad_emb_c, hidden_c, seg_column, conv_one, conv_two, got_convs, nb
-    )
-    task, arrange = to_frames(grad_hidden_c)
-    got, (sums_got,), (got_conv_grads,) = transfer(
-        [task, spray_task(sums_out, False), columns_back_task(conv_sums)], 11
-    )
-    grad_hidden_conv = arrange(got)
+    if fused:
+        late_parts = [(0, 0), (0, 1), (1, 0), (1, 1)]
+        late_tasks = []
+        for k, (which, side) in enumerate(late_parts):
+            x = late_grads[which].reshape(nb, n, -1, D)
+            size = x.shape[2] // 2
+            late_tasks.append(quad_scatter_task(x, LATE_RESTS[k], side * size, size))
+        *late_got, (sums_got,), (grad_hidden_conv, conv_sums) = transfer(
+            late_tasks
+            + [
+                spray_task(sums_out, False),
+                conv_back_task(
+                    grad_emb_c, hidden_c, seg_column, conv_one, conv_two, got_convs, frames
+                ),
+            ],
+            11,
+        )
+        late_sum = jnp.concatenate([jnp.sum(x[0].astype(F32), axis=0) for x in late_got], axis=0)
+    else:
+        late_sum = lax.psum_scatter(
+            jnp.concatenate(late_grads, axis=1), ("batch", "seq"), scatter_dimension=0, tiled=False
+        ).astype(F32)
+        grad_hidden_c, conv_sums = conv_backward(
+            grad_emb_c, hidden_c, seg_column, conv_one, conv_two, got_convs, nb
+        )
+        task, arrange = to_frames(grad_hidden_c)
+        got, (sums_got,) = transfer([task, spray_task(sums_out, False)], 11)
+        grad_hidden_conv = arrange(got)
     sums_got = sums_got.reshape(nb, n, slots, 6 * part)
     grad_mod = jnp.sum(sums_got, axis=1).astype(BF16).reshape(nb * slots, 6 * part)
     grad_adaln = rows_sum(soft_cond, grad_mod)
     soft_part = times_t(grad_mod, adaln_proj)
     soft_out = soft_part.reshape(nb * slots, ndev, part).transpose(1, 0, 2)
-    grad_convs = jnp.sum(got_conv_grads.astype(F32), axis=0)[0]
-    grad_first, grad_second = grad_convs[..., :CHAN], grad_convs[..., CHAN:]
     grad_qkv_own = jnp.sum(got_qkv_grads.astype(F32), axis=0).reshape(3 * part, D).T
 
     grad_hidden = (grad_embedded + grad_hidden_conv.astype(F32)).astype(BF16).reshape(tokens, D)
@@ -2237,14 +2378,17 @@
     grad_embed = grad_joined[:, 2 * MEL :].astype(BF16)
     grad_text = rows_sum(grad_embed, text_hot).astype(BF16)
     scatter = quad_scatter_task if n == 8 and nb % 2 == 0 else scatter_task
-    (in_sum,), (text_sum,), (soft_got,) = transfer(
+    (in_sum,), (text_sum,), (soft_got,), (got_conv_grads,) = transfer(
         [
             scatter(grad_input.reshape(nb, n, part, -1)),
             scatter(grad_text.reshape(nb, n, -1, VOCAB)),
             spray_task(soft_out, False),
+            columns_back_task(conv_sums),
         ],
         13,
     )
+    grad_convs = jnp.sum(got_conv_grads.astype(F32), axis=0)[0]
+    grad_first, grad_second = grad_convs[..., :CHAN], grad_convs[..., CHAN:]
     grad_soft = jnp.sum(soft_got, axis=0)
     own_cond = times(step_hot, time_table)
     grad_cond = jax.vjp(jax.nn.silu, own_cond)[1](grad_soft)[0]

time: 594 us -> 574 us (0.966)
  Pallas kernels: 497 us -> 480 us
    pallas_call x1 -> x0, Pallas kernels: 43.5 us -> none  [conv_backward(): pl.pallas_call(functools.partial(conv_backward_kernel, count, length, gro...]
    pallas_call x8, Pallas kernels: 329 us -> 351 us  [transfer(): pl.pallas_call(functools.partial(transfer_kernel, [t.body for t in tasks]...]
  transfers between devices with their start and end apart: 2 -> 1, of which waited for: 1 -> 0; matrix products, arithmetic and copies ran while one was open for 8% -> 5% of each run, Pallas kernels for 52% -> 26%
where the time goes in v4:
time: 574 us; the launch traced here: 569 us
  Pallas kernels  480 us (84%)
  matrix products  27.4 us (5%)
  local copies, waits for them, and re-layouts  23.5 us (4%)
  other arithmetic  23.1 us (4%)
  between operations  15.1 us (3%)
    pallas_call x8, Pallas kernels, transfer(): pl.pallas_call(functools.partial(transfer_kernel, [t.body for t in tasks]...  351 us
    pallas_call x1, Pallas kernels, attention_backward(): pl.pallas_call(functools.partial(attention_backward_kernel, length, width...  46.8 us
    pallas_call x1, Pallas kernels, feed_both(): pl.pallas_call(functools.partial(feed_kernel, rows, frames, part), in_spe...  25.7 us
    pallas_call x1, Pallas kernels, conv_forward(): pl.pallas_call(functools.partial(conv_forward_kernel, count, length, grou...  23.6 us
    pallas_call x1, Pallas kernels, attention_forward(): pl.pallas_call(functools.partial(attention_forward_kernel, width), grid=(...  22.9 us
  transfers between devices with their start and end apart: 1, of which 0 were waited for; matrix products, arithmetic and copies ran while one was open for 5% of the time, Pallas kernels for 26%

profile of v4, /device:TPU:1, one launch (start us, length us, event | category | flops | bytes accessed | tf_op | source)
XLA Modules:
  0.0 568.8 jit_solution(6339470512726739642)
XLA Ops:
  7.3 1.4 copy.84
  9.5 1.9 maximum_bitcast_fusion.1.refs_4_
  11.4 1.7 pad_maximum_fusion.3
  13.1 48.7 %shard_map.274 = (bf16[4,8,32,712]{3,2,1,0:T(8,128)(2,1)}, bf16[4,8,16,2546]{3,2,1,0:T(8,128)(2,1)}, bf16[4,8,32,32]{3,2,1,0:T(8,128)(2,1)}, s32[4,8,2,4]{3,2,1,0:T(2,128)}, bf16[1,4,31,32,128]{4,3,2,1,0:T(8,128)(2,1)}) custom-call(bf16[32,712]{1,0:T(8,128)(2,1)} %bitcast.186, bf16[16,2546]{1,0:T(8,128)(2,1)} %bitcast.184, bf16[32,32]{1,0:T(8,128)(2,1)} %bitcast.187, ...), custom_call_target="tpu_custom_call" | custom-call | tf_op jit(solution)/shard_map/pallas_call | solution.py:137
  66.1 1.7 copy.85.seg.q_code.k_code.refs_7_
  70.0 3.1 fusion.3
  73.2 2.2 fusion.43
  75.4 22.8 %shard_map.275 = (bf16[2,1536,128]{2,1,0:T(8,128)(2,1)}, f32[32,8,192]{2,1,0:T(8,128)}) custom-call(bf16[2,192,1024]{2,1,0:T(8,128)(2,1)} %bitcast.157, f32[4,8,192]{2,1,0:T(8,128)} %convolution_bitcast_fusion.1.refs_1_), custom_call_target="tpu_custom_call" | custom-call | tf_op jit(solution)/shard_map/pallas_call | solution.py:137
  101.2 23.6 %shard_map.276 = (f32[2,2,400,256]{3,2,1,0:T(8,128)}, f32[2,2,400,256]{3,2,1,0:T(8,128)}, bf16[2,1536,128]{2,1,0:T(8,128)(2,1)}) custom-call(bf16[2,1536,128]{2,1,0:T(8,128)(2,1)} %get-tuple-element.62.u.refs_6_, s32[2,1536,1]{2,1,0:T(8,128)} %copy.85.seg.q_code.k_code.refs_7_, bf16[4,31,32,128]{3,2,1,0:T(8,128)(2,1)} %bitcast.151), custom_call_target="tpu_custom_call" | custom-call | tf_op jit(solution)/shard_map/pallas_call | solution.py:1167
  124.9 58.6 %shard_map.277 = (f32[384,1024]{1,0:T(8,128)}, bf16[2,8,192,1024]{3,2,1,0:T(8,128)(2,1)}, bf16[3,4,32,1024]{3,2,1,0:T(8,128)(2,1)}) custom-call(bf16[2,1536,128]{2,1,0:T(8,128)(2,1)} %get-tuple-element.64.refs_0_, f32[384,1024]{1,0:T(8,128)} %get-tuple-element.184.refs_1_, s32[384,1]{1,0:T(8,128)} %reshape.231.refs_2_.ids.refs_3_, ...), custom_call_target="tpu_custom_call" | custom-call | tf_op jit(solution)/shard_map/pallas_call | solution.py:137
  183.7 4.2 multiply_subtract_fusion
  187.9 9.4 %shard_map.278 = (bf16[2,1536,128]{2,1,0:T(8,128)(2,1)}, bf16[2,1536,128]{2,1,0:T(8,128)(2,1)}, bf16[2,1536,128]{2,1,0:T(8,128)(2,1)}) custom-call(bf16[2,1536,1024]{2,1,0:T(8,128)(2,1)} %bitcast.135, bf16[384,1024]{1,0:T(8,128)(2,1)} %bitcast.163, f32[2,1536,128]{2,1,0:T(8,128)} %get-tuple-element.157.cos, f32[2,1536,128]{2,1,0:T(8,128)} %get-tuple-element.156.sin), custom_call_target="tpu_custom_call" | custom-call | tf_op jit(solution)/shard_map/pallas_call | solution.py:1362
  197.3 22.9 %shard_map.279 = (f32[2,1536,128]{2,1,0:T(8,128)}, bf16[2,1536,128]{2,1,0:T(8,128)(2,1)}, f32[2,1536,128]{2,1,0:T(8,128)}) custom-call(bf16[2,1536,128]{2,1,0:T(8,128)(2,1)} %get-tuple-element.68.q, bf16[2,1536,128]{2,1,0:T(8,128)(2,1)} %get-tuple-element.69.k, bf16[2,1536,128]{2,1,0:T(8,128)(2,1)} %get-tuple-element.70.v, ...), custom_call_target="tpu_custom_call" | custom-call | tf_op jit(solution)/shard_map/pallas_call | solution.py:1406
  220.2 12.3 %shard_map.280 = bf16[2,192,1024]{2,1,0:T(8,128)(2,1)} custom-call(bf16[2,1536,128]{2,1,0:T(8,128)(2,1)} %get-tuple-element.71.refs_0_), custom_call_target="tpu_custom_call" | custom-call | tf_op jit(solution)/shard_map/pallas_call | solution.py:137
  236.2 1.5 fusion.26
  237.7 25.7 %shard_map.281 = (bf16[384,1024]{1,0:T(8,128)(2,1)}, bf16[384,1024]{1,0:T(8,128)(2,1)}, f32[384,1024]{1,0:T(8,128)}, f32[2,2,4,8,1024]{4,3,2,1,0:T(8,128)}, bf16...) custom-call(bf16[384,1024]{1,0:T(8,128)(2,1)} %bitcast.147, ...), custom_call_target="tpu_custom_call" | custom-call | tf_op jit(solution)/shard_map/pallas_call | solution.py:1671
  263.4 12.3 %shard_map.282.g = bf16[2,1536,128]{2,1,0:T(8,128)(2,1)} custom-call(bf16[2,192,1024]{2,1,0:T(8,128)(2,1)} %bitcast.165), custom_call_target="tpu_custom_call" | custom-call | tf_op jit(solution)/shard_map/pallas_call | solution.py:137
  275.7 1.3 convert_multiply_fusion
  278.2 46.8 %shard_map.283 = bf16[2,1536,384]{2,1,0:T(8,128)(2,1)} custom-call(s32[2,6]{1,0:T(2,128)} %get-tuple-element.186.low_edge, s32[2,6]{1,0:T(2,128)} %get-tuple-element.185.high_edge, bf16[2,1536,128]{2,1,0:T(8,128)(2,1)} %get-tuple-element.68.q, bf16[2,1536,128]{2,1,0:T(8,128)(2,1)} %get-tuple-element.69.k, bf16[2,1536,128]{2,1,0:T(8,128)(2,1)} %get-tuple-element.70.v, ...), custom_call_target="tpu_custom_call" | custom-call | tf_op jit(solution)/shard_map/pallas_call | solution.py:1502
  325.1 7.7 %convolution_convert_fusion = bf16[3072,1024]{1,0:T(8,128)(2,1)} fusion(bf16[3072,384]{1,0:T(8,128)(2,1)} %bitcast.141, bf16[384,1024]{1,0:T(8,128)(2,1)S(1)} %bitcast.164), kind=kOutput, calls=%fused_computation | convolution fusion | flops 2419064832 | bytes 9437184 | tf_op jit(solution)/shard_map/dot_general | solution.py:980
  332.8 3.5 convolution_convert_fusion.3
  336.3 59.9 %shard_map.284 = (f32[384,1024]{1,0:T(8,128)}, bf16[2,1536,128]{2,1,0:T(8,128)(2,1)}, f32[2,2,2,8,1024]{4,3,2,1,0:T(8,128)}, bf16[4,3,32,1024]{3,2,1,0:T(8,128)(...) custom-call(bf16[2,8,192,1024]{3,2,1,0:T(8,128)(2,1)} %bitcast.149, ...), custom_call_target="tpu_custom_call" | custom-call | tf_op jit(solution)/shard_map/pallas_call | solution.py:137
  399.1 78.1 %shard_map.285 = (bf16[4,48,1024]{2,1,0:T(8,128)(2,1)}, bf16[4,48,1024]{2,1,0:T(8,128)(2,1)}, bf16[4,32,1024]{2,1,0:T(8,128)(2,1)}, bf16[4,32,1024]{2,1,0:T(8,12...) custom-call(bf16[4,8,96,1024]{3,2,1,0:T(8,128)(2,1)} %bitcast.139, ...), custom_call_target="tpu_custom_call" | custom-call | tf_op jit(solution)/shard_map/pallas_call | solution.py:137
  477.3 1.5 add_convert_fusion
  480.0 2.3 convolution_convert_fusion.2
  482.3 1.6 convolution_convert_fusion.1
  486.5 2.9 copy.106
  489.3 2.7 copy.105
  492.0 1.2 fusion.18
  493.2 1.3 convolution_bitcast_fusion.refs_2_
  494.5 58.5 %shard_map.286 = (bf16[4,32,712]{2,1,0:T(8,128)(2,1)}, bf16[4,16,2546]{2,1,0:T(8,128)(2,1)}, f32[32,32,32]{2,1,0:T(8,128)}, bf16[4,1,31,32,128]{4,3,2,1,0:T(8,128)(2,1)}) custom-call(bf16[4,8,32,712]{3,2,1,0:T(8,128)(2,1)} %bitcast.150, bf16[4,8,16,2546]{3,2,1,0:T(8,128)(2,1)} %bitcast.145, f32[32,32,32]{2,1,0:T(8,128)} %convolution_bitcast_fusion.refs_2_, ...), custom_call_target="tpu_custom_call" | custom-call | tf_op jit(solution)/shard_map/pallas_call | solution.py:137
  554.1 1.4 convert_reduce_fusion
  (149 shorter events, 28.9 us)
Async XLA Ops:
  7.2 55.4 %copy-start.22 = (s32[2,1536]{1,0:T(2,128)S(1)}, s32[2,1536]{1,0:T(2,128)}, u32[]{:S(2)}) copy-start(s32[2,1536]{1,0:T(2,128)} %param.21) | copy-start | bytes 36868
  7.2 58.2 %copy-start.27 = (s32[2,192]{1,0:T(2,128)S(1)}, s32[2,192]{1,0:T(2,128)}, u32[]{:S(2)}) copy-start(s32[2,192]{1,0:T(2,128)} %param.20) | copy-start | bytes 4612
  7.2 58.3 %copy-start.26 = (s32[2,1536]{1,0:T(2,128)S(1)}, s32[2,1536]{1,0:T(2,128)}, u32[]{:S(2)}) copy-start(s32[2,1536]{1,0:T(2,128)} %param.22) | copy-start | bytes 36868
  7.2 230.5 %all-gather.2.cloned.1.call-start = ((), (), s32[]{:S(2)}) async-start(), calls=%async_computation | async-start | bytes 10813440 | tf_op jit(solution)/shard_map/all_gather | solution.py:2161
  11.4 56.4 %copy-start.6 = (bf16[1024,192]{0,1:T(8,128)(2,1)S(1)}, bf16[1024,192]{0,1:T(8,128)(2,1)}, u32[]{:S(2)}) copy-start(bf16[1024,192]{0,1:T(8,128)(2,1)} %param.28) | copy-start | bytes 1179652
  61.8 7.0 %copy-start.33 = (bf16[4,8,32,32]{3,2,1,0:T(8,128)(2,1)S(1)}, bf16[4,8,32,32]{3,2,1,0:T(8,128)(2,1)}, u32[]{:S(2)}) copy-start(bf16[4,8,32,32]{3,2,1,0:T(8,128)(2,1)} %get-tuple-element.61) | copy-start | bytes 196612
  65.4 4.5 copy-start.28
  65.5 3.6 copy-start.30
  70.0 3.2 copy-start.2
  70.0 3.2 copy-start.23
  124.8 58.6 %copy-start.32 = (f32[128]{0:T(128)S(1)}, f32[128]{0:T(128)}, u32[]{:S(2)}) copy-start(f32[128]{0:T(128)} %constant.57.clone) | copy-start | bytes 1540
  124.8 58.8 %copy-start.11 = (f32[1536,128]{1,0:T(8,128)S(1)}, f32[1536,128]{1,0:T(8,128)}, u32[]{:S(2)}) copy-start(f32[1536,128]{1,0:T(8,128)} %constant.55.clone) | copy-start | bytes 2359300
  124.9 58.8 %copy-start.12 = (f32[1536,128]{1,0:T(8,128)S(1)}, f32[1536,128]{1,0:T(8,128)}, u32[]{:S(2)}) copy-start(f32[1536,128]{1,0:T(8,128)} %constant.56.clone) | copy-start | bytes 2359300
  220.2 12.3 %copy-start.5 = (f32[2,1536,128]{2,1,0:T(8,128)S(1)}, f32[2,1536,128]{2,1,0:T(8,128)}, u32[]{:S(2)}) copy-start(f32[2,1536,128]{2,1,0:T(8,128)} %get-tuple-element.76) | copy-start | bytes 4718596
  263.4 12.3 %copy-start.7 = (f32[2,1536,128]{2,1,0:T(8,128)S(1)}, f32[2,1536,128]{2,1,0:T(8,128)}, u32[]{:S(2)}) copy-start(f32[2,1536,128]{2,1,0:T(8,128)} %get-tuple-element.77) | copy-start | bytes 4718596
  278.2 46.9 %copy-start.9 = (bf16[3,4,32,1024]{3,2,1,0:T(8,128)(2,1)S(1)}, bf16[3,4,32,1024]{3,2,1,0:T(8,128)(2,1)}, u32[]{:S(2)}) copy-start(bf16[3,4,32,1024]{3,2,1,0:T(8,128)(2,1)} %get-tuple-element.67) | copy-start | bytes 2359300
  278.2 54.5 %slice-start = ((s8[6291456]{0:T(1024)(128)(4,1)}), s8[2097152]{0:T(1024)(128)(4,1)S(1)}, s32[]{:S(2)}) async-start(s8[6291456]{0:T(1024)(128)(4,1)} %bitcast.136), calls=%async_computation.1 | async-start | bytes 4194304
  325.0 7.7 %slice-start.1 = ((s8[6291456]{0:T(1024)(128)(4,1)}), s8[4194304]{0:T(1024)(128)(4,1)S(1)}, s32[]{:S(2)}) async-start(s8[6291456]{0:T(1024)(128)(4,1)} %bitcast.136), calls=%async_computation.2 | async-start | bytes 8388608
  325.1 7.7 %copy-start = (bf16[2,1536,384]{2,1,0:T(8,128)(2,1)S(1)}, bf16[2,1536,384]{2,1,0:T(8,128)(2,1)}, u32[]{:S(2)}) copy-start(bf16[2,1536,384]{2,1,0:T(8,128)(2,1)} %shard_map.283) | copy-start | bytes 7077892
  336.3 61.0 %copy-start.13 = (f32[2,2,4,8,1024]{4,3,2,1,0:T(8,128)S(1)}, f32[2,2,4,8,1024]{4,3,2,1,0:T(8,128)}, u32[]{:S(2)}) copy-start(f32[2,2,4,8,1024]{4,3,2,1,0:T(8,128)} %get-tuple-element.88) | copy-start | bytes 1572868
  399.1 78.2 %copy-start.4 = (f32[384,1024]{1,0:T(8,128)S(1)}, f32[384,1024]{1,0:T(8,128)}, u32[]{:S(2)}) copy-start(f32[384,1024]{1,0:T(8,128)} %get-tuple-element.84) | copy-start | bytes 4718596
  479.9 4.0 copy-start.8
  479.9 2.3 copy-start.29
  489.3 2.7 copy-start.19
  489.3 2.7 copy-start.21
  489.3 3.9 copy-start.1
  554.1 2.6 copy-start.16
  555.6 1.9 copy-start.25
  555.6 2.5 slice-start.2
  555.6 3.4 copy-start.10
  556.7 3.9 copy-start.31
  556.7 3.9 copy-start.34
  (7 other events, 9.0 us)
Sparse Core Ops, SparseCore 0:
  62.0 109.7 all-gather.1

commit v5 on v4

--- a/solution.py
+++ b/solution.py
@@ -1343,35 +1343,85 @@
     return jnp.where(lax.rem(lane, 2) == 0, -after, before)[:, :width]
 
 
-def qkv_kernel(width, x, w, cos, sin, q, k, v):
-    got = lax.dot_general(
-        x[0], w[...], (((1,), (1,)), ((), ())), preferred_element_type=F32
-    )
+def qkv_kernel(width, x, w, cos_t, sin_t, offset, seg, q, k, v, cos, sin):
+    got = times(x[0], w[...])
+    ids = seg[0] & 7
+    size = cos_t.shape[0]
+    cos_o, sin_o = pick(ids, offset[0, 0], size), pick(ids, offset[0, 1], size)
+    cos[0] = cos_t[...] * cos_o + sin_t[...] * sin_o
+    sin[0] = sin_t[...] * cos_o - cos_t[...] * sin_o
     for p, out in enumerate((q, k)):
         part = got[:, p * width : (p + 1) * width]
         out[0] = (part * cos[0] + pair_swap(part) * sin[0]).astype(BF16)
     v[0] = got[:, 2 * width :].astype(BF16)
 
 
-def qkv_forward(x, w, cos, sin):
+def qkv_forward(x, w, starts, seg):
     rows, length, depth = x.shape
-    width = w.shape[0] // 3
+    width = w.shape[1] // 3
+    pairs = (np.arange(width) % HEAD) // 2
+    freq = 10000.0 ** (-2.0 * pairs / HEAD)
+    angle = np.arange(length)[:, None] * freq[None, :]
+    cos_t = jnp.asarray(np.cos(angle).astype(np.float32))
+    sin_t = jnp.asarray(np.sin(angle).astype(np.float32))
+    turned = starts.astype(F32)[:, :, None] * jnp.asarray(freq.astype(np.float32))
+    offset = jnp.stack([jnp.cos(turned), jnp.sin(turned)], axis=1)
     block = 512
     spec = pl.BlockSpec((1, block, width), lambda r, i: (r, i, 0))
+    table = pl.BlockSpec((block, width), lambda r, i: (i, 0))
     shape = jax.ShapeDtypeStruct((rows, length, width), BF16)
+    angles = jax.ShapeDtypeStruct((rows, length, width), F32)
     return pl.pallas_call(
         functools.partial(qkv_kernel, width),
         grid=(rows, length // block),
         in_specs=[
             pl.BlockSpec((1, block, depth), lambda r, i: (r, i, 0)),
             whole(w.shape),
-            spec,
-            spec,
+            table,
+            table,
+            pl.BlockSpec((1, 2, SEGS, width), lambda r, i: (r, 0, 0, 0)),
+            pl.BlockSpec((1, block, 1), lambda r, i: (r, i, 0)),
         ],
-        out_specs=[spec] * 3,
-        out_shape=[shape] * 3,
+        out_specs=[spec] * 5,
+        out_shape=[shape] * 3 + [angles] * 2,
         compiler_params=params(),
-    )(x, w, cos, sin)
+    )(x, w, cos_t, sin_t, offset, seg)
+
+
+def qkv_back_kernel(p, w, x, partial, grad, total):
+    i = pl.program_id(0) * pl.num_programs(1) + pl.program_id(1)
+
+    @pl.when(i == 0)
+    def _():
+        total[...] = jnp.zeros_like(total)
+
+    partial[0] = times(p[0], w[...]).astype(BF16)
+    total[...] = total[...] + rows_sum(p[0], x[0])
+
+    @pl.when(i == pl.num_programs(0) * pl.num_programs(1) - 1)
+    def _():
+        grad[...] = total[...].astype(BF16)
+
+
+def qkv_backward(p, w, x):
+    rows, length, depth = x.shape
+    block = 512
+
+    def spec(size):
+        return pl.BlockSpec((1, block, size), lambda r, i: (r, i, 0))
+
+    return pl.pallas_call(
+        qkv_back_kernel,
+        grid=(rows, length // block),
+        in_specs=[spec(p.shape[2]), whole(w.shape), spec(depth)],
+        out_specs=[spec(depth), whole(w.shape)],
+        out_shape=[
+            jax.ShapeDtypeStruct((rows, length, depth), BF16),
+            jax.ShapeDtypeStruct(w.shape, BF16),
+        ],
+        scratch_shapes=[pltpu.VMEM(w.shape, F32)],
+        compiler_params=params(),
+    )(p, w, x)
 
 
 def attention_forward_kernel(width, q, k, v, q_code, k_code, out, low, log_sum):
@@ -1423,11 +1473,11 @@
     )(q, k, v, q_code, k_code)
 
 
-BLOCK = 256
+BLOCK = 512
 
 
 def attention_backward_kernel(
-    length, width, low_edge, high_edge, q, k, v, g, log_sum, delta, k_code, q_code, cos, sin, out, dq, dk, dv
+    length, width, ids, q, k, v, g, log_sum, delta, k_code, q_code, cos, sin, out, dq, dk, dv
 ):
     heads = width // HEAD
     row = pl.program_id(0)
@@ -1443,8 +1493,16 @@
         queries_of = [jnp.where(lane == h, queries, zero) for h in range(heads)]
         grads_of = [jnp.where(lane == h, grads, zero) for h in range(heads)]
         dq[...] = jnp.zeros_like(dq)
+        first_id, last_id = ids[row, i * BLOCK], ids[row, i * BLOCK + BLOCK - 1]
 
         def inner(j, carry):
+            @pl.when((ids[row, j * BLOCK + BLOCK - 1] >= first_id) & (ids[row, j * BLOCK] <= last_id))
+            def _():
+                pair(j)
+
+            return carry
+
+        def pair(j):
             to = pl.ds(pl.multiple_of(j * BLOCK, BLOCK), BLOCK)
             keys, values = k[0, to, :], v[0, to, :]
             allowed = k_code[0, to, :] == q_code[0, :, at]
@@ -1470,9 +1528,8 @@
             dv[to, :] = dv[to, :] + dv_part
             dk[to, :] = dk[to, :] + dk_part
             dq[...] = dq[...] + dq_part
-            return carry
-
-        lax.fori_loop(low_edge[row, i], high_edge[row, i], inner, 0)
+
+        lax.fori_loop(0, length // BLOCK, inner, 0)
         grad = dq[...] * 0.125
         turned = grad * cos[0, at, :] - pair_swap(grad) * sin[0, at, :]
         out[0, at, 0:width] = turned.astype(BF16)
@@ -1491,7 +1548,7 @@
     lax.fori_loop(0, length // BLOCK, finish, 0)
 
 
-def attention_backward(q, k, v, g, log_sum, delta, k_code, q_code, cos, sin, low_edge, high_edge):
+def attention_backward(ids, q, k, v, g, log_sum, delta, k_code, q_code, cos, sin):
     rows, length, width = q.shape
 
     def spec(shape):
@@ -1502,7 +1559,7 @@
     return pl.pallas_call(
         functools.partial(attention_backward_kernel, length, width),
         grid_spec=pltpu.PrefetchScalarGridSpec(
-            num_scalar_prefetch=2,
+            num_scalar_prefetch=1,
             grid=(rows,),
             in_specs=[spec(a.shape) for a in arrays],
             out_specs=spec(out),
@@ -1514,7 +1571,7 @@
         ),
         out_shape=jax.ShapeDtypeStruct(out, BF16),
         compiler_params=params(),
-    )(low_edge, high_edge, *arrays)
+    )(ids, *arrays)
 
 
 def pick(ids, table, rows):
@@ -1532,7 +1589,6 @@
 
 
 STEP = 32
-LATE_RESTS = ((0, 1, 3), (0, 2, 3), (1, 3, 2), (1, 4, 2))
 
 
 def feed_kernel(
@@ -2076,6 +2132,42 @@
     )
 
 
+def tail_kernel(grad_embedded, grad_conv, joined, in_t, ids, grad_in, mels, grad_text, hidden):
+    tokens = joined.shape[0]
+    for i in range(tokens // 64):
+        at = slice(64 * i, 64 * (i + 1))
+        hidden[at, :] = (grad_embedded[at, :] + grad_conv[at, :].astype(F32)).astype(BF16)
+    back = times(hidden[...], in_t[...])
+    mels[...] = back[:, : 2 * MEL]
+    embed = back[:, 2 * MEL :].astype(BF16)
+    for start in range(0, D, 256):
+        at = slice(start, start + 256)
+        grad_in[at, :] = rows_sum(hidden[:, at], joined[...]).astype(BF16)
+    turned = embed.astype(F32).T.astype(BF16)
+    for start in range(0, VOCAB, 512):
+        stop = min(start + 512, VOCAB)
+        word = lax.broadcasted_iota(jnp.int32, (tokens, stop - start), 1) + start
+        hot = (word == ids[...]).astype(F32).astype(BF16)
+        grad_text[:, start:stop] = times(turned, hot).astype(BF16)
+
+
+def tail_back(grad_embedded, grad_conv, joined, in_t, ids):
+    tokens, inner = joined.shape
+    vmem = pl.BlockSpec(memory_space=pltpu.VMEM)
+    return pl.pallas_call(
+        tail_kernel,
+        in_specs=[vmem] * 5,
+        out_specs=[vmem] * 3,
+        out_shape=[
+            jax.ShapeDtypeStruct((D, inner), BF16),
+            jax.ShapeDtypeStruct((tokens, 2 * MEL), F32),
+            jax.ShapeDtypeStruct((inner - 2 * MEL, VOCAB), BF16),
+        ],
+        scratch_shapes=[pltpu.VMEM((tokens, D), BF16)],
+        compiler_params=params(),
+    )(grad_embedded, grad_conv, joined, in_t, ids)
+
+
 def layer_norm(field):
     centre = field - jnp.mean(field, axis=-1, keepdims=True)
     return centre * lax.rsqrt(jnp.mean(centre * centre, axis=-1, keepdims=True) + EPSILON)
@@ -2094,19 +2186,6 @@
     for u in range(SEGS - 2, -1, -1):
         value = jnp.where(ids[:, :, None] == u, table[:, u][:, None, :], value)
     return value
-
-
-def rope_tables(segment_ids, starts, width):
-    length = segment_ids.shape[1]
-    pairs = (np.arange(width) % HEAD) // 2
-    freq = 10000.0 ** (-2.0 * pairs / HEAD)
-    angle = np.arange(length)[:, None] * freq[None, :]
-    cos_t = jnp.asarray(np.cos(angle).astype(np.float32))[None]
-    sin_t = jnp.asarray(np.sin(angle).astype(np.float32))[None]
-    offset = starts.astype(F32)[:, :, None] * jnp.asarray(freq.astype(np.float32))
-    cos_o = by_segment(segment_ids, jnp.cos(offset))
-    sin_o = by_segment(segment_ids, jnp.sin(offset))
-    return cos_t * cos_o + sin_t * sin_o, sin_t * cos_o - cos_t * sin_o
 
 
 def on_device(
@@ -2215,8 +2294,7 @@
         (normed_all,), (got_qkv,) = transfer([gather_task(normed), qkv_task], 4)
     normed_all = normed_all.reshape(rows, length, D)
     qkv_t = got_qkv.reshape(3 * width, D)
-    cos, sin = rope_tables(segment_ids, starts, width)
-    query, key, value = qkv_forward(normed_all, qkv_t, cos, sin)
+    query, key, value, cos, sin = qkv_forward(normed_all, qkv_t.T, starts, seg_column)
     attended, attended_low, log_lanes = attention_forward(
         query, key, value, seg_column, key_code[:, None, :]
     )
@@ -2258,19 +2336,8 @@
         (grad_att_c.astype(F32) * attended).reshape(rows, length, heads, HEAD), axis=3
     ).transpose(0, 2, 1)
     log_rows = log_lanes.reshape(rows, length, heads, HEAD)[:, :, :, 0].transpose(0, 2, 1)
-    block_first_ids = segment_ids[:, ::BLOCK]
-    block_last_ids = segment_ids[:, BLOCK - 1 :: BLOCK]
-    ends = jnp.sum((segment_ids[:, None, :] <= seg_index[None, :, None]).astype(jnp.int32), axis=2)
-    low_edge = (
-        jnp.sum(jnp.where(block_first_ids[:, :, None] == seg_index, starts[:, None, :], 0), axis=2)
-        // BLOCK
-    )
-    high_edge = (
-        jnp.sum(jnp.where(block_last_ids[:, :, None] == seg_index, ends[:, None, :], 0), axis=2)
-        + BLOCK
-        - 1
-    ) // BLOCK
     grad_projected = attention_backward(
+        segment_ids,
         query,
         key,
         value,
@@ -2281,11 +2348,9 @@
         segment_ids[:, None, :],
         cos,
         sin,
-        low_edge,
-        high_edge,
-    ).reshape(rows * length, 3 * width)
-    grad_qkv = rows_sum(grad_projected, normed_all.reshape(rows * length, D)).astype(BF16)
-    partial = times(grad_projected, qkv_t).astype(BF16).reshape(rows, n, frames, D)
+    )
+    partial, grad_qkv = qkv_backward(grad_projected, qkv_t, normed_all)
+    partial = partial.reshape(rows, n, frames, D)
     qkv_back = columns_back_task(grad_qkv.reshape(3, nb, part, D))
     if fused:
         (grad_embedded, grad_emb_c, attn_sums), (got_qkv_grads,), late_grads = transfer(
@@ -2337,12 +2402,13 @@
     slots = rows * SEGS
     sums_out = local_sums.reshape(slots, ndev, 6 * part).transpose(1, 0, 2)
     if fused:
-        late_parts = [(0, 0), (0, 1), (1, 0), (1, 1)]
         late_tasks = []
-        for k, (which, side) in enumerate(late_parts):
-            x = late_grads[which].reshape(nb, n, -1, D)
-            size = x.shape[2] // 2
-            late_tasks.append(quad_scatter_task(x, LATE_RESTS[k], side * size, size))
+        for x, sides in zip(late_grads, (3, 2)):
+            x = x.reshape(nb, n, -1, D)
+            size = x.shape[2] // sides
+            for side in range(sides):
+                rests = (len(late_tasks), 2, 2)
+                late_tasks.append(quad_scatter_task(x, rests, side * size, size))
         *late_got, (sums_got,), (grad_hidden_conv, conv_sums) = transfer(
             late_tasks
             + [
@@ -2371,12 +2437,14 @@
     soft_out = soft_part.reshape(nb * slots, ndev, part).transpose(1, 0, 2)
     grad_qkv_own = jnp.sum(got_qkv_grads.astype(F32), axis=0).reshape(3 * part, D).T
 
-    grad_hidden = (grad_embedded + grad_hidden_conv.astype(F32)).astype(BF16).reshape(tokens, D)
-    grad_input = rows_sum(grad_hidden, joined).astype(BF16)
-    grad_joined = times(grad_hidden, in_t)
-    grad_mels = grad_joined[:, : 2 * MEL].reshape(rows, frames, 2 * MEL)
-    grad_embed = grad_joined[:, 2 * MEL :].astype(BF16)
-    grad_text = rows_sum(grad_embed, text_hot).astype(BF16)
+    grad_input, grad_mels, grad_text = tail_back(
+        grad_embedded.reshape(tokens, D),
+        grad_hidden_conv.reshape(tokens, D),
+        joined,
+        in_t,
+        text_ids.reshape(tokens, 1),
+    )
+    grad_mels = grad_mels.reshape(rows, frames, 2 * MEL)
     scatter = quad_scatter_task if n == 8 and nb % 2 == 0 else scatter_task
     (in_sum,), (text_sum,), (soft_got,), (got_conv_grads,) = transfer(
         [

time: 574 us -> 554 us (0.965)
  matrix products: 27.4 us -> 8.82 us
  local copies, waits for them, and re-layouts: 23.5 us -> 17.1 us
    pallas_call x0 -> x2, Pallas kernels: none -> 18.1 us  [the longest x1 11.4 us: qkv_backward(): pl.pallas_call(qkv_back_kernel, grid=(rows, length // block), in_specs=[s...]
    pallas_call x1, Pallas kernels: 46.8 us -> 35.7 us  [attention_backward(): pl.pallas_call(functools.partial(attention_backward_kernel, length, width...]
    dot_general x4 -> x2, matrix products: 11 us -> 1.74 us  [times(): lax.dot_general(left, right, (((1,), (0,)), ((), ())), preferred_element_...]
    dot_general x4 -> x1, matrix products: 8.64 us -> 1.18 us  [rows_sum(): lax.dot_general(left, right, (((0,), (0,)), ((), ())), preferred_element_...]
  transfers between devices with their start and end apart: 1 -> 1, of which waited for: 0 -> 0; matrix products, arithmetic and copies ran while one was open for 5% -> 4% of each run, Pallas kernels for 26% -> 28%
where the time goes in v5:
time: 554 us; the launch traced here: 547 us
  Pallas kernels  485 us (88%)
  other arithmetic  21.8 us (4%)
  local copies, waits for them, and re-layouts  17.1 us (3%)
  between operations  14.7 us (3%)
  matrix products  8.82 us (2%)
    pallas_call x8, Pallas kernels, transfer(): pl.pallas_call(functools.partial(transfer_kernel, [t.body for t in tasks]...  349 us
    pallas_call x1, Pallas kernels, attention_backward(): pl.pallas_call(functools.partial(attention_backward_kernel, length, width...  35.7 us
    pallas_call x1, Pallas kernels, feed_both(): pl.pallas_call(functools.partial(feed_kernel, rows, frames, part), in_spe...  25.6 us
    pallas_call x1, Pallas kernels, conv_forward(): pl.pallas_call(functools.partial(conv_forward_kernel, count, length, grou...  24.1 us
    pallas_call x1, Pallas kernels, attention_forward(): pl.pallas_call(functools.partial(attention_forward_kernel, width), grid=(...  22.9 us
    pallas_call x1, Pallas kernels, qkv_backward(): pl.pallas_call(qkv_back_kernel, grid=(rows, length // block), in_specs=[s...  11.4 us
  transfers between devices with their start and end apart: 1, of which 0 were waited for; matrix products, arithmetic and copies ran while one was open for 4% of the time, Pallas kernels for 28%

profile of v5, /device:TPU:1, one launch (start us, length us, event | category | flops | bytes accessed | tf_op | source)
XLA Modules:
  0.0 547.4 jit_solution(18065492389821563892)
XLA Ops:
  7.3 1.4 copy.79
  9.5 1.9 maximum_bitcast_fusion.2.refs_4_
  11.4 1.7 pad_maximum_fusion.1
  13.1 48.7 %shard_map.274 = (bf16[4,8,32,712]{3,2,1,0:T(8,128)(2,1)}, bf16[4,8,16,2546]{3,2,1,0:T(8,128)(2,1)}, bf16[4,8,32,32]{3,2,1,0:T(8,128)(2,1)}, s32[4,8,2,4]{3,2,1,0:T(2,128)}, bf16[1,4,31,32,128]{4,3,2,1,0:T(8,128)(2,1)}) custom-call(bf16[32,712]{1,0:T(8,128)(2,1)} %bitcast.152, bf16[16,2546]{1,0:T(8,128)(2,1)} %bitcast.150, bf16[32,32]{1,0:T(8,128)(2,1)} %bitcast.153, ...), custom_call_target="tpu_custom_call" | custom-call | tf_op jit(solution)/shard_map/pallas_call | solution.py:137
  64.9 1.7 copy.80.seg.q_code.k_code.refs_8_
  68.7 1.2 fusion.2
  70.1 2.2 fusion.39
  72.3 20.9 %shard_map.275 = (bf16[2,1536,128]{2,1,0:T(8,128)(2,1)}, f32[32,8,192]{2,1,0:T(8,128)}) custom-call(bf16[2,192,1024]{2,1,0:T(8,128)(2,1)} %bitcast.128, f32[4,8,192]{2,1,0:T(8,128)} %convolution_bitcast_fusion.1.refs_1_), custom_call_target="tpu_custom_call" | custom-call | tf_op jit(solution)/shard_map/pallas_call | solution.py:137
  93.2 1.0 copy.81
  96.2 24.1 %shard_map.276 = (f32[2,2,400,256]{3,2,1,0:T(8,128)}, f32[2,2,400,256]{3,2,1,0:T(8,128)}, bf16[2,1536,128]{2,1,0:T(8,128)(2,1)}) custom-call(bf16[2,1536,128]{2,1,0:T(8,128)(2,1)} %get-tuple-element.70.u.refs_7_, s32[2,1536,1]{2,1,0:T(8,128)} %copy.80.seg.q_code.k_code.refs_8_, bf16[4,31,32,128]{3,2,1,0:T(8,128)(2,1)} %bitcast.121), custom_call_target="tpu_custom_call" | custom-call | tf_op jit(solution)/shard_map/pallas_call | solution.py:1167
  120.3 65.6 %shard_map.277 = (f32[384,1024]{1,0:T(8,128)}, bf16[2,8,192,1024]{3,2,1,0:T(8,128)(2,1)}, bf16[3,4,32,1024]{3,2,1,0:T(8,128)(2,1)}) custom-call(bf16[2,1536,128]{2,1,0:T(8,128)(2,1)} %get-tuple-element.72.refs_0_, f32[384,1024]{1,0:T(8,128)} %get-tuple-element.137.refs_1_, s32[384,1]{1,0:T(8,128)} %reshape.219.refs_2_.ids.refs_3_, ...), custom_call_target="tpu_custom_call" | custom-call | tf_op jit(solution)/shard_map/pallas_call | solution.py:137
  185.9 2.3 copy.84.w
  189.1 9.8 %shard_map.278 = (bf16[2,1536,128]{2,1,0:T(8,128)(2,1)}, bf16[2,1536,128]{2,1,0:T(8,128)(2,1)}, bf16[2,1536,128]{2,1,0:T(8,128)(2,1)}, f32[2,1536,128]{2,1,0:T(8,128)}, f32[2,1536,128]{2,1,0:T(8,128)}) custom-call(bf16[2,1536,1024]{2,1,0:T(8,128)(2,1)} %bitcast.111, bf16[1024,384]{1,0:T(8,128)(2,1)} %copy.84.w, f32[1536,128]{1,0:T(8,128)} %constant.26.clone.cos_t, ...), custom_call_target="tpu_custom_call" | custom-call | tf_op jit(solution)/shard_map/pallas_call | solution.py:1374
  198.9 22.9 %shard_map.279 = (f32[2,1536,128]{2,1,0:T(8,128)}, bf16[2,1536,128]{2,1,0:T(8,128)(2,1)}, f32[2,1536,128]{2,1,0:T(8,128)}) custom-call(bf16[2,1536,128]{2,1,0:T(8,128)(2,1)} %get-tuple-element.76.q, bf16[2,1536,128]{2,1,0:T(8,128)(2,1)} %get-tuple-element.77.k, bf16[2,1536,128]{2,1,0:T(8,128)(2,1)} %get-tuple-element.78.v, ...), custom_call_target="tpu_custom_call" | custom-call | tf_op jit(solution)/shard_map/pallas_call | solution.py:1456
  221.8 12.3 %shard_map.280 = bf16[2,192,1024]{2,1,0:T(8,128)(2,1)} custom-call(bf16[2,1536,128]{2,1,0:T(8,128)(2,1)} %get-tuple-element.79.refs_0_), custom_call_target="tpu_custom_call" | custom-call | tf_op jit(solution)/shard_map/pallas_call | solution.py:137
  235.7 2.1 pad_maximum_fusion.joined
  238.6 25.6 %shard_map.281 = (bf16[384,1024]{1,0:T(8,128)(2,1)}, bf16[384,1024]{1,0:T(8,128)(2,1)}, f32[384,1024]{1,0:T(8,128)}, f32[2,2,4,8,1024]{4,3,2,1,0:T(8,128)}, bf16...) custom-call(bf16[384,1024]{1,0:T(8,128)(2,1)} %bitcast.116, ...), custom_call_target="tpu_custom_call" | custom-call | tf_op jit(solution)/shard_map/pallas_call | solution.py:1727
  264.3 12.1 %shard_map.282.g = bf16[2,1536,128]{2,1,0:T(8,128)(2,1)} custom-call(bf16[2,192,1024]{2,1,0:T(8,128)(2,1)} %bitcast.137), custom_call_target="tpu_custom_call" | custom-call | tf_op jit(solution)/shard_map/pallas_call | solution.py:137
  276.4 1.3 convert_multiply_fusion
  278.9 35.7 %shard_map.283.p = bf16[2,1536,384]{2,1,0:T(8,128)(2,1)} custom-call(s32[2,1536]{1,0:T(2,128)} %ids.1, bf16[2,1536,128]{2,1,0:T(8,128)(2,1)} %get-tuple-element.76.q, bf16[2,1536,128]{2,1,0:T(8,128)(2,1)} %get-tuple-element.77.k, bf16[2,1536,128]{2,1,0:T(8,128)(2,1)} %get-tuple-element.78.v, bf16[2,1536,128]{2,1,0:T(8,128)(2,1)} %shard_map.282.g, ...), custom_call_target="tpu_custom_call" | custom-call | tf_op jit(solution)/shard_map/pallas_call | solution.py:1559
  314.6 11.4 %shard_map.284 = (bf16[2,1536,1024]{2,1,0:T(8,128)(2,1)}, bf16[384,1024]{1,0:T(8,128)(2,1)}) custom-call(bf16[2,1536,384]{2,1,0:T(8,128)(2,1)} %shard_map.283.p, bf16[384,1024]{1,0:T(8,128)(2,1)} %bitcast.127, bf16[2,1536,1024]{2,1,0:T(8,128)(2,1)} %bitcast.112), custom_call_target="tpu_custom_call" | custom-call | tf_op jit(solution)/shard_map/pallas_call | solution.py:1413
  326.0 62.5 %shard_map.285 = (f32[384,1024]{1,0:T(8,128)}, bf16[2,1536,128]{2,1,0:T(8,128)(2,1)}, f32[2,2,2,8,1024]{4,3,2,1,0:T(8,128)}, bf16[4,3,32,1024]{3,2,1,0:T(8,128)(...) custom-call(bf16[2,8,192,1024]{3,2,1,0:T(8,128)(2,1)} %bitcast.118, ...), custom_call_target="tpu_custom_call" | custom-call | tf_op jit(solution)/shard_map/pallas_call | solution.py:137
  388.5 1.0 reduce_sum.137
  391.5 72.2 %shard_map.286 = (bf16[4,32,1024]{2,1,0:T(8,128)(2,1)}, bf16[4,32,1024]{2,1,0:T(8,128)(2,1)}, bf16[4,32,1024]{2,1,0:T(8,128)(2,1)}, bf16[4,32,1024]{2,1,0:T(8,12...) custom-call(bf16[4,8,96,1024]{3,2,1,0:T(8,128)(2,1)} %bitcast.108, ...), custom_call_target="tpu_custom_call" | custom-call | tf_op jit(solution)/shard_map/pallas_call | solution.py:137
  463.7 1.1 convert_reduce_fusion.3
  467.8 1.2 fusion.15
  469.0 1.3 convolution_bitcast_fusion.refs_2_
  470.3 6.7 %shard_map.287 = (bf16[1024,712]{1,0:T(8,128)(2,1)}, f32[384,200]{1,0:T(8,128)}, bf16[512,2546]{1,0:T(8,128)(2,1)}) custom-call(f32[384,1024]{1,0:T(8,128)} %get-tuple-element.96.grad_embedded, bf16[384,1024]{1,0:T(8,128)(2,1)} %bitcast.136, bf16[384,712]{1,0:T(8,128)(2,1)} %pad_maximum_fusion.joined, bf16[1024,712]{1,0:T(8,128)(2,1)} %bitcast.119, ...), custom_call_target="tpu_custom_call" | custom-call | tf_op jit(solution)/shard_map/pallas_call | solution.py:2157
  477.0 54.3 %shard_map.288 = (bf16[4,32,712]{2,1,0:T(8,128)(2,1)}, bf16[4,16,2546]{2,1,0:T(8,128)(2,1)}, f32[32,32,32]{2,1,0:T(8,128)}, bf16[4,1,31,32,128]{4,3,2,1,0:T(8,128)(2,1)}) custom-call(bf16[4,8,32,712]{3,2,1,0:T(8,128)(2,1)} %bitcast.132, bf16[4,8,16,2546]{3,2,1,0:T(8,128)(2,1)} %bitcast.129, f32[32,32,32]{2,1,0:T(8,128)} %convolution_bitcast_fusion.refs_2_, ...), custom_call_target="tpu_custom_call" | custom-call | tf_op jit(solution)/shard_map/pallas_call | solution.py:137
  531.4 1.1 reduce_sum.142
  532.5 1.4 convert_reduce_fusion
  533.9 1.1 fusion.34
  (99 shorter events, 22.8 us)
Async XLA Ops:
  7.2 55.4 %copy-start.16 = (s32[2,192]{1,0:T(2,128)S(1)}, s32[2,192]{1,0:T(2,128)}, u32[]{:S(2)}) copy-start(s32[2,192]{1,0:T(2,128)} %param.20) | copy-start | bytes 4612
  7.2 56.4 %copy-start.13 = (s32[2,1536]{1,0:T(2,128)S(1)}, s32[2,1536]{1,0:T(2,128)}, u32[]{:S(2)}) copy-start(s32[2,1536]{1,0:T(2,128)} %ids.1) | copy-start | bytes 36868
  7.2 57.0 %copy-start.15 = (s32[2,1536]{1,0:T(2,128)S(1)}, s32[2,1536]{1,0:T(2,128)}, u32[]{:S(2)}) copy-start(s32[2,1536]{1,0:T(2,128)} %param.22) | copy-start | bytes 36868
  7.2 231.4 %all-gather.2.cloned.1.call-start = ((), (), s32[]{:S(2)}) async-start(), calls=%async_computation | async-start | bytes 10813440 | tf_op jit(solution)/shard_map/all_gather | solution.py:2240
  11.4 55.1 %copy-start.3 = (bf16[1024,192]{0,1:T(8,128)(2,1)S(1)}, bf16[1024,192]{0,1:T(8,128)(2,1)}, u32[]{:S(2)}) copy-start(bf16[1024,192]{0,1:T(8,128)(2,1)} %param.28) | copy-start | bytes 1179652
  61.8 5.7 %copy-start.19 = (bf16[4,8,32,32]{3,2,1,0:T(8,128)(2,1)S(1)}, bf16[4,8,32,32]{3,2,1,0:T(8,128)(2,1)}, u32[]{:S(2)}) copy-start(bf16[4,8,32,32]{3,2,1,0:T(8,128)(2,1)} %get-tuple-element.69) | copy-start | bytes 196612
  64.9 3.8 copy-start.18
  67.8 0.9 copy-start.11
  68.7 1.4 copy-start
  68.7 1.4 copy-start.5
  120.3 68.1 %copy-start.17 = (f32[128]{0:T(128)S(1)}, f32[128]{0:T(128)}, u32[]{:S(2)}) copy-start(f32[128]{0:T(128)} %constant.28.clone) | copy-start | bytes 1540
  221.8 12.3 %copy-start.2 = (f32[2,1536,128]{2,1,0:T(8,128)S(1)}, f32[2,1536,128]{2,1,0:T(8,128)}, u32[]{:S(2)}) copy-start(f32[2,1536,128]{2,1,0:T(8,128)} %get-tuple-element.84) | copy-start | bytes 4718596
  264.3 12.1 %copy-start.4 = (f32[2,1536,128]{2,1,0:T(8,128)S(1)}, f32[2,1536,128]{2,1,0:T(8,128)}, u32[]{:S(2)}) copy-start(f32[2,1536,128]{2,1,0:T(8,128)} %get-tuple-element.85) | copy-start | bytes 4718596
  325.9 63.7 %copy-start.7 = (f32[2,2,4,8,1024]{4,3,2,1,0:T(8,128)S(1)}, f32[2,2,4,8,1024]{4,3,2,1,0:T(8,128)}, u32[]{:S(2)}) copy-start(f32[2,2,4,8,1024]{4,3,2,1,0:T(8,128)} %get-tuple-element.100) | copy-start | bytes 1572868
  463.7 4.1 copy-start.10
  463.7 4.1 copy-start.12
  463.7 5.3 copy-start.1
  532.5 2.6 copy-start.8
  533.9 1.8 copy-start.14
  533.9 2.5 copy-start.9
  533.9 3.2 copy-start.6
Sparse Core Ops, SparseCore 0:
  62.0 118.3 all-gather.1
